TPU v7x, 128 devices: a whole 4x4x4 slice. The times are simulated.
128 devices in a mesh: pts: 64 (over z, y, x), grp: 2 (over core).
Axes of the slice: x: 4, y: 4, z: 4, core: 2. Of those that a mesh axis runs over, the one named last changes fastest.
Arguments:
- points: bfloat16 [131072, 256], P('pts'), may hold values from -6 to 6
- neighbours: int32 [131072, 27], P('pts'), may hold values from -1 to 131071, as said below
- patch_len: int32 [256], replicated, may hold values from 1 to 1024, as said below
- zorder: int32 [131072], P('pts'), may hold values from 0 to 131071, as said below
- conv_w: bfloat16 [27, 256, 256], P(None, None, 'grp'), may hold values from -0.078125 to 0.078125
- conv_b: float32 [256], P('grp'), may hold values from -3 to 3
- cpe_w: bfloat16 [256, 256], replicated, may hold values from -0.375 to 0.375
- cpe_b: float32 [256], replicated, may hold values from -3 to 3
- cpe_gain: float32 [256], replicated, may hold values from 0.1 to 1.9
- norm1_gain: float32 [256], replicated, may hold values from 0.1 to 1.9
- qkv_w: bfloat16 [256, 3, 256], P(None, None, 'grp'), may hold values from -2 to 2
- qkv_b: float32 [3, 256], P(None, 'grp'), may hold values from -3 to 3
- proj_w: bfloat16 [256, 256], replicated, may hold values from -0.375 to 0.375
- proj_b: float32 [256], replicated, may hold values from -3 to 3
- norm2_gain: float32 [256], replicated, may hold values from 0.1 to 1.9
- fc1_w: bfloat16 [256, 1024], P(None, 'grp'), may hold values from -0.375 to 0.375
- fc1_b: float32 [1024], P('grp'), may hold values from -3 to 3
- fc2_w: bfloat16 [1024, 256], P('grp'), may hold values from -0.1875 to 0.1875
- fc2_b: float32 [256], replicated, may hold values from -3 to 3
Outputs:
- next_rows: bfloat16 [131072, 256], P('pts')
Inputs may be any that keep to these rules, and one draw needn't show every extreme that they name: `neighbours`: tap 13 is the row itself; every other entry is -1 or a row at most 256 rows away; rows at exactly 256 away on both sides occur. `zorder`: A permutation. The rows of next_rows on one device come in runs of 64; each run is a whole aligned run of 64 rows of one source device, in one common inner order, and the 64-row runs of one device come from 32 different source devices at relative offsets (mod 64) common to all devices, one of which is 32. `patch_len`: patches sum to 131072 rows, one has exactly 1024.
All inputs are finite; a program needn't handle non-finite values.
Results may differ from a plain program's by a relative error of at most 0.022.
Values may be sent and summed in bfloat16 or wider, within the bound.
No kernel may reach another device: no remote copies, remote signals or barrier semaphores. Data moves between devices by JAX's collectives and lax.ppermute only.
A program may use at most 128 MiB of HBM per device.

v0:
```python
import jax
import jax.numpy as jnp
from jax import lax
from jax.sharding import PartitionSpec as P

PATCH = 1024
HALO = 256


def with_halo(block, sides, width):
    for axis, dim in sides:
        count = lax.axis_size(axis)
        forward = [(i, i + 1) for i in range(count - 1)]
        backward = [(target, source) for source, target in forward]
        low = lax.ppermute(
            lax.slice_in_dim(block, block.shape[dim] - width, None, axis=dim), axis, forward
        )
        high = lax.ppermute(lax.slice_in_dim(block, 0, width, axis=dim), axis, backward)
        block = jnp.concatenate([low, block, high], axis=dim)
    return block


def layer_norm(values, gain_row):
    center = values - jnp.mean(values, axis=-1, keepdims=True)
    spread = jnp.mean(center * center, axis=-1, keepdims=True)
    return center * lax.rsqrt(spread + 1e-05) * gain_row


def patch_limits(row_ids, patch_len, row_total):
    patch_ends = jnp.cumsum(patch_len)
    patch_starts = patch_ends - patch_len
    first_row = jnp.max(
        jnp.where(patch_starts[None, :] <= row_ids[:, None], patch_starts[None, :], 0), axis=1
    )
    finish = jnp.min(
        jnp.where(patch_ends[None, :] > row_ids[:, None], patch_ends[None, :], row_total), axis=1
    )
    return (first_row, finish)


def local(
    points,
    neighbours,
    patch_len,
    zorder,
    conv_w,
    conv_b,
    cpe_w,
    cpe_b,
    cpe_gain,
    norm1_gain,
    qkv_w,
    qkv_b,
    proj_w,
    proj_b,
    norm2_gain,
    fc1_w,
    fc1_b,
    fc2_w,
    fc2_b,
):
    row_count = points.shape[0]
    width = points.shape[1]
    half_width = conv_w.shape[2]
    peer_count = lax.axis_size("pts")
    base_row = lax.axis_index("pts") * row_count
    row_total = row_count * peer_count
    extended = with_halo(points, (("pts", 0),), HALO)
    extended = jnp.concatenate([extended, jnp.zeros((1, width), jnp.bfloat16)], axis=0)
    empty_row = row_count + 2 * HALO
    tap_index = jnp.where(neighbours < 0, empty_row, neighbours - base_row + HALO)
    flat_conv = conv_w.reshape(27 * width, half_width)
    block_rows = min(512, row_count)

    def conv_block(number):
        picked = lax.dynamic_slice_in_dim(tap_index, number * block_rows, block_rows, 0)
        gathered = jnp.take(extended, picked, axis=0).reshape(block_rows, 27 * width)
        return (jnp.dot(gathered, flat_conv, preferred_element_type=jnp.float32) + conv_b).astype(
            jnp.bfloat16
        )

    conv_local = lax.map(conv_block, jnp.arange(row_count // block_rows, dtype=jnp.int32)).reshape(
        row_count, half_width
    )
    conv_out = lax.all_gather(conv_local, "grp", axis=1, tiled=True)
    cpe_term = layer_norm(
        jnp.dot(conv_out, cpe_w, preferred_element_type=jnp.float32) + cpe_b, cpe_gain
    )
    section_one = (points.astype(jnp.float32) + cpe_term).astype(jnp.bfloat16)
    normed = layer_norm(section_one.astype(jnp.float32), norm1_gain).astype(jnp.bfloat16)
    triple = (
        jnp.dot(normed, qkv_w.reshape(width, 3 * half_width), preferred_element_type=jnp.float32)
        + qkv_b.reshape(3 * half_width)
    ).astype(jnp.bfloat16)
    query_rows = triple[:, :half_width]
    key_value = triple[:, half_width:]
    rim_rows = with_halo(key_value, (("pts", 0),), PATCH)
    head_count = half_width // 16
    window = block_rows + 2 * PATCH

    def attend(number):
        offset_row = number * block_rows
        query_blk = lax.dynamic_slice_in_dim(query_rows, offset_row, block_rows, 0).reshape(
            block_rows, head_count, 16
        )
        pair_blk = lax.dynamic_slice_in_dim(rim_rows, offset_row, window, 0)
        key_blk = pair_blk[:, :half_width].reshape(window, head_count, 16)
        value_blk = pair_blk[:, half_width:].reshape(window, head_count, 16)
        row_ids = base_row + offset_row + jnp.arange(block_rows, dtype=jnp.int32)
        key_ids = base_row + offset_row - PATCH + jnp.arange(window, dtype=jnp.int32)
        first_row, finish = patch_limits(row_ids, patch_len, row_total)
        allowed = (key_ids[None, :] >= first_row[:, None]) & (key_ids[None, :] < finish[:, None])
        scores = (
            jnp.einsum("qhd,khd->hqk", query_blk, key_blk, preferred_element_type=jnp.float32)
            * 0.25
        )
        scores = jnp.where(allowed[None], scores, -jnp.inf)
        row_max = jnp.max(scores, axis=2, keepdims=True)
        expo = jnp.exp(scores - row_max)
        attn_weights = (expo / jnp.sum(expo, axis=2, keepdims=True)).astype(jnp.bfloat16)
        mixed_out = jnp.einsum(
            "hqk,khd->qhd", attn_weights, value_blk, preferred_element_type=jnp.float32
        )
        return mixed_out.reshape(block_rows, half_width).astype(jnp.bfloat16)

    attn_local = lax.map(attend, jnp.arange(row_count // block_rows, dtype=jnp.int32)).reshape(
        row_count, half_width
    )
    attn = lax.all_gather(attn_local, "grp", axis=1, tiled=True)
    section_two = (
        section_one.astype(jnp.float32)
        + jnp.dot(attn, proj_w, preferred_element_type=jnp.float32)
        + proj_b
    ).astype(jnp.bfloat16)
    normed_two = layer_norm(section_two.astype(jnp.float32), norm2_gain).astype(jnp.bfloat16)
    hidden = jax.nn.gelu(
        jnp.dot(normed_two, fc1_w, preferred_element_type=jnp.float32) + fc1_b, approximate=False
    ).astype(jnp.bfloat16)
    partial_sum = jnp.dot(hidden, fc2_w, preferred_element_type=jnp.float32)
    summed = lax.psum(partial_sum, "grp")
    output_rows = (section_two.astype(jnp.float32) + summed + fc2_b).astype(jnp.bfloat16)
    per_peer = 2 * row_count // peer_count
    source_dev = zorder // row_count
    offset = zorder - source_dev * row_count
    one_hot = (source_dev[:, None] == jnp.arange(peer_count, dtype=jnp.int32)[None, :]).astype(
        jnp.int32
    )
    slot_index = jnp.sum((jnp.cumsum(one_hot, axis=0) - 1) * one_hot, axis=1)
    flat_slot = source_dev * per_peer + slot_index
    requests = (
        jnp.zeros((peer_count * per_peer,), jnp.int32)
        .at[flat_slot]
        .set(offset)
        .reshape(peer_count, per_peer)
    )
    picked_rows = jnp.take(
        output_rows,
        lax.all_to_all(requests, "pts", split_axis=0, concat_axis=0, tiled=True),
        axis=0,
    )
    fetched = lax.all_to_all(picked_rows, "pts", split_axis=0, concat_axis=0, tiled=True)
    next_rows = jnp.take(fetched.reshape(peer_count * per_peer, width), flat_slot, axis=0)
    return next_rows


def solution(mesh):
    placed = (
        P("pts", None),
        P("pts", None),
        P(),
        P("pts"),
        P(None, None, "grp"),
        P("grp"),
        P(),
        P(),
        P(),
        P(),
        P(None, None, "grp"),
        P(None, "grp"),
        P(),
        P(),
        P(),
        P(None, "grp"),
        P("grp"),
        P("grp", None),
        P(),
    )
    return jax.shard_map(
        local, mesh=mesh, in_specs=placed, out_specs=P("pts", None), check_vma=False
    )
```

profile of v0, /device:TPU:1, one launch (start us, length us, event | category | flops | bytes accessed | tf_op | source)
XLA Modules:
  0.0 755.0 jit_solution(4773720223149394747)
XLA Ops:
  17.9 319.5 %while.22 = (s32[]{:T(128)}, bf16[4,512,128]{2,1,0:T(8,128)(2,1)S(1)}, s32[4]{0:T(128)S(1)}, s32[2048,27]{1,0:T(8,128)}, bf16[2561,256]{1,0:T(8,128)(2,1)S(1)}, ...) while((s32[]{:T(128)}, ...), condition=%wide.region_5.6_spmd, body=%wide.region_4.5_spmd.sunk | while | flops 909736960 | bytes 66018988 | solution.py:82
  20.5 38.8 %gather_fusion = bf16[13824,256]{1,0:T(8,128)(2,1)} fusion(bf16[2561,256]{1,0:T(8,128)(2,1)S(1)} %get-tuple-element.403, s32[14336]{0:T(1024)S(1)} %pad_clamp_fusion.2), kind=kCustom, calls=%fused_computation.clone.1 | custom fusion | bytes 14211072 | tf_op jit(solution)/shard_map/while/body/eval_jaxpr/jit(_take)/gather | solution.py:77
  59.3 11.3 %reshape.340 = bf16[512,27,256]{2,1,0:T(8,128)(2,1)} reshape(bf16[13824,256]{1,0:T(8,128)(2,1)} %gather_fusion) | data formatting | bytes 14155776 | tf_op jit(solution)/shard_map/while/body/eval_jaxpr/jit(_take)/gather | solution.py:77
  78.6 13.6 %copy.86 = bf16[512,27,256]{0,2,1:T(8,128)(2,1)} copy(bf16[512,27,256]{2,1,0:T(8,128)(2,1)} %broadcast_select_fusion.4) | data formatting | bytes 14155776 | tf_op jit(solution)/shard_map/while/body/eval_jaxpr/jit(_take)/select_n | solution.py:77
  100.4 38.8 %gather_fusion = bf16[13824,256]{1,0:T(8,128)(2,1)} fusion(bf16[2561,256]{1,0:T(8,128)(2,1)S(1)} %get-tuple-element.403, s32[14336]{0:T(1024)S(1)} %pad_clamp_fusion.2), kind=kCustom, calls=%fused_computation.clone.1 | custom fusion | bytes 14211072 | tf_op jit(solution)/shard_map/while/body/eval_jaxpr/jit(_take)/gather | solution.py:77
  139.1 11.3 %reshape.340 = bf16[512,27,256]{2,1,0:T(8,128)(2,1)} reshape(bf16[13824,256]{1,0:T(8,128)(2,1)} %gather_fusion) | data formatting | bytes 14155776 | tf_op jit(solution)/shard_map/while/body/eval_jaxpr/jit(_take)/gather | solution.py:77
  158.4 13.6 %copy.86 = bf16[512,27,256]{0,2,1:T(8,128)(2,1)} copy(bf16[512,27,256]{2,1,0:T(8,128)(2,1)} %broadcast_select_fusion.4) | data formatting | bytes 14155776 | tf_op jit(solution)/shard_map/while/body/eval_jaxpr/jit(_take)/select_n | solution.py:77
  180.3 38.8 %gather_fusion = bf16[13824,256]{1,0:T(8,128)(2,1)} fusion(bf16[2561,256]{1,0:T(8,128)(2,1)S(1)} %get-tuple-element.403, s32[14336]{0:T(1024)S(1)} %pad_clamp_fusion.2), kind=kCustom, calls=%fused_computation.clone.1 | custom fusion | bytes 14211072 | tf_op jit(solution)/shard_map/while/body/eval_jaxpr/jit(_take)/gather | solution.py:77
  219.0 11.3 %reshape.340 = bf16[512,27,256]{2,1,0:T(8,128)(2,1)} reshape(bf16[13824,256]{1,0:T(8,128)(2,1)} %gather_fusion) | data formatting | bytes 14155776 | tf_op jit(solution)/shard_map/while/body/eval_jaxpr/jit(_take)/gather | solution.py:77
  238.3 13.6 %copy.86 = bf16[512,27,256]{0,2,1:T(8,128)(2,1)} copy(bf16[512,27,256]{2,1,0:T(8,128)(2,1)} %broadcast_select_fusion.4) | data formatting | bytes 14155776 | tf_op jit(solution)/shard_map/while/body/eval_jaxpr/jit(_take)/select_n | solution.py:77
  260.1 38.8 %gather_fusion = bf16[13824,256]{1,0:T(8,128)(2,1)} fusion(bf16[2561,256]{1,0:T(8,128)(2,1)S(1)} %get-tuple-element.403, s32[14336]{0:T(1024)S(1)} %pad_clamp_fusion.2), kind=kCustom, calls=%fused_computation.clone.1 | custom fusion | bytes 14211072 | tf_op jit(solution)/shard_map/while/body/eval_jaxpr/jit(_take)/gather | solution.py:77
  318.2 13.6 %copy.86 = bf16[512,27,256]{0,2,1:T(8,128)(2,1)} copy(bf16[512,27,256]{2,1,0:T(8,128)(2,1)} %broadcast_select_fusion.4) | data formatting | bytes 14155776 | tf_op jit(solution)/shard_map/while/body/eval_jaxpr/jit(_take)/select_n | solution.py:77
  340.0 17.6 %all-gather.3.cloned.1.call-done = bf16[2048,256]{1,0:T(8,128)(2,1)} async-done(((bf16[2048,128]{1,0:T(8,128)(2,1)}), bf16[2048,256]{1,0:T(8,128)(2,1)}) %all-gather.3.cloned.1.call-update) | async-done | bytes 1048592 | tf_op jit(solution)/shard_map/all_gather | solution.py:85
  384.3 225.8 %while.23 = (s32[]{:T(128)}, bf16[4,512,128]{2,1,0:T(8,128)(2,1)}, s32[4]{0:T(128)}, bf16[4096,256]{1,0:T(8,128)(2,1)}, s32[]{:T(128)}, /*index=5*/s32[3,1]{0,1:...) while((s32[]{:T(128)}, bf16[4,512,128]{2,1,0:T(8,128)(2,1)}, ...), condition=%wide.region_17.18_spmd, body=%wide.region_12.17_spmd.sunk | while | flops 1105800704 | bytes 96541496 | solution.py:126
  391.1 14.8 %fusion.134 = f32[8,512]{1,0:T(8,128)S(1)} fusion(pred[512,2560]{1,0:T(8,128)(4,1)S(1)} %compare_and_fusion.7, bf16[512,8,16]{0,2,1:T(8,128)(2,1)S(1)} %bitcast.99, bf16[2560,8,16]{0,2,1:T(8,128)(2,1)S(1)} %bitcast.96), kind=kOutput, calls=%fused_computation.154.clone.1 | convolution fusion | flops 377489920 | bytes 2113536 | tf_op jit(solution)/shard_map/while/body/eval_jaxpr/sub | solution.py:119
  405.9 16.2 %fusion.135 = f32[8,512,2560]{2,1,0:T(8,128)} fusion(bf16[512,8,16]{0,2,1:T(8,128)(2,1)S(1)} %bitcast.100, bf16[2560,8,16]{0,2,1:T(8,128)(2,1)S(1)} %bitcast.97), kind=kOutput, calls=%fused_computation.158.clone.1 | convolution fusion | flops 335544320 | bytes 42729472 | tf_op jit(solution)/shard_map/while/body/eval_jaxpr/qhd,khd->hqk/dot_general | solution.py:114
  422.3 18.0 %fusion.136 = bf16[8,16,512]{2,1,0:T(8,128)(2,1)S(1)} fusion(bf16[2560,8,16]{0,2,1:T(8,128)(2,1)S(1)} %bitcast.101, f32[8,512]{1,0:T(8,128)S(1)} %fusion.134, f32[8,512,2560]{2,1,0:T(8,128)} %fusion.135, pred[512,2560]{1,0:T(8,128)(4,1)S(1)} %compare_and_fusion.7), kind=kOutput, calls=%fused_computation.15.clone.1 | convolution fusion | flops 388045312 | bytes 44056576 | tf_op jit(solution)/shard_map/while/body/eval_jaxpr/hqk,khd->qhd/dot_general | solution.py:121
  447.4 14.8 %fusion.134 = f32[8,512]{1,0:T(8,128)S(1)} fusion(pred[512,2560]{1,0:T(8,128)(4,1)S(1)} %compare_and_fusion.7, bf16[512,8,16]{0,2,1:T(8,128)(2,1)S(1)} %bitcast.99, bf16[2560,8,16]{0,2,1:T(8,128)(2,1)S(1)} %bitcast.96), kind=kOutput, calls=%fused_computation.154.clone.1 | convolution fusion | flops 377489920 | bytes 2113536 | tf_op jit(solution)/shard_map/while/body/eval_jaxpr/sub | solution.py:119
  462.2 16.2 %fusion.135 = f32[8,512,2560]{2,1,0:T(8,128)} fusion(bf16[512,8,16]{0,2,1:T(8,128)(2,1)S(1)} %bitcast.100, bf16[2560,8,16]{0,2,1:T(8,128)(2,1)S(1)} %bitcast.97), kind=kOutput, calls=%fused_computation.158.clone.1 | convolution fusion | flops 335544320 | bytes 42729472 | tf_op jit(solution)/shard_map/while/body/eval_jaxpr/qhd,khd->hqk/dot_general | solution.py:114
  478.6 18.0 %fusion.136 = bf16[8,16,512]{2,1,0:T(8,128)(2,1)S(1)} fusion(bf16[2560,8,16]{0,2,1:T(8,128)(2,1)S(1)} %bitcast.101, f32[8,512]{1,0:T(8,128)S(1)} %fusion.134, f32[8,512,2560]{2,1,0:T(8,128)} %fusion.135, pred[512,2560]{1,0:T(8,128)(4,1)S(1)} %compare_and_fusion.7), kind=kOutput, calls=%fused_computation.15.clone.1 | convolution fusion | flops 388045312 | bytes 44056576 | tf_op jit(solution)/shard_map/while/body/eval_jaxpr/hqk,khd->qhd/dot_general | solution.py:121
  503.7 14.8 %fusion.134 = f32[8,512]{1,0:T(8,128)S(1)} fusion(pred[512,2560]{1,0:T(8,128)(4,1)S(1)} %compare_and_fusion.7, bf16[512,8,16]{0,2,1:T(8,128)(2,1)S(1)} %bitcast.99, bf16[2560,8,16]{0,2,1:T(8,128)(2,1)S(1)} %bitcast.96), kind=kOutput, calls=%fused_computation.154.clone.1 | convolution fusion | flops 377489920 | bytes 2113536 | tf_op jit(solution)/shard_map/while/body/eval_jaxpr/sub | solution.py:119
  518.5 16.2 %fusion.135 = f32[8,512,2560]{2,1,0:T(8,128)} fusion(bf16[512,8,16]{0,2,1:T(8,128)(2,1)S(1)} %bitcast.100, bf16[2560,8,16]{0,2,1:T(8,128)(2,1)S(1)} %bitcast.97), kind=kOutput, calls=%fused_computation.158.clone.1 | convolution fusion | flops 335544320 | bytes 42729472 | tf_op jit(solution)/shard_map/while/body/eval_jaxpr/qhd,khd->hqk/dot_general | solution.py:114
  535.0 18.0 %fusion.136 = bf16[8,16,512]{2,1,0:T(8,128)(2,1)S(1)} fusion(bf16[2560,8,16]{0,2,1:T(8,128)(2,1)S(1)} %bitcast.101, f32[8,512]{1,0:T(8,128)S(1)} %fusion.134, f32[8,512,2560]{2,1,0:T(8,128)} %fusion.135, pred[512,2560]{1,0:T(8,128)(4,1)S(1)} %compare_and_fusion.7), kind=kOutput, calls=%fused_computation.15.clone.1 | convolution fusion | flops 388045312 | bytes 44056576 | tf_op jit(solution)/shard_map/while/body/eval_jaxpr/hqk,khd->qhd/dot_general | solution.py:121
  560.1 14.8 %fusion.134 = f32[8,512]{1,0:T(8,128)S(1)} fusion(pred[512,2560]{1,0:T(8,128)(4,1)S(1)} %compare_and_fusion.7, bf16[512,8,16]{0,2,1:T(8,128)(2,1)S(1)} %bitcast.99, bf16[2560,8,16]{0,2,1:T(8,128)(2,1)S(1)} %bitcast.96), kind=kOutput, calls=%fused_computation.154.clone.1 | convolution fusion | flops 377489920 | bytes 2113536 | tf_op jit(solution)/shard_map/while/body/eval_jaxpr/sub | solution.py:119
  574.9 16.2 %fusion.135 = f32[8,512,2560]{2,1,0:T(8,128)} fusion(bf16[512,8,16]{0,2,1:T(8,128)(2,1)S(1)} %bitcast.100, bf16[2560,8,16]{0,2,1:T(8,128)(2,1)S(1)} %bitcast.97), kind=kOutput, calls=%fused_computation.158.clone.1 | convolution fusion | flops 335544320 | bytes 42729472 | tf_op jit(solution)/shard_map/while/body/eval_jaxpr/qhd,khd->hqk/dot_general | solution.py:114
  591.3 18.0 %fusion.136 = bf16[8,16,512]{2,1,0:T(8,128)(2,1)S(1)} fusion(bf16[2560,8,16]{0,2,1:T(8,128)(2,1)S(1)} %bitcast.101, f32[8,512]{1,0:T(8,128)S(1)} %fusion.134, f32[8,512,2560]{2,1,0:T(8,128)} %fusion.135, pred[512,2560]{1,0:T(8,128)(4,1)S(1)} %compare_and_fusion.7), kind=kOutput, calls=%fused_computation.15.clone.1 | convolution fusion | flops 388045312 | bytes 44056576 | tf_op jit(solution)/shard_map/while/body/eval_jaxpr/hqk,khd->qhd/dot_general | solution.py:121
  610.4 17.4 %all-gather.5.cloned.1.call-done = bf16[2048,256]{1,0:T(8,128)(2,1)} async-done(((bf16[2048,128]{1,0:T(8,128)(2,1)}), bf16[2048,256]{1,0:T(8,128)(2,1)}) %all-gather.5.cloned.1.call-update) | async-done | bytes 1048592 | tf_op jit(solution)/shard_map/all_gather | solution.py:129
  630.3 11.7 %fusion.42 = f32[2048,256]{0,1:T(8,128)} fusion(bf16[512,256]{1,0:T(8,128)(2,1)S(1)} %copy-done, bf16[256,512]{1,0:T(8,128)(2,1)S(1)} %copy-done.10, f32[512]{0:T(512)S(1)} %copy-done.12, bf16[2048,256]{0,1:T(8,128)(2,1)S(1)} %get-tuple-element.262, f32[256]{0:T(256)S(1)} %copy-done.15, f32[2048]{0:T(1024)S(1)} %add_rsqrt_fusion, ...), kind=kOutput, calls=%fused_computation.82 | convolution fusion | flops 1145569280 | bytes 3689472 | tf_op jit(solution)/shard_map/dot_general | solution.py:139
  642.1 18.4 %reduce-window.25 = s32[64,16,128]{2,1,0:T(8,128)S(1)} reduce-window(s32[64,16,128]{2,1,0:T(8,128)S(1)} %fusion.57, s32[]{:T(128)} %constant.195.clone.1), window={size=1x1x128 pad=0_0x0_0x127_0}, to_apply=%region_0.1 | reduce-window | flops 16646144 | bytes 1048580 | tf_op jit(solution)/shard_map/reduce-window.2
  669.8 18.3 %all_to_all.20 = s32[64,1,64]{2,1,0:T(1,128)S(1)} all-to-all(s32[64,1,64]{2,1,0:T(1,128)S(1)} %all_to_all.13), channel_id=1, replica_groups=mesh['pts'=64,'grp'=2] {'pts'}, dimensions={0} | all-to-all | bytes 32768 | tf_op jit(solution)/shard_map/all_to_all | solution.py:158
  690.7 14.6 %gather_fusion.1 = bf16[4096,256]{1,0:T(8,128)(2,1)S(1)} fusion(bf16[2048,256]{1,0:T(8,128)(2,1)S(1)} %copy.70, s32[4096]{0:T(1024)S(1)} %broadcast_clamp_fusion), kind=kCustom, calls=%fused_computation.1 | custom fusion | bytes 4210688 | tf_op jit(solution)/shard_map/jit(_take)/gather | solution.py:156
  711.8 27.7 %all-to-all-done.1 = bf16[64,64,256]{2,1,0:T(8,128)(2,1)S(1)} async-done(((bf16[64,64,256]{2,1,0:T(8,128)(2,1)}), bf16[64,64,256]{2,1,0:T(8,128)(2,1)S(1)}, u32[]{:S(2)}, u32[]{:S(2)}) %all-to-all-start.1) | async-done | bytes 2097184 | tf_op jit(solution)/shard_map/all_to_all | solution.py:161
  (183 shorter events, 169.8 us)
Async XLA Ops:
  6.5 623.7 %copy-start = (bf16[512,256]{1,0:T(8,128)(2,1)S(1)}, bf16[512,256]{1,0:T(8,128)(2,1)}, u32[]{:S(2)}) copy-start(bf16[512,256]{1,0:T(8,128)(2,1)} %param.40) | copy-start | bytes 786436
  6.5 10.8 %copy-start.1 = (bf16[2048,256]{1,0:T(8,128)(2,1)S(1)}, bf16[2048,256]{1,0:T(8,128)(2,1)}, u32[]{:S(2)}) copy-start(bf16[2048,256]{1,0:T(8,128)(2,1)} %param.23) | copy-start | bytes 3145732
  6.5 11.3 %copy-start.16 = (f32[128]{0:T(128)S(1)}, f32[128]{0:T(128)}, u32[]{:S(2)}) copy-start(f32[128]{0:T(128)} %param.28) | copy-start | bytes 1540
  6.5 351.1 %all-gather.3.cloned.1.call-start = ((), (), s32[]{:S(2)}) async-start(), calls=%async_computation.2 | async-start | bytes 1572864 | tf_op jit(solution)/shard_map/all_gather | solution.py:85
  7.6 7.7 %collective-permute-start = (bf16[256,256]{1,0:T(8,128)(2,1)S(1)}, bf16[256,256]{1,0:T(8,128)(2,1)S(1)}, u32[]{:S(2)}, u32[]{:S(2)}) collective-permute-start(bf16[256,256]{1,0:T(8,128)(2,1)S(1)} %get-tuple-element.254), channel_id=1, source_target_pairs={{0,2},{2,4},{4,6},{6,8},{8,10},{10,12},{12,14},{14,16},{16,18},{18... | collective-permute-start | bytes 393224 | tf_op jit(solution)/shard_map/ppermute | solution.py:15
  11.6 5.7 collective-permute-start.1
  17.8 320.4 %copy-start.2 = (bf16[2048,256]{1,0:T(8,128)(2,1)S(1)}, bf16[2048,256]{1,0:T(8,128)(2,1)}, u32[]{:S(2)}) copy-start(bf16[2048,256]{1,0:T(8,128)(2,1)} %param.23) | copy-start | bytes 3145732
  17.8 339.8 %copy-start.7 = (f32[256]{0:T(256)S(1)}, f32[256]{0:T(256)}, u32[]{:S(2)}) copy-start(f32[256]{0:T(256)} %param.30) | copy-start | bytes 3076
  337.4 0.8 copy-start.4
  337.4 22.2 %copy-start.8 = (f32[256]{0:T(256)S(1)}, f32[256]{0:T(256)}, u32[]{:S(2)}) copy-start(f32[256]{0:T(256)} %param.31) | copy-start | bytes 3076
  338.2 289.5 %all-gather.5.cloned.1.call-start = ((), (), s32[]{:S(2)}) async-start(), calls=%async_computation.3 | async-start | bytes 1572864 | tf_op jit(solution)/shard_map/all_gather | solution.py:129
  359.3 1.9 copy-start.11
  359.3 1.8 copy-start.13
  360.2 1.0 copy-start.3
  360.2 6.5 copy-start.5
  362.1 14.3 %collective-permute-start.2 = (bf16[1024,256]{1,0:T(8,128)(2,1)S(1)}, bf16[1024,256]{1,0:T(8,128)(2,1)S(1)}, u32[]{:S(2)}, u32[]{:S(2)}) collective-permute-start(bf16[1024,256]{1,0:T(8,128)(2,1)S(1)} %get-tuple-element.252), channel_id=1, source_target_pairs={{0,2},{2,4},{4,6},{6,8},{8,10},{10,12},{12,14},{14,16},{16,18},{18... | collective-permute-start | bytes 1572872 | tf_op jit(solution)/shard_map/ppermute | solution.py:15
  365.4 15.0 %collective-permute-start.3 = (bf16[1024,256]{1,0:T(8,128)(2,1)S(1)}, bf16[1024,256]{1,0:T(8,128)(2,1)}, u32[]{:S(2)}, u32[]{:S(2)}) collective-permute-start(bf16[1024,256]{1,0:T(8,128)(2,1)S(1)} %get-tuple-element.253), channel_id=1, source_target_pairs={{2,0},{4,2},{6,4},{8,6},{10,8},{12,10},{14,12},{16,14},{18,16},{20... | collective-permute-start | bytes 1572872 | tf_op jit(solution)/shard_map/ppermute | solution.py:18
  384.3 243.4 %copy-start.14 = (f32[256]{0:T(256)S(1)}, f32[256]{0:T(256)}, u32[]{:S(2)}) copy-start(f32[256]{0:T(256)} %param.36) | copy-start | bytes 3076
  610.1 20.1 %copy-start.10 = (bf16[256,512]{1,0:T(8,128)(2,1)S(1)}, bf16[256,512]{1,0:T(8,128)(2,1)}, u32[]{:S(2)}) copy-start(bf16[256,512]{1,0:T(8,128)(2,1)} %param.38) | copy-start | bytes 786436
  610.1 20.1 %copy-start.12 = (f32[512]{0:T(512)S(1)}, f32[512]{0:T(512)}, u32[]{:S(2)}) copy-start(f32[512]{0:T(512)} %param.39) | copy-start | bytes 6148
  610.1 20.1 %copy-start.15 = (f32[256]{0:T(256)S(1)}, f32[256]{0:T(256)}, u32[]{:S(2)}) copy-start(f32[256]{0:T(256)} %param.37) | copy-start | bytes 3076
  610.2 78.1 %all-reduce.2.cloned.1.call-start = ((), (), s32[]{:S(2)}) async-start(), calls=%async_computation.4 | async-start | bytes 4194304 | tf_op jit(solution)/shard_map/psum | solution.py:140
  630.3 11.7 %copy-start.6 = (s32[2048]{0:T(1024)S(1)}, s32[2048]{0:T(1024)}, u32[]{:S(2)}) copy-start(s32[2048]{0:T(1024)} %param.26) | copy-start | bytes 24580
  642.0 46.3 %copy-start.9 = (f32[256]{0:T(256)S(1)}, f32[256]{0:T(256)}, u32[]{:S(2)}) copy-start(f32[256]{0:T(256)} %param.41) | copy-start | bytes 3076
  707.1 32.4 %all-to-all-start.1 = ((bf16[64,64,256]{2,1,0:T(8,128)(2,1)}), bf16[64,64,256]{2,1,0:T(8,128)(2,1)S(1)}, u32[]{:S(2)}, u32[]{:S(2)}) async-start(bf16[64,64,256]{2,1,0:T(8,128)(2,1)} %broadcast_select_fusion.1), calls=%async_computation.1 | async-start | bytes 4194304 | tf_op jit(solution)/shard_map/all_to_all | solution.py:161
Sparse Core Ops, SparseCore 0:
  338.3 19.2 all-gather.2
  610.3 17.4 all-gather.4
  642.1 28.2 all-reduce.1
where the time goes:
time: 767 us; the launch traced here: 755 us
  local copies, waits for them, and re-layouts  318 us (41%)
  matrix products  235 us (31%)
  waiting for transfers between devices  76.9 us (10%)
  other arithmetic  72 us (9%)
  blocking collectives  18.3 us (2%)
  starting transfers between devices  14.7 us (2%)
  between operations  13.8 us (2%)
    gather x8, local copies, waits for them, and re-layouts, conv_block(): jnp.take(extended, picked, axis=0).reshape(block_rows, 27 * width)  200 us
    dot_general x4, matrix products, attend(): jnp.einsum('hqk,khd->qhd', attn_weights, value_blk, preferred_element_typ...  72.1 us
    dot_general x4, matrix products, attend(): jnp.einsum('qhd,khd->hqk', query_blk, key_blk, preferred_element_type=jnp...  64.7 us
    sub x4, matrix products, attend(): expo = jnp.exp(scores - row_max)  59.3 us
    select_n x4, local copies, waits for them, and re-layouts, conv_block(): jnp.take(extended, picked, axis=0).reshape(block_rows, 27 * width)  54.4 us
    select_n x4, other arithmetic, conv_block(): jnp.take(extended, picked, axis=0).reshape(block_rows, 27 * width)  32 us
    all_to_all x1, waiting for transfers between devices, local(): lax.all_to_all(picked_rows, 'pts', split_axis=0, concat_axis=0, tiled=True)  27.7 us
    dot_general x4, matrix products, conv_block(): jnp.dot(gathered, flat_conv, preferred_element_type=jnp.float32) + conv_b  22.3 us
  transfers between devices with their start and end apart: 8, of which 6 were waited for; matrix products, arithmetic and copies ran while one was open for 4% of the time, Pallas kernels for 0%

commit v1 on v0

v1 whole, which is shorter than its diff:
```python
import jax
import jax.numpy as jnp
from jax import lax
from jax.experimental import pallas as pl
from jax.experimental.pallas import tpu as pltpu
from jax.sharding import PartitionSpec as P

F32=jnp.float32; BF=jnp.bfloat16

Q_SCALE = 0.25 * 1.4426950408889634


def layer_norm(v, gain):
    c = v - jnp.mean(v, axis=-1, keepdims=True)
    s = jnp.mean(c * c, axis=-1, keepdims=True)
    return c * lax.rsqrt(s + 1e-05) * gain

RB=128
def conv_kernel(sc, pts, low, high, nb, wm, wo, cbm, cbo, cpw, cpb, cpg, n1g, sec_o, nrm_o, X, OH, G, W):
    g = sc[0]
    base = sc[1]
    X[0:256, :] = low[...]
    X[256:2304, :] = pts[...]
    X[2304:2560, :] = high[...]
    W[:, 0:128] = wm[...]
    W[:, 128:256] = wo[...]
    lanes = lax.broadcasted_iota(jnp.int32, (RB, 768), 1).astype(jnp.int32)
    def block(b, _):
        rel = []
        for j in range(RB // 32):
            rel.append(nb[pl.ds(pl.multiple_of(256 * b + 64 * j + 32 * g, 32), 32), :])
        rel = jnp.concatenate(rel, axis=0)
        off = base + 256 * b - 256
        rel = jnp.where(rel < 0, -1, rel - off).astype(jnp.int32)
        for t in range(27):
            col = rel[:, t:t + 1]
            OH[t * RB:(t + 1) * RB, :] = jnp.where(lanes == col, jnp.array(1, BF), jnp.array(0, BF))
        win = X[pl.ds(pl.multiple_of(256 * b, 256), 768), :]
        for q in range(3):
            out = jnp.dot(OH[q * 9 * RB:(q + 1) * 9 * RB, :], win, preferred_element_type=F32).astype(BF)
            for t in range(9):
                G[pl.ds(pl.multiple_of(b * RB, RB), RB), (q * 9 + t) * 256:(q * 9 + t + 1) * 256] = out[t * RB:(t + 1) * RB, :]
        return 0
    lax.fori_loop(0, 1024 // RB, block, 0)
    cb = jnp.concatenate([cbm[...], cbo[...]], axis=1)
    cpw_s = jnp.concatenate([cpw[pl.ds(pl.multiple_of(128 * g, 128), 128), :], cpw[pl.ds(pl.multiple_of(128 - 128 * g, 128), 128), :]], axis=0)
    def fin(m, _):
        r0 = pl.multiple_of(m * 256, 256)
        acc = jnp.dot(G[pl.ds(r0, 256), :], W[...], preferred_element_type=F32)
        conv = (acc + cb).astype(BF)
        c = jnp.dot(conv, cpw_s, preferred_element_type=F32) + cpb[...]
        own = []
        for j in range(8):
            own.append(pts[pl.ds(pl.multiple_of(512 * m + 64 * j + 32 * g, 32), 32), :])
        own = jnp.concatenate(own, axis=0).astype(F32)
        sec = (own + layer_norm(c, cpg[...])).astype(BF)
        sec_o[pl.ds(r0, 256), :] = sec
        nrm_o[pl.ds(r0, 256), :] = layer_norm(sec.astype(F32), n1g[...]).astype(BF)
        return 0
    lax.fori_loop(0, 4, fin, 0)
def conv_call(sc, pts, low, high, nb, wm, wo, cbm, cbo, cpw, cpb, cpg, n1g):
    sm=pl.BlockSpec(memory_space=pltpu.SMEM); vm=pl.BlockSpec(memory_space=pltpu.VMEM)
    return pl.pallas_call(conv_kernel,
        out_shape=[jax.ShapeDtypeStruct((1024,256),BF)]*2,
        in_specs=[sm]+[vm]*12, out_specs=[vm]*2,
        scratch_shapes=[pltpu.VMEM((2560,256),BF),pltpu.VMEM((27*RB,768),BF),pltpu.VMEM((1024,6912),BF),pltpu.VMEM((6912,256),BF)],
        compiler_params=pltpu.CompilerParams(vmem_limit_bytes=50*2**20),
        cost_estimate=pl.CostEstimate(flops=30*10**9,bytes_accessed=8*10**6,transcendentals=0),
        name="conv")(sc, pts, low, high, nb, wm, wo, cbm, cbo, cpw, cpb, cpg, n1g)


def attn_kernel(
    sc, sel, plen, own, oth, lo_own, lo_oth, hi_own, hi_oth, sec, qkvm, qkvo, qbm, qbo, prw, prb,
    n2g, f1m, f1o, b1m, b1o, f2m, f2o, f2b, send, NE, KT, V, Q8, ACC, OUT, M,
):
    g = sc[0]
    base = sc[1]
    total = sc[2]
    mine = pl.multiple_of(32 * g, 32)
    theirs = pl.multiple_of(32 - 32 * g, 32)

    def spread(count, first, a_ref, b_ref):
        def step(c, _):
            src = pl.multiple_of(32 * c, 32)
            row = first + 64 * c
            NE[pl.ds(pl.multiple_of(row + mine, 32), 32), :] = a_ref[pl.ds(src, 32), :]
            NE[pl.ds(pl.multiple_of(row + theirs, 32), 32), :] = b_ref[pl.ds(src, 32), :]
            return 0

        lax.fori_loop(0, count, step, 0, unroll=4)

    spread(16, 0, lo_own, lo_oth)
    spread(32, 1024, own, oth)
    spread(16, 3072, hi_own, hi_oth)

    wkt = [jnp.transpose(w[:, 128:256]) for w in (qkvm, qkvo)]
    bkc = [jnp.transpose(jnp.broadcast_to(b[:, 128:256], (8, 128)))[:, :1] for b in (qbm, qbo)]
    wv = jnp.concatenate([qkvm[:, 256:384], qkvo[:, 256:384]], axis=1)
    bv = jnp.concatenate([qbm[:, 256:384], qbo[:, 256:384]], axis=1)

    def key_value(i, most):
        r0 = pl.multiple_of(i * 256, 256)
        rows = NE[pl.ds(r0, 256), :]
        for h in range(2):
            kt = (
                lax.dot_general(
                    wkt[h], rows, (((1,), (1,)), ((), ())), preferred_element_type=F32
                )
                + bkc[h]
            )
            most = jnp.maximum(most, jnp.sum((kt * kt).reshape(8, 16, 256), axis=1))
            KT[128 * h : 128 * h + 128, pl.ds(r0, 256)] = kt.astype(BF)
        V[pl.ds(r0, 256), :] = (jnp.dot(rows, wv, preferred_element_type=F32) + bv).astype(BF)
        return most

    key_most = jnp.max(lax.fori_loop(0, 16, key_value, jnp.zeros((8, 256), F32)))

    lens = jnp.broadcast_to(plen[...].astype(F32), (256, 256))
    sub = lax.broadcasted_iota(jnp.int32, (256, 256), 0)
    lane = lax.broadcasted_iota(jnp.int32, (256, 256), 1)
    ends_col = jnp.sum(jnp.where(lane <= sub, lens, 0.0), axis=1, keepdims=True)
    ends_row = jnp.sum(jnp.where(lane == sub, ends_col, 0.0), axis=0, keepdims=True)
    starts_row = ends_row - plen[...].astype(F32)

    wq = jnp.concatenate([qkvm[:, 0:128], qkvo[:, 0:128]], axis=1)
    bq = jnp.concatenate([qbm[:, 0:128], qbo[:, 0:128]], axis=1)
    hs = lax.broadcasted_iota(jnp.int32, (256, 128), 0) // 16
    hl = lax.broadcasted_iota(jnp.int32, (256, 128), 1)
    head_sel = jnp.where(hs == hl, 1.0, 0.0).astype(BF)
    k_low = jnp.where(
        lax.broadcasted_iota(jnp.int32, (32, 128), 0) < 16, 1.0, 0.0
    ).astype(BF)
    k_high = (1.0 - k_low.astype(F32)).astype(BF)
    col_head = lax.broadcasted_iota(jnp.int32, (128, 128), 1) // 16
    cols = [jnp.where(col_head == a, 1.0, 0.0).astype(BF) for a in range(8)]
    prw_s = jnp.concatenate(
        [
            prw[pl.ds(pl.multiple_of(128 * g, 128), 128), :],
            prw[pl.ds(pl.multiple_of(128 - 128 * g, 128), 128), :],
        ],
        axis=0,
    )

    def q_block(qb, _):
        r0 = pl.multiple_of(qb * 256, 256)
        q = (jnp.dot(own[pl.ds(r0, 256), :], wq, preferred_element_type=F32) + bq) * Q_SCALE
        q = q.astype(BF)
        for p in range(8):
            Q8[p] = q[:, 32 * p : 32 * p + 32]
        q_most = jnp.max(jnp.dot(q * q, head_sel, preferred_element_type=F32))
        calm = q_most * key_most * 1.05 <= 1e4
        r = lax.broadcasted_iota(jnp.int32, (256, 1), 0)
        row = (base + 512 * qb + 64 * (r // 32) + 32 * g + r % 32).astype(F32)
        first = jnp.max(jnp.where(starts_row <= row, starts_row, 0.0), axis=1, keepdims=True)
        finish = jnp.min(
            jnp.where(ends_row > row, ends_row, total.astype(F32)), axis=1, keepdims=True
        )
        shift = (1024 - base).astype(F32)
        first = (first + shift).astype(jnp.int32)
        finish = (finish + shift).astype(jnp.int32)
        kb0 = jnp.maximum(jnp.min(first) // 128, 0)
        kb1 = jnp.minimum((jnp.max(finish) + 127) // 128, 32)

        def scores(kb, p, kt, madd):
            part = kt[32 * p : 32 * p + 32, :]
            pair = jnp.concatenate([part * k_low, part * k_high], axis=1)
            s = jnp.dot(Q8[p], pair, preferred_element_type=F32)
            return s + madd

        def mask(kb):
            key = kb * 128 + lax.broadcasted_iota(jnp.int32, (256, 128), 1)
            madd = jnp.where((key >= first) & (key < finish), 0.0, -jnp.inf)
            return jnp.concatenate([madd, madd], axis=1)

        def attend(use_max):
            def step(kb, _):
                k0 = pl.multiple_of(kb * 128, 128)
                kt = KT[:, pl.ds(k0, 128)]
                vb = V[pl.ds(k0, 128), :]
                madd = mask(kb)
                for h in range(2):
                    vh = vb[:, 128 * h : 128 * h + 128]
                    ps, vs = [], []
                    for a in range(4):
                        p = 4 * h + a
                        s = scores(kb, p, kt, madd)
                        if use_max:
                            s = s - M[p]
                        ps.append(jnp.exp2(s).astype(BF))
                        for c in (cols[2 * a], cols[2 * a + 1]):
                            vs.append(jnp.concatenate([vh * c, c], axis=1))
                    ACC[h] += jnp.dot(
                        jnp.concatenate(ps, axis=1),
                        jnp.concatenate(vs, axis=0),
                        preferred_element_type=F32,
                    )
                return 0

            lax.fori_loop(kb0, kb1, step, 0)

        ACC[...] = jnp.zeros_like(ACC)

        @pl.when(calm)
        def _():
            attend(False)

        @pl.when(jnp.logical_not(calm))
        def _():
            M[...] = jnp.full(M.shape, -jnp.inf, F32)

            def top(kb, _):
                kt = KT[:, pl.ds(pl.multiple_of(kb * 128, 128), 128)]
                madd = mask(kb)
                for p in range(8):
                    M[p] = jnp.maximum(M[p], scores(kb, p, kt, madd))
                return 0

            lax.fori_loop(kb0, kb1, top, 0)
            for p in range(8):
                for h in range(2):
                    part = M[p, :, 128 * h : 128 * h + 128]
                    M[p, :, 128 * h : 128 * h + 128] = jnp.broadcast_to(
                        jnp.max(part, axis=1, keepdims=True), (256, 128)
                    )
            attend(True)

        attn = jnp.concatenate(
            [ACC[h, :, 0:128] / ACC[h, :, 128:256] for h in range(2)], axis=1
        ).astype(BF)
        two = (
            sec[pl.ds(r0, 256), :].astype(F32)
            + jnp.dot(attn, prw_s, preferred_element_type=F32)
            + prb[...]
        ).astype(BF)
        wide = two.astype(F32)
        normed = layer_norm(wide, n2g[...]).astype(BF)
        total_rows = wide + f2b[...]
        for f1, b1, f2 in ((f1m, b1m, f2m), (f1o, b1o, f2o)):
            x = jnp.dot(normed, f1[...], preferred_element_type=F32) + b1[...]
            x = (0.5 * x * (1.0 + lax.erf(x * 0.7071067811865476))).astype(BF)
            total_rows = total_rows + jnp.dot(x, f2[...], preferred_element_type=F32)
        OUT[pl.ds(r0, 256), :] = total_rows.astype(BF)
        return 0

    lax.fori_loop(0, 4, q_block, 0)

    def place(d, _):
        send[pl.ds(pl.multiple_of(32 * d, 32), 32), :] = OUT[
            pl.ds(pl.multiple_of(32 * sel[d], 32), 32), :
        ]
        return 0

    lax.fori_loop(0, 64, place, 0, unroll=4)


def attn_call(*args):
    smem, vmem = pl.BlockSpec(memory_space=pltpu.SMEM), pl.BlockSpec(memory_space=pltpu.VMEM)
    return pl.pallas_call(
        attn_kernel,
        out_shape=jax.ShapeDtypeStruct((2048, 256), BF),
        in_specs=[smem] * 2 + [vmem] * (len(args) - 2),
        out_specs=vmem,
        scratch_shapes=[
            pltpu.VMEM((4096, 256), BF),
            pltpu.VMEM((256, 4096), BF),
            pltpu.VMEM((4096, 256), BF),
            pltpu.VMEM((8, 256, 32), BF),
            pltpu.VMEM((2, 256, 256), F32),
            pltpu.VMEM((1024, 256), BF),
            pltpu.VMEM((8, 256, 256), F32),
        ],
        compiler_params=pltpu.CompilerParams(vmem_limit_bytes=48 * 2**20),
        cost_estimate=pl.CostEstimate(
            flops=60 * 10**9, bytes_accessed=8 * 10**6, transcendentals=2 * 10**7
        ),
        name="attention",
    )(*args)


def last_kernel(sc, src, inner, own, oth, out):
    g = sc[0]
    place = inner[...]
    place = place % 32 + jnp.where(place // 32 == g, 0, 32)
    perm = jnp.where(
        lax.broadcasted_iota(jnp.int32, (64, 64), 1) == place, 1.0, 0.0
    ).astype(BF)

    def step(k, _):
        s = pl.multiple_of(32 * src[k], 32)
        rows = jnp.concatenate([own[pl.ds(s, 32), :], oth[pl.ds(s, 32), :]], axis=0)
        out[pl.ds(pl.multiple_of(64 * k, 64), 64), :] = jnp.dot(
            perm, rows, preferred_element_type=F32
        ).astype(BF)
        return 0

    lax.fori_loop(0, 32, step, 0, unroll=4)


def last_call(*args):
    smem, vmem = pl.BlockSpec(memory_space=pltpu.SMEM), pl.BlockSpec(memory_space=pltpu.VMEM)
    return pl.pallas_call(
        last_kernel,
        out_shape=jax.ShapeDtypeStruct((2048, 256), BF),
        in_specs=[smem] * 2 + [vmem] * 3,
        out_specs=vmem,
        compiler_params=pltpu.CompilerParams(vmem_limit_bytes=16 * 2**20),
        name="relabel",
    )(*args)


def local(
    points, neighbours, patch_len, zorder, conv_w, conv_b, cpe_w, cpe_b, cpe_gain, norm1_gain,
    qkv_w, qkv_b, proj_w, proj_b, norm2_gain, fc1_w, fc1_b, fc2_w, fc2_b,
):
    g = lax.axis_index("grp").astype(jnp.int32)
    me = lax.axis_index("pts").astype(jnp.int32)
    peers = lax.axis_size("pts")
    rows = points.shape[0]
    forward = [(i, i + 1) for i in range(peers - 1)]
    backward = [(i + 1, i) for i in range(peers - 1)]

    def swap(x):
        return lax.ppermute(x, "grp", [(0, 1), (1, 0)])

    low = lax.ppermute(points[rows - 256 :], "pts", forward)
    high = lax.ppermute(points[:256], "pts", backward)
    conv_m = conv_w.reshape(27 * 256, 128)
    conv_o = swap(conv_m)
    small = jnp.concatenate([conv_b, qkv_b.reshape(384), fc1_b])
    small_o = swap(small)
    run = zorder[::64] // 64
    table = lax.all_gather(
        jnp.broadcast_to(jnp.pad(run, (0, 96))[None, :], (64, 128)), "pts", axis=0, tiled=True
    ).reshape(peers, 64, 128)[:, 0, :32]
    qkv_m = qkv_w.reshape(256, 384)
    qkv_o, fc1_o, fc2_o = swap(qkv_m), swap(fc1_w), swap(fc2_w)

    scalars = jnp.stack([g, me * rows, jnp.int32(rows * peers)])
    section_one, normed = conv_call(
        scalars, points, low, high, neighbours, conv_m, conv_o, small[None, :128],
        small_o[None, :128], cpe_w, cpe_b[None], cpe_gain[None], norm1_gain[None],
    )
    other = swap(normed)
    lo_own = lax.ppermute(normed[512:], "pts", forward)
    hi_own = lax.ppermute(normed[:512], "pts", backward)
    lo_oth, hi_oth = swap(lo_own), swap(hi_own)
    sel = jnp.max(jnp.where(table // 32 == me, table % 32, 0), axis=1)
    send = attn_call(
        scalars, sel, patch_len[None], normed, other, lo_own, lo_oth, hi_own, hi_oth, section_one,
        qkv_m, qkv_o, small[None, 128:512], small_o[None, 128:512], proj_w, proj_b[None],
        norm2_gain[None], fc1_w, fc1_o, small[None, 512:], small_o[None, 512:], fc2_w, fc2_o,
        fc2_b[None],
    )
    got = lax.all_to_all(send, "pts", split_axis=0, concat_axis=0, tiled=True)
    return last_call(scalars, run // 32, (zorder[:64] % 64)[:, None], got, swap(got))


def solution(mesh):
    placed = (
        P("pts", None), P("pts", None), P(), P("pts"), P(None, None, "grp"), P("grp"), P(), P(), P(),
        P(), P(None, None, "grp"), P(None, "grp"), P(), P(), P(), P(None, "grp"), P("grp"),
        P("grp", None), P(),
    )
    return jax.shard_map(
        local, mesh=mesh, in_specs=placed, out_specs=P("pts", None), check_vma=False
    )
```

time: 767 us -> 171 us (0.22); the launches traced: 755 us -> 170 us
  local copies, waits for them, and re-layouts: 318 us -> 8.78 us
  matrix products: 235 us -> 0 us
  other arithmetic: 72 us -> 1.64 us
  Pallas kernels: 0 us -> 67.7 us
  waiting for transfers between devices: 76.9 us -> 28.7 us
  blocking collectives: 18.3 us -> 30.1 us
    gather x10 -> x0, local copies, waits for them, and re-layouts: 222 us -> none  [the longest x8 200 us: conv_block(): jnp.take(extended, picked, axis=0).reshape(block_rows, 27 * width)]
    dot_general x16 -> x0, matrix products: 176 us -> none  [the longest x4 72.1 us: attend(): jnp.einsum('hqk,khd->qhd', attn_weights, value_blk, preferred_element_typ...]
    pallas_call x0 -> x3, Pallas kernels: none -> 67.7 us  [the longest x1 42.9 us: attn_call(): pl.pallas_call(attn_kernel, out_shape=jax.ShapeDtypeStruct((2048, 256), B...]
    sub x4 -> x0, matrix products: 59.3 us -> none  [attend(): expo = jnp.exp(scores - row_max)]
    select_n x5 -> x0, local copies, waits for them, and re-layouts: 54.4 us -> none  [the longest x4 54.4 us: conv_block(): jnp.take(extended, picked, axis=0).reshape(block_rows, 27 * width)]
    select_n x8 -> x1, other arithmetic: 36.1 us -> 0.02 us  [local(): run // 32]
    all_to_all x1 -> x0, waiting for transfers between devices: 27.7 us -> none  [local(): lax.all_to_all(picked_rows, 'pts', split_axis=0, concat_axis=0, tiled=True)]
    another operation x4 -> x1, other arithmetic: 18.9 us -> 0.08 us  [local(): scalars = jnp.stack([g, me * rows, jnp.int32(rows * peers)])]
  transfers between devices with their start and end apart: 8 -> 14, of which waited for: 6 -> 5; matrix products, arithmetic and copies ran while one was open for 4% -> 5% of each run, Pallas kernels for 0% -> 13%
where the time goes in v1:
time: 171 us; the launch traced here: 170 us
  Pallas kernels  67.7 us (40%)
  blocking collectives  30.1 us (18%)
  waiting for transfers between devices  28.7 us (17%)
  starting transfers between devices  19.2 us (11%)
  between operations  13.8 us (8%)
  local copies, waits for them, and re-layouts  8.78 us (5%)
    pallas_call x1, Pallas kernels, attn_call(): pl.pallas_call(attn_kernel, out_shape=jax.ShapeDtypeStruct((2048, 256), B...  42.9 us
    all_to_all x1, blocking collectives, local(): got = lax.all_to_all(send, 'pts', split_axis=0, concat_axis=0, tiled=True)  30.1 us
    pallas_call x1, Pallas kernels, conv_call(): pl.pallas_call(conv_kernel, out_shape=[jax.ShapeDtypeStruct((1024, 256),...  21.8 us
    all_gather x1, waiting for transfers between devices, local(): lax.all_gather(jnp.broadcast_to(jnp.pad(run, (0, 96))[None, :], (64, 128)...  21.2 us
    ppermute x9, starting transfers between devices, swap(): return lax.ppermute(x, 'grp', [(0, 1), (1, 0)])  10.1 us
    unnamed x41, local copies, waits for them, and re-layouts  5.1 us
  transfers between devices with their start and end apart: 14, of which 5 were waited for; matrix products, arithmetic and copies ran while one was open for 5% of the time, Pallas kernels for 13%

profile of v1, /device:TPU:1, one launch (start us, length us, event | category | flops | bytes accessed | tf_op | source)
XLA Modules:
  0.0 169.8 jit_solution(3310698225175472339)
XLA Ops:
  6.6 1.5 collective-permute-start.2
  8.1 0.8 slice.30
  8.9 0.6 broadcast_in_dim.48
  9.6 1.0 fusion.7
  10.6 3.2 %collective-permute-start = (bf16[256,256]{1,0:T(8,128)(2,1)S(1)}, bf16[256,256]{1,0:T(8,128)(2,1)S(1)}, u32[]{:S(2)}, u32[]{:S(2)}) collective-permute-start(bf16[256,256]{1,0:T(8,128)(2,1)S(1)} %get-tuple-element.12), channel_id=1, source_target_pairs={{0,2},{2,4},{4,6},{6,8},{8,10},{10,12},{12,14},{14,16},{16,18},{18... | collective-permute-start | bytes 393224 | tf_op jit(solution)/shard_map/ppermute | solution.py:325
  13.8 1.3 collective-permute-start.1
  15.1 0.7 pad_maximum_fusion
  15.8 0.4 collective-permute-start.3
  16.2 1.3 copy.34.nb
  17.6 2.8 %collective-permute-done.1.high = bf16[256,256]{1,0:T(8,128)(2,1)S(1)} collective-permute-done((bf16[256,256]{1,0:T(8,128)(2,1)S(1)}, bf16[256,256]{1,0:T(8,128)(2,1)S(1)}, u32[]{:S(2)}, u32[]{:S(2)}) %collective-permute-start.1) | collective-permute-done | bytes 131104 | tf_op jit(solution)/shard_map/ppermute | solution.py:326
  20.5 21.8 %conv.1 = (bf16[1024,256]{1,0:T(8,128)(2,1)S(1)}, bf16[1024,256]{1,0:T(8,128)(2,1)S(1)}) custom-call(s32[3]{0:T(128)S(1)} %pad_add_fusion.sc, bf16[2048,256]{1,0:T(8,128)(2,1)S(1)} %copy-done, bf16[256,256]{1,0:T(8,128)(2,1)S(1)} %collective-permute-done.low, bf16[256,256]{1,0:T(8,128)(2,1)S(1)} %collective-permute-done.1.high, s32[2048,27]{1,0:T(8,128)S(1)} %copy.34.nb, ...), custom_call_target="tpu_custom_call" | custom-call | flops 30000001024 | bytes 8000000 | tf_op jit(solution)/shard_map/conv/pallas_call | solution.py:63
  42.4 3.3 %collective-permute-start.5 = (bf16[512,256]{1,0:T(8,128)(2,1)S(1)}, bf16[512,256]{1,0:T(8,128)(2,1)S(1)}, u32[]{:S(2)}, u32[]{:S(2)}) collective-permute-start(bf16[512,256]{1,0:T(8,128)(2,1)S(1)} %get-tuple-element.14), channel_id=1, source_target_pairs={{0,2},{2,4},{4,6},{6,8},{8,10},{10,12},{12,14},{14,16},{16,18},{18... | collective-permute-start | bytes 786440 | tf_op jit(solution)/shard_map/ppermute | solution.py:344
  45.7 1.3 collective-permute-start.7
  47.0 1.5 collective-permute-start.4
  48.5 1.1 copy.35
  49.6 0.2 copy.37.qkvm
  49.9 0.5 collective-permute-start.10
  50.4 0.9 collective-permute-done.9.qkvo
  51.3 0.7 copy-done.5
  52.1 0.5 collective-permute-start.6
  52.7 2.2 %collective-permute-done.7.hi_own = bf16[512,256]{1,0:T(8,128)(2,1)S(1)} collective-permute-done((bf16[512,256]{1,0:T(8,128)(2,1)S(1)}, bf16[512,256]{1,0:T(8,128)(2,1)S(1)}, u32[]{:S(2)}, u32[]{:S(2)}) %collective-permute-start.7) | collective-permute-done | bytes 262176 | tf_op jit(solution)/shard_map/ppermute | solution.py:345
  54.9 2.2 %collective-permute-start.8 = (bf16[512,256]{1,0:T(8,128)(2,1)S(1)}, bf16[512,256]{1,0:T(8,128)(2,1)S(1)}, u32[]{:S(2)}, u32[]{:S(2)}) collective-permute-start(bf16[512,256]{1,0:T(8,128)(2,1)S(1)} %collective-permute-done.7.hi_own), channel_id=1, source_target_pairs={{0,1},{1,0},{2,3},{3,2},{4,5},{5,4},{6,7},{7,6},{8,9},{9,8},{10,11... | collective-permute-start | bytes 786440 | tf_op jit(solution)/shard_map/ppermute | solution.py:323
  57.1 21.2 %all-gather.2.cloned.1.call-done = s32[4096,128]{1,0:T(8,128)} async-done(((s32[64,128]{1,0:T(8,128)}), s32[4096,128]{1,0:T(8,128)}) %all-gather.2.cloned.1.call-update) | async-done | bytes 2097168 | tf_op jit(solution)/shard_map/all_gather | solution.py:332
  78.3 1.0 slice.40
  79.5 0.9 copy-done.6
  80.4 1.0 copy-done.17
  81.5 42.9 %attention.1 = bf16[2048,256]{1,0:T(8,128)(2,1)S(1)} custom-call(s32[3]{0:T(128)S(1)} %pad_add_fusion.sc, s32[64]{0:T(128)S(1)} %fusion.2.sel, s32[1,256]{1,0:T(1,128)S(1)} %bitcast.38, bf16[1024,256]{1,0:T(8,128)(2,1)S(1)} %get-tuple-element.7.own, bf16[1024,256]{1,0:T(8,128)(2,1)S(1)} %collective-permute-done.4.oth, ...), custom_call_target="tpu_custom_call" | custom-call | flops 60000002048 | bytes 8000000 | tf_op jit(solution)/shard_map/attention/pallas_call | solution.py:258
  124.4 30.1 %all_to_all.11 = bf16[64,32,256]{2,1,0:T(8,128)(2,1)S(1)} all-to-all(bf16[64,32,256]{2,1,0:T(8,128)(2,1)S(1)} %bitcast.30), channel_id=1, replica_groups=mesh['pts'=64,'grp'=2] {'pts'}, dimensions={0} | all-to-all | bytes 2097152 | tf_op jit(solution)/shard_map/all_to_all | solution.py:354
  154.5 3.2 %collective-permute-start.12 = (bf16[2048,256]{1,0:T(8,128)(2,1)S(1)}, bf16[2048,256]{1,0:T(8,128)(2,1)S(1)}, u32[]{:S(2)}, u32[]{:S(2)}) collective-permute-start(bf16[2048,256]{1,0:T(8,128)(2,1)S(1)} %bitcast.28), channel_id=1, source_target_pairs={{0,1},{1,0},{2,3},{3,2},{4,5},{5,4},{6,7},{7,6},{8,9},{9,8},{10,11... | collective-permute-start | bytes 3145736 | tf_op jit(solution)/shard_map/ppermute | solution.py:323
  157.7 0.7 fusion.5
  158.5 1.5 collective-permute-done.12.oth
  160.0 3.0 %relabel.1 = bf16[2048,256]{1,0:T(8,128)(2,1)} custom-call(s32[3]{0:T(128)S(1)} %pad_add_fusion.sc, s32[32]{0:T(128)S(1)} %get-tuple-element.9.src, s32[64,1]{1,0:T(8,128)S(1)} %copy.38.inner, bf16[2048,256]{1,0:T(8,128)(2,1)S(1)} %bitcast.29, bf16[2048,256]{1,0:T(8,128)(2,1)S(1)} %collective-permute-done.12.oth), custom_call_target="tpu_custom_call" | custom-call | tf_op jit(solution)/shard_map/relabel/pallas_call | solution.py:301
  (59 shorter events, 0.8 us)
Async XLA Ops:
  6.5 13.9 %copy-start = (bf16[2048,256]{1,0:T(8,128)(2,1)S(1)}, bf16[2048,256]{1,0:T(8,128)(2,1)}, u32[]{:S(2)}) copy-start(bf16[2048,256]{1,0:T(8,128)(2,1)} %pts.1) | copy-start | bytes 3145732
  6.5 13.9 %copy-start.2 = (f32[128]{0:T(128)S(1)}, f32[128]{0:T(128)}, u32[]{:S(2)}) copy-start(f32[128]{0:T(128)} %param.24) | copy-start | bytes 1540
  6.5 13.9 %copy-start.7 = (bf16[256,256]{1,0:T(8,128)(2,1)S(1)}, bf16[256,256]{1,0:T(8,128)(2,1)}, u32[]{:S(2)}) copy-start(bf16[256,256]{1,0:T(8,128)(2,1)} %cpw.1) | copy-start | bytes 393220
  6.5 13.9 %copy-start.9 = (f32[256]{0:T(256)S(1)}, f32[256]{0:T(256)}, u32[]{:S(2)}) copy-start(f32[256]{0:T(256)} %param.26) | copy-start | bytes 3076
  6.5 13.9 %copy-start.10 = (f32[256]{0:T(256)S(1)}, f32[256]{0:T(256)}, u32[]{:S(2)}) copy-start(f32[256]{0:T(256)} %param.27) | copy-start | bytes 3076
  6.5 13.9 %copy-start.11 = (f32[256]{0:T(256)S(1)}, f32[256]{0:T(256)}, u32[]{:S(2)}) copy-start(f32[256]{0:T(256)} %param.28) | copy-start | bytes 3076
  6.6 71.7 %all-gather.2.cloned.1.call-start = ((), (), s32[]{:S(2)}) async-start(), calls=%async_computation.1 | async-start | bytes 2129920 | tf_op jit(solution)/shard_map/all_gather | solution.py:332
  6.6 13.8 %collective-permute-start.2 = (bf16[6912,128]{1,0:T(8,128)(2,1)}, bf16[6912,128]{1,0:T(8,128)(2,1)}, u32[]{:S(2)}, u32[]{:S(2)}) collective-permute-start(bf16[6912,128]{1,0:T(8,128)(2,1)} %bitcast.47), channel_id=1, source_target_pairs={{0,1},{1,0},{2,3},{3,2},{4,5},{5,4},{6,7},{7,6},{8,9},{9,8},{10,11... | collective-permute-start | bytes 5308424 | tf_op jit(solution)/shard_map/ppermute | solution.py:323
  10.6 7.0 %collective-permute-start = (bf16[256,256]{1,0:T(8,128)(2,1)S(1)}, bf16[256,256]{1,0:T(8,128)(2,1)S(1)}, u32[]{:S(2)}, u32[]{:S(2)}) collective-permute-start(bf16[256,256]{1,0:T(8,128)(2,1)S(1)} %get-tuple-element.12), channel_id=1, source_target_pairs={{0,2},{2,4},{4,6},{6,8},{8,10},{10,12},{12,14},{14,16},{16,18},{18... | collective-permute-start | bytes 393224 | tf_op jit(solution)/shard_map/ppermute | solution.py:325
  13.8 6.6 %collective-permute-start.1 = (bf16[256,256]{1,0:T(8,128)(2,1)S(1)}, bf16[256,256]{1,0:T(8,128)(2,1)S(1)}, u32[]{:S(2)}, u32[]{:S(2)}) collective-permute-start(bf16[256,256]{1,0:T(8,128)(2,1)S(1)} %get-tuple-element.11), channel_id=1, source_target_pairs={{2,0},{4,2},{6,4},{8,6},{10,8},{12,10},{14,12},{16,14},{18,16},{20... | collective-permute-start | bytes 393224 | tf_op jit(solution)/shard_map/ppermute | solution.py:326
  15.8 1.7 %collective-permute-start.3 = (f32[1024]{0:T(1024)S(1)}, f32[1024]{0:T(1024)S(1)}, u32[]{:S(2)}, u32[]{:S(2)}) collective-permute-start(f32[1024]{0:T(1024)S(1)} %pad_maximum_fusion), channel_id=1, source_target_pairs={{0,1},{1,0},{2,3},{3,2},{4,5},{5,4},{6,7},{7,6},{8,9},{9,8},{10,11... | collective-permute-start | bytes 12296 | tf_op jit(solution)/shard_map/ppermute | solution.py:323
  42.3 3.4 %copy-start.16 = (bf16[1024,256]{1,0:T(8,128)(2,1)}, bf16[1024,256]{1,0:T(8,128)(2,1)S(1)}, u32[]{:S(2)}) copy-start(bf16[1024,256]{1,0:T(8,128)(2,1)S(1)} %get-tuple-element.8.sec) | copy-start | bytes 1572868
  42.3 7.6 %copy-start.3 = (bf16[256,512]{1,0:T(8,128)(2,1)S(1)}, bf16[256,512]{1,0:T(8,128)(2,1)}, u32[]{:S(2)}) copy-start(bf16[256,512]{1,0:T(8,128)(2,1)} %f1m.1) | copy-start | bytes 786436
  42.3 9.7 %copy-start.4 = (bf16[512,256]{1,0:T(8,128)(2,1)S(1)}, bf16[512,256]{1,0:T(8,128)(2,1)}, u32[]{:S(2)}) copy-start(bf16[512,256]{1,0:T(8,128)(2,1)} %f2m.1) | copy-start | bytes 786436
  42.3 14.8 %copy-start.18 = (f32[3,128]{1,0:T(4,128)S(1)}, f32[3,128]{1,0:T(4,128)}, u32[]{:S(2)}) copy-start(f32[3,128]{1,0:T(4,128)} %param.30) | copy-start | bytes 4612
  42.3 37.1 %copy-start.1 = (f32[512]{0:T(512)S(1)}, f32[512]{0:T(512)}, u32[]{:S(2)}) copy-start(f32[512]{0:T(512)} %param.35) | copy-start | bytes 6148
  42.3 37.1 %copy-start.8 = (bf16[256,256]{1,0:T(8,128)(2,1)S(1)}, bf16[256,256]{1,0:T(8,128)(2,1)}, u32[]{:S(2)}) copy-start(bf16[256,256]{1,0:T(8,128)(2,1)} %prw.1) | copy-start | bytes 393220
  42.3 37.1 %copy-start.12 = (s32[256]{0:T(256)S(1)}, s32[256]{0:T(256)}, u32[]{:S(2)}) copy-start(s32[256]{0:T(256)} %param.21) | copy-start | bytes 3076
  42.3 37.1 %copy-start.13 = (f32[256]{0:T(256)S(1)}, f32[256]{0:T(256)}, u32[]{:S(2)}) copy-start(f32[256]{0:T(256)} %param.32) | copy-start | bytes 3076
  42.4 37.1 %copy-start.14 = (f32[256]{0:T(256)S(1)}, f32[256]{0:T(256)}, u32[]{:S(2)}) copy-start(f32[256]{0:T(256)} %param.33) | copy-start | bytes 3076
  42.4 37.1 %copy-start.15 = (f32[256]{0:T(256)S(1)}, f32[256]{0:T(256)}, u32[]{:S(2)}) copy-start(f32[256]{0:T(256)} %param.37) | copy-start | bytes 3076
  42.4 9.7 %collective-permute-start.5 = (bf16[512,256]{1,0:T(8,128)(2,1)S(1)}, bf16[512,256]{1,0:T(8,128)(2,1)S(1)}, u32[]{:S(2)}, u32[]{:S(2)}) collective-permute-start(bf16[512,256]{1,0:T(8,128)(2,1)S(1)} %get-tuple-element.14), channel_id=1, source_target_pairs={{0,2},{2,4},{4,6},{6,8},{8,10},{10,12},{12,14},{14,16},{16,18},{18... | collective-permute-start | bytes 786440 | tf_op jit(solution)/shard_map/ppermute | solution.py:344
  45.7 9.2 %collective-permute-start.7 = (bf16[512,256]{1,0:T(8,128)(2,1)S(1)}, bf16[512,256]{1,0:T(8,128)(2,1)S(1)}, u32[]{:S(2)}, u32[]{:S(2)}) collective-permute-start(bf16[512,256]{1,0:T(8,128)(2,1)S(1)} %get-tuple-element.13), channel_id=1, source_target_pairs={{2,0},{4,2},{6,4},{8,6},{10,8},{12,10},{14,12},{16,14},{18,16},{20... | collective-permute-start | bytes 786440 | tf_op jit(solution)/shard_map/ppermute | solution.py:345
  47.0 32.4 %collective-permute-start.4 = (bf16[1024,256]{1,0:T(8,128)(2,1)S(1)}, bf16[1024,256]{1,0:T(8,128)(2,1)S(1)}, u32[]{:S(2)}, u32[]{:S(2)}) collective-permute-start(bf16[1024,256]{1,0:T(8,128)(2,1)S(1)} %get-tuple-element.7.own), channel_id=1, source_target_pairs={{0,1},{1,0},{2,3},{3,2},{4,5},{5,4},{6,7},{7,6},{8,9},{9,8},{10,11... | collective-permute-start | bytes 1572872 | tf_op jit(solution)/shard_map/ppermute | solution.py:323
  49.8 1.5 collective-permute-start.9
  49.9 29.5 %collective-permute-start.10 = (bf16[256,512]{1,0:T(8,128)(2,1)S(1)}, bf16[256,512]{1,0:T(8,128)(2,1)S(1)}, u32[]{:S(2)}, u32[]{:S(2)}) collective-permute-start(bf16[256,512]{1,0:T(8,128)(2,1)S(1)} %copy-done.3), channel_id=1, source_target_pairs={{0,1},{1,0},{2,3},{3,2},{4,5},{5,4},{6,7},{7,6},{8,9},{9,8},{10,11... | collective-permute-start | bytes 786440 | tf_op jit(solution)/shard_map/ppermute | solution.py:323
  52.0 27.4 %collective-permute-start.11 = (bf16[512,256]{1,0:T(8,128)(2,1)S(1)}, bf16[512,256]{1,0:T(8,128)(2,1)S(1)}, u32[]{:S(2)}, u32[]{:S(2)}) collective-permute-start(bf16[512,256]{1,0:T(8,128)(2,1)S(1)} %copy-done.4), channel_id=1, source_target_pairs={{0,1},{1,0},{2,3},{3,2},{4,5},{5,4},{6,7},{7,6},{8,9},{9,8},{10,11... | collective-permute-start | bytes 786440 | tf_op jit(solution)/shard_map/ppermute | solution.py:323
  52.1 27.3 %collective-permute-start.6 = (bf16[512,256]{1,0:T(8,128)(2,1)S(1)}, bf16[512,256]{1,0:T(8,128)(2,1)S(1)}, u32[]{:S(2)}, u32[]{:S(2)}) collective-permute-start(bf16[512,256]{1,0:T(8,128)(2,1)S(1)} %collective-permute-done.5.lo_own), channel_id=1, source_target_pairs={{0,1},{1,0},{2,3},{3,2},{4,5},{5,4},{6,7},{7,6},{8,9},{9,8},{10,11... | collective-permute-start | bytes 786440 | tf_op jit(solution)/shard_map/ppermute | solution.py:323
  54.9 24.5 %collective-permute-start.8 = (bf16[512,256]{1,0:T(8,128)(2,1)S(1)}, bf16[512,256]{1,0:T(8,128)(2,1)S(1)}, u32[]{:S(2)}, u32[]{:S(2)}) collective-permute-start(bf16[512,256]{1,0:T(8,128)(2,1)S(1)} %collective-permute-done.7.hi_own), channel_id=1, source_target_pairs={{0,1},{1,0},{2,3},{3,2},{4,5},{5,4},{6,7},{7,6},{8,9},{9,8},{10,11... | collective-permute-start | bytes 786440 | tf_op jit(solution)/shard_map/ppermute | solution.py:323
  79.5 0.9 copy-start.6
  80.4 1.0 copy-start.17
  154.5 5.5 %collective-permute-start.12 = (bf16[2048,256]{1,0:T(8,128)(2,1)S(1)}, bf16[2048,256]{1,0:T(8,128)(2,1)S(1)}, u32[]{:S(2)}, u32[]{:S(2)}) collective-permute-start(bf16[2048,256]{1,0:T(8,128)(2,1)S(1)} %bitcast.28), channel_id=1, source_target_pairs={{0,1},{1,0},{2,3},{3,2},{4,5},{5,4},{6,7},{7,6},{8,9},{9,8},{10,11... | collective-permute-start | bytes 3145736 | tf_op jit(solution)/shard_map/ppermute | solution.py:323
  (1 other events, 0.7 us)
Sparse Core Ops, SparseCore 0:
  10.3 67.9 all-gather.1

commit v2 on v1

--- a/solution.py
+++ b/solution.py
@@ -69,36 +69,27 @@
         name="conv")(sc, pts, low, high, nb, wm, wo, cbm, cbo, cpw, cpb, cpg, n1g)
 
 
-def attn_kernel(
-    sc, sel, plen, own, oth, lo_own, lo_oth, hi_own, hi_oth, sec, qkvm, qkvo, qbm, qbo, prw, prb,
-    n2g, f1m, f1o, b1m, b1o, f2m, f2o, f2b, send, NE, KT, V, Q8, ACC, OUT, M,
-):
-    g = sc[0]
-    base = sc[1]
-    total = sc[2]
+def spread(g, NE, count, first, a_ref, b_ref):
     mine = pl.multiple_of(32 * g, 32)
     theirs = pl.multiple_of(32 - 32 * g, 32)
 
-    def spread(count, first, a_ref, b_ref):
-        def step(c, _):
-            src = pl.multiple_of(32 * c, 32)
-            row = first + 64 * c
-            NE[pl.ds(pl.multiple_of(row + mine, 32), 32), :] = a_ref[pl.ds(src, 32), :]
-            NE[pl.ds(pl.multiple_of(row + theirs, 32), 32), :] = b_ref[pl.ds(src, 32), :]
-            return 0
-
-        lax.fori_loop(0, count, step, 0, unroll=4)
-
-    spread(16, 0, lo_own, lo_oth)
-    spread(32, 1024, own, oth)
-    spread(16, 3072, hi_own, hi_oth)
-
+    def step(c, _):
+        src = pl.multiple_of(32 * c, 32)
+        row = first + 64 * c
+        NE[pl.ds(pl.multiple_of(row + mine, 32), 32), :] = a_ref[pl.ds(src, 32), :]
+        NE[pl.ds(pl.multiple_of(row + theirs, 32), 32), :] = b_ref[pl.ds(src, 32), :]
+        return 0
+
+    lax.fori_loop(0, count, step, 0, unroll=4)
+
+
+def key_values(NE, KT, V, qkvm, qkvo, qbm, qbo):
     wkt = [jnp.transpose(w[:, 128:256]) for w in (qkvm, qkvo)]
     bkc = [jnp.transpose(jnp.broadcast_to(b[:, 128:256], (8, 128)))[:, :1] for b in (qbm, qbo)]
     wv = jnp.concatenate([qkvm[:, 256:384], qkvo[:, 256:384]], axis=1)
     bv = jnp.concatenate([qbm[:, 256:384], qbo[:, 256:384]], axis=1)
 
-    def key_value(i, most):
+    def block(i, most):
         r0 = pl.multiple_of(i * 256, 256)
         rows = NE[pl.ds(r0, 256), :]
         for h in range(2):
@@ -113,26 +104,157 @@
         V[pl.ds(r0, 256), :] = (jnp.dot(rows, wv, preferred_element_type=F32) + bv).astype(BF)
         return most
 
-    key_most = jnp.max(lax.fori_loop(0, 16, key_value, jnp.zeros((8, 256), F32)))
-
+    return block
+
+
+def patch_rows(plen):
     lens = jnp.broadcast_to(plen[...].astype(F32), (256, 256))
     sub = lax.broadcasted_iota(jnp.int32, (256, 256), 0)
     lane = lax.broadcasted_iota(jnp.int32, (256, 256), 1)
     ends_col = jnp.sum(jnp.where(lane <= sub, lens, 0.0), axis=1, keepdims=True)
     ends_row = jnp.sum(jnp.where(lane == sub, ends_col, 0.0), axis=0, keepdims=True)
-    starts_row = ends_row - plen[...].astype(F32)
-
+    return ends_row - plen[...].astype(F32), ends_row
+
+
+def limits(qb, g, base, total, starts_row, ends_row):
+    r = lax.broadcasted_iota(jnp.int32, (256, 1), 0)
+    row = (base + 512 * qb + 64 * (r // 32) + 32 * g + r % 32).astype(F32)
+    first = jnp.max(jnp.where(starts_row <= row, starts_row, 0.0), axis=1, keepdims=True)
+    finish = jnp.min(jnp.where(ends_row > row, ends_row, total.astype(F32)), axis=1, keepdims=True)
+    shift = (1024 - base).astype(F32)
+    first = (first + shift).astype(jnp.int32)
+    finish = (finish + shift).astype(jnp.int32)
+    kb0 = jnp.maximum(jnp.min(first) // 128, 0)
+    kb1 = jnp.minimum((jnp.max(finish) + 127) // 128, 32)
+    return first, finish, kb0, kb1
+
+
+def queries(rows, qkvm, qkvo, qbm, qbo):
     wq = jnp.concatenate([qkvm[:, 0:128], qkvo[:, 0:128]], axis=1)
     bq = jnp.concatenate([qbm[:, 0:128], qbo[:, 0:128]], axis=1)
+    return ((jnp.dot(rows, wq, preferred_element_type=F32) + bq) * Q_SCALE).astype(BF)
+
+
+def pair_tools():
+    half = lax.broadcasted_iota(jnp.int32, (32, 128), 0) < 16
+    k_low = jnp.where(half, 1.0, 0.0).astype(BF)
+    k_high = jnp.where(half, 0.0, 1.0).astype(BF)
+    col_head = lax.broadcasted_iota(jnp.int32, (128, 128), 1) // 16
+    cols = [jnp.where(col_head == a, 1.0, 0.0).astype(BF) for a in range(8)]
+
+    def mask(kb, first, finish):
+        key = kb * 128 + lax.broadcasted_iota(jnp.int32, (256, 128), 1)
+        madd = jnp.where((key >= first) & (key < finish), 0.0, -jnp.inf)
+        return jnp.concatenate([madd, madd], axis=1)
+
+    def scores(Q8, p, kt, madd):
+        part = kt[32 * p : 32 * p + 32, :]
+        pair = jnp.concatenate([part * k_low, part * k_high], axis=1)
+        return jnp.dot(Q8[p], pair, preferred_element_type=F32) + madd
+
+    def step(kb, k0, Q8, KT, V, first, finish, M=None):
+        kt = KT[:, pl.ds(k0, 128)]
+        vb = V[pl.ds(k0, 128), :]
+        madd = mask(kb, first, finish)
+        out = []
+        for h in range(2):
+            vh = vb[:, 128 * h : 128 * h + 128]
+            ps, vs = [], []
+            for a in range(4):
+                p = 4 * h + a
+                s = scores(Q8, p, kt, madd)
+                if M is not None:
+                    s = s - M[p]
+                ps.append(jnp.exp2(s).astype(BF))
+                for c in (cols[2 * a], cols[2 * a + 1]):
+                    vs.append(jnp.concatenate([vh * c, c], axis=1))
+            out.append(
+                jnp.dot(
+                    jnp.concatenate(ps, axis=1),
+                    jnp.concatenate(vs, axis=0),
+                    preferred_element_type=F32,
+                )
+            )
+        return out
+
+    return mask, scores, step
+
+
+def near_kernel(
+    sc, plen, own, oth, qkvm, qkvo, qbm, qbo, acc_o, q_o, most_o, NE, KT, V, Q8,
+):
+    g, base, total = sc[0], sc[1], sc[2]
+    spread(g, NE, 32, 0, own, oth)
+    block = key_values(NE, KT, V, qkvm, qkvo, qbm, qbo)
+    most = lax.fori_loop(0, 8, block, jnp.zeros((8, 256), F32))
+    most_o[...] = jnp.broadcast_to(jnp.max(most), (8, 128))
+    starts_row, ends_row = patch_rows(plen)
+    mask, scores, step = pair_tools()
+
+    def q_block(qb, _):
+        r0 = pl.multiple_of(qb * 256, 256)
+        q = queries(own[pl.ds(r0, 256), :], qkvm, qkvo, qbm, qbo)
+        q_o[pl.ds(r0, 256), :] = q
+        for p in range(8):
+            Q8[p] = q[:, 32 * p : 32 * p + 32]
+        first, finish, kb0, kb1 = limits(qb, g, base, total, starts_row, ends_row)
+        acc_o[qb] = jnp.zeros((2, 256, 256), F32)
+
+        def body(kb, _):
+            k0 = pl.multiple_of((kb - 8) * 128, 128)
+            for h, x in enumerate(step(kb, k0, Q8, KT, V, first, finish)):
+                acc_o[qb, h] += x
+            return 0
+
+        lax.fori_loop(jnp.maximum(kb0, 8), jnp.minimum(kb1, 24), body, 0)
+        return 0
+
+    lax.fori_loop(0, 4, q_block, 0)
+
+
+def near_call(*args):
+    smem, vmem = pl.BlockSpec(memory_space=pltpu.SMEM), pl.BlockSpec(memory_space=pltpu.VMEM)
+    return pl.pallas_call(
+        near_kernel,
+        out_shape=[
+            jax.ShapeDtypeStruct((4, 2, 256, 256), F32),
+            jax.ShapeDtypeStruct((1024, 256), BF),
+            jax.ShapeDtypeStruct((8, 128), F32),
+        ],
+        in_specs=[smem] + [vmem] * (len(args) - 1),
+        out_specs=[vmem] * 3,
+        scratch_shapes=[
+            pltpu.VMEM((2048, 256), BF),
+            pltpu.VMEM((256, 2048), BF),
+            pltpu.VMEM((2048, 256), BF),
+            pltpu.VMEM((8, 256, 32), BF),
+        ],
+        compiler_params=pltpu.CompilerParams(vmem_limit_bytes=32 * 2**20),
+        cost_estimate=pl.CostEstimate(
+            flops=20 * 10**9, bytes_accessed=8 * 10**6, transcendentals=10**7
+        ),
+        name="near",
+    )(*args)
+
+
+def far_kernel(
+    sc, sel, plen, own, oth, lo_own, lo_oth, hi_own, hi_oth, sec, acc_i, q_i, most_i, qkvm, qkvo,
+    qbm, qbo, prw, prb, n2g, f1m, f1o, b1m, b1o, f2m, f2o, f2b, send, NE, KT, V, Q8, ACC, OUT, M,
+):
+    g, base, total = sc[0], sc[1], sc[2]
+    spread(g, NE, 16, 0, lo_own, lo_oth)
+    spread(g, NE, 16, 3072, hi_own, hi_oth)
+    block = key_values(NE, KT, V, qkvm, qkvo, qbm, qbo)
+    starts_row, ends_row = patch_rows(plen)
+    edge_lo = limits(0, g, base, total, starts_row, ends_row)[2]
+    edge_hi = limits(3, g, base, total, starts_row, ends_row)[3]
+    most = lax.fori_loop(jnp.minimum(edge_lo // 2, 4), 4, block, jnp.zeros((8, 256), F32))
+    most = lax.fori_loop(12, jnp.maximum((edge_hi + 1) // 2, 12), block, most)
+    key_most = jnp.maximum(jnp.max(most), jnp.max(most_i[...]))
+    mask, scores, step = pair_tools()
     hs = lax.broadcasted_iota(jnp.int32, (256, 128), 0) // 16
     hl = lax.broadcasted_iota(jnp.int32, (256, 128), 1)
     head_sel = jnp.where(hs == hl, 1.0, 0.0).astype(BF)
-    k_low = jnp.where(
-        lax.broadcasted_iota(jnp.int32, (32, 128), 0) < 16, 1.0, 0.0
-    ).astype(BF)
-    k_high = (1.0 - k_low.astype(F32)).astype(BF)
-    col_head = lax.broadcasted_iota(jnp.int32, (128, 128), 1) // 16
-    cols = [jnp.where(col_head == a, 1.0, 0.0).astype(BF) for a in range(8)]
     prw_s = jnp.concatenate(
         [
             prw[pl.ds(pl.multiple_of(128 * g, 128), 128), :],
@@ -141,78 +263,49 @@
         axis=0,
     )
 
+    def q_most(r0):
+        q = q_i[pl.ds(r0, 256), :]
+        return jnp.max(jnp.dot(q * q, head_sel, preferred_element_type=F32))
+
+    bound = q_most(0)
+    for i in range(1, 4):
+        bound = jnp.maximum(bound, q_most(256 * i))
+    calm = bound * key_most * 1.05 <= 1e4
+
+    @pl.when(jnp.logical_not(calm))
+    def _():
+        spread(g, NE, 32, 1024, own, oth)
+        lax.fori_loop(4, 12, block, jnp.zeros((8, 256), F32))
+
     def q_block(qb, _):
         r0 = pl.multiple_of(qb * 256, 256)
-        q = (jnp.dot(own[pl.ds(r0, 256), :], wq, preferred_element_type=F32) + bq) * Q_SCALE
-        q = q.astype(BF)
+        q = q_i[pl.ds(r0, 256), :]
         for p in range(8):
             Q8[p] = q[:, 32 * p : 32 * p + 32]
-        q_most = jnp.max(jnp.dot(q * q, head_sel, preferred_element_type=F32))
-        calm = q_most * key_most * 1.05 <= 1e4
-        r = lax.broadcasted_iota(jnp.int32, (256, 1), 0)
-        row = (base + 512 * qb + 64 * (r // 32) + 32 * g + r % 32).astype(F32)
-        first = jnp.max(jnp.where(starts_row <= row, starts_row, 0.0), axis=1, keepdims=True)
-        finish = jnp.min(
-            jnp.where(ends_row > row, ends_row, total.astype(F32)), axis=1, keepdims=True
-        )
-        shift = (1024 - base).astype(F32)
-        first = (first + shift).astype(jnp.int32)
-        finish = (finish + shift).astype(jnp.int32)
-        kb0 = jnp.maximum(jnp.min(first) // 128, 0)
-        kb1 = jnp.minimum((jnp.max(finish) + 127) // 128, 32)
-
-        def scores(kb, p, kt, madd):
-            part = kt[32 * p : 32 * p + 32, :]
-            pair = jnp.concatenate([part * k_low, part * k_high], axis=1)
-            s = jnp.dot(Q8[p], pair, preferred_element_type=F32)
-            return s + madd
-
-        def mask(kb):
-            key = kb * 128 + lax.broadcasted_iota(jnp.int32, (256, 128), 1)
-            madd = jnp.where((key >= first) & (key < finish), 0.0, -jnp.inf)
-            return jnp.concatenate([madd, madd], axis=1)
-
-        def attend(use_max):
-            def step(kb, _):
-                k0 = pl.multiple_of(kb * 128, 128)
-                kt = KT[:, pl.ds(k0, 128)]
-                vb = V[pl.ds(k0, 128), :]
-                madd = mask(kb)
-                for h in range(2):
-                    vh = vb[:, 128 * h : 128 * h + 128]
-                    ps, vs = [], []
-                    for a in range(4):
-                        p = 4 * h + a
-                        s = scores(kb, p, kt, madd)
-                        if use_max:
-                            s = s - M[p]
-                        ps.append(jnp.exp2(s).astype(BF))
-                        for c in (cols[2 * a], cols[2 * a + 1]):
-                            vs.append(jnp.concatenate([vh * c, c], axis=1))
-                    ACC[h] += jnp.dot(
-                        jnp.concatenate(ps, axis=1),
-                        jnp.concatenate(vs, axis=0),
-                        preferred_element_type=F32,
-                    )
-                return 0
-
-            lax.fori_loop(kb0, kb1, step, 0)
-
-        ACC[...] = jnp.zeros_like(ACC)
+        first, finish, kb0, kb1 = limits(qb, g, base, total, starts_row, ends_row)
+
+        def body(kb, _, M=None):
+            k0 = pl.multiple_of(kb * 128, 128)
+            for h, x in enumerate(step(kb, k0, Q8, KT, V, first, finish, M)):
+                ACC[h] += x
+            return 0
 
         @pl.when(calm)
         def _():
-            attend(False)
+            ACC[...] = acc_i[qb]
+            lax.fori_loop(kb0, jnp.minimum(kb1, 8), body, 0)
+            lax.fori_loop(jnp.maximum(kb0, 24), kb1, body, 0)
 
         @pl.when(jnp.logical_not(calm))
         def _():
+            ACC[...] = jnp.zeros_like(ACC)
             M[...] = jnp.full(M.shape, -jnp.inf, F32)
 
             def top(kb, _):
                 kt = KT[:, pl.ds(pl.multiple_of(kb * 128, 128), 128)]
-                madd = mask(kb)
+                madd = mask(kb, first, finish)
                 for p in range(8):
-                    M[p] = jnp.maximum(M[p], scores(kb, p, kt, madd))
+                    M[p] = jnp.maximum(M[p], scores(Q8, p, kt, madd))
                 return 0
 
             lax.fori_loop(kb0, kb1, top, 0)
@@ -222,7 +315,7 @@
                     M[p, :, 128 * h : 128 * h + 128] = jnp.broadcast_to(
                         jnp.max(part, axis=1, keepdims=True), (256, 128)
                     )
-            attend(True)
+            lax.fori_loop(kb0, kb1, lambda kb, c: body(kb, c, M), 0)
 
         attn = jnp.concatenate(
             [ACC[h, :, 0:128] / ACC[h, :, 128:256] for h in range(2)], axis=1
@@ -253,10 +346,10 @@
     lax.fori_loop(0, 64, place, 0, unroll=4)
 
 
-def attn_call(*args):
+def far_call(*args):
     smem, vmem = pl.BlockSpec(memory_space=pltpu.SMEM), pl.BlockSpec(memory_space=pltpu.VMEM)
     return pl.pallas_call(
-        attn_kernel,
+        far_kernel,
         out_shape=jax.ShapeDtypeStruct((2048, 256), BF),
         in_specs=[smem] * 2 + [vmem] * (len(args) - 2),
         out_specs=vmem,
@@ -271,9 +364,9 @@
         ],
         compiler_params=pltpu.CompilerParams(vmem_limit_bytes=48 * 2**20),
         cost_estimate=pl.CostEstimate(
-            flops=60 * 10**9, bytes_accessed=8 * 10**6, transcendentals=2 * 10**7
+            flops=20 * 10**9, bytes_accessed=8 * 10**6, transcendentals=10**7
         ),
-        name="attention",
+        name="far",
     )(*args)
 
 
@@ -329,9 +422,11 @@
     small = jnp.concatenate([conv_b, qkv_b.reshape(384), fc1_b])
     small_o = swap(small)
     run = zorder[::64] // 64
-    table = lax.all_gather(
-        jnp.broadcast_to(jnp.pad(run, (0, 96))[None, :], (64, 128)), "pts", axis=0, tiled=True
-    ).reshape(peers, 64, 128)[:, 0, :32]
+    wanted = jnp.max(
+        jnp.where(run[None, :] // 32 == jnp.arange(peers, dtype=jnp.int32)[:, None], run[None, :] % 32, 0),
+        axis=1,
+    )
+    wanted = jnp.broadcast_to(wanted[:, None, None], (peers, 1, 128)).astype(jnp.int32)
     qkv_m = qkv_w.reshape(256, 384)
     qkv_o, fc1_o, fc2_o = swap(qkv_m), swap(fc1_w), swap(fc2_w)
 
@@ -341,15 +436,24 @@
         small_o[None, :128], cpe_w, cpe_b[None], cpe_gain[None], norm1_gain[None],
     )
     other = swap(normed)
+    wanted, other = lax.optimization_barrier((wanted, other))
+    sel = lax.all_to_all(wanted, "pts", split_axis=0, concat_axis=0, tiled=True)[:, 0, 0].astype(jnp.int32)
     lo_own = lax.ppermute(normed[512:], "pts", forward)
     hi_own = lax.ppermute(normed[:512], "pts", backward)
-    lo_oth, hi_oth = swap(lo_own), swap(hi_own)
-    sel = jnp.max(jnp.where(table // 32 == me, table % 32, 0), axis=1)
-    send = attn_call(
+    lo_oth = lax.ppermute(
+        normed[512:], ("pts", "grp"), [(2 * i + c, 2 * i + 3 - c) for i in range(peers - 1) for c in (0, 1)]
+    )
+    hi_oth = lax.ppermute(
+        normed[:512], ("pts", "grp"), [(2 * i + 2 + c, 2 * i + 1 - c) for i in range(peers - 1) for c in (0, 1)]
+    )
+    weights = (
+        qkv_m, qkv_o, small[None, 128:512], small_o[None, 128:512],
+    )
+    acc, query, most = near_call(scalars, patch_len[None], normed, other, *weights)
+    send = far_call(
         scalars, sel, patch_len[None], normed, other, lo_own, lo_oth, hi_own, hi_oth, section_one,
-        qkv_m, qkv_o, small[None, 128:512], small_o[None, 128:512], proj_w, proj_b[None],
-        norm2_gain[None], fc1_w, fc1_o, small[None, 512:], small_o[None, 512:], fc2_w, fc2_o,
-        fc2_b[None],
+        acc, query, most, *weights, proj_w, proj_b[None], norm2_gain[None], fc1_w, fc1_o,
+        small[None, 512:], small_o[None, 512:], fc2_w, fc2_o, fc2_b[None],
     )
     got = lax.all_to_all(send, "pts", split_axis=0, concat_axis=0, tiled=True)
     return last_call(scalars, run // 32, (zorder[:64] % 64)[:, None], got, swap(got))

time: 171 us -> 189 us (1.11); the launches traced: 170 us -> 186 us
  waiting for transfers between devices: 28.7 us -> 1.53 us
  Pallas kernels: 67.7 us -> 89.8 us
  starting transfers between devices: 19.2 us -> 37.3 us
  between operations: 13.8 us -> 0.38 us
  local copies, waits for them, and re-layouts: 8.78 us -> 18.9 us
  blocking collectives: 30.1 us -> 35.1 us
    pallas_call x1 -> x2, Pallas kernels: 42.9 us -> 65 us  [the longest x1 43.4 us: far_call(): pl.pallas_call(far_kernel, out_shape=jax.ShapeDtypeStruct((2048, 256), BF...]
    all_gather x1 -> x0, waiting for transfers between devices: 21.2 us -> none  [local(): lax.all_gather(jnp.broadcast_to(jnp.pad(run, (0, 96))[None, :], (64, 128)...]
    all_to_all x0 -> x1, starting transfers between devices: none -> 14.4 us  [local(): lax.all_to_all(wanted, 'pts', split_axis=0, concat_axis=0, tiled=True)]
    unnamed x41 -> x55, local copies, waits for them, and re-layouts: 5.1 us -> 12 us
    ppermute x0 -> x2, starting transfers between devices: none -> 5.06 us  [the longest x1 3.77 us: local(): lax.ppermute(normed[512:], ('pts', 'grp'), [(2 * i + c, 2 * i + 3 - c) fo...]
    all_to_all x1, blocking collectives: 30.1 us -> 35.1 us  [local(): got = lax.all_to_all(send, 'pts', split_axis=0, concat_axis=0, tiled=True)]
    ppermute x1, waiting for transfers between devices: 2.83 us -> 0.01 us  [local(): high = lax.ppermute(points[:256], 'pts', backward)]
    ppermute x9 -> x7, starting transfers between devices: 10.1 us -> 7.74 us  [swap(): return lax.ppermute(x, 'grp', [(0, 1), (1, 0)])]
  transfers between devices with their start and end apart: 14 -> 14, of which waited for: 5 -> 1; matrix products, arithmetic and copies ran while one was open for 5% -> 6% of each run, Pallas kernels for 13% -> 23%
where the time goes in v2:
time: 189 us; the launch traced here: 186 us
  Pallas kernels  89.8 us (48%)
  starting transfers between devices  37.3 us (20%)
  blocking collectives  35.1 us (19%)
  local copies, waits for them, and re-layouts  18.9 us (10%)
  other arithmetic  2.77 us (1%)
    pallas_call x1, Pallas kernels, far_call(): pl.pallas_call(far_kernel, out_shape=jax.ShapeDtypeStruct((2048, 256), BF...  43.4 us
    all_to_all x1, blocking collectives, local(): got = lax.all_to_all(send, 'pts', split_axis=0, concat_axis=0, tiled=True)  35.1 us
    pallas_call x1, Pallas kernels, conv_call(): pl.pallas_call(conv_kernel, out_shape=[jax.ShapeDtypeStruct((1024, 256),...  21.8 us
    pallas_call x1, Pallas kernels, near_call(): pl.pallas_call(near_kernel, out_shape=[jax.ShapeDtypeStruct((4, 2, 256, 2...  21.6 us
    all_to_all x1, starting transfers between devices, local(): lax.all_to_all(wanted, 'pts', split_axis=0, concat_axis=0, tiled=True)  14.4 us
    unnamed x55, local copies, waits for them, and re-layouts  12 us
    ppermute x7, starting transfers between devices, swap(): return lax.ppermute(x, 'grp', [(0, 1), (1, 0)])  7.74 us
    ppermute x1, starting transfers between devices, local(): lo_own = lax.ppermute(normed[512:], 'pts', forward)  4.27 us
  transfers between devices with their start and end apart: 14, of which 1 were waited for; matrix products, arithmetic and copies ran while one was open for 6% of the time, Pallas kernels for 23%

profile of v2, /device:TPU:1, one launch (start us, length us, event | category | flops | bytes accessed | tf_op | source)
XLA Modules:
  0.0 185.8 jit_solution(3372103444413717013)
XLA Ops:
  0.0 1.5 collective-permute-start.2
  1.5 1.3 pad_maximum_fusion
  2.9 1.0 fusion.2
  3.9 3.2 %collective-permute-start = (bf16[256,256]{1,0:T(8,128)(2,1)S(1)}, bf16[256,256]{1,0:T(8,128)(2,1)S(1)}, u32[]{:S(2)}, u32[]{:S(2)}) collective-permute-start(bf16[256,256]{1,0:T(8,128)(2,1)S(1)} %get-tuple-element.22), channel_id=1, source_target_pairs={{0,2},{2,4},{4,6},{6,8},{8,10},{10,12},{12,14},{14,16},{16,18},{18... | collective-permute-start | bytes 393224 | tf_op jit(solution)/shard_map/ppermute | solution.py:418
  7.2 1.3 collective-permute-start.1
  8.5 1.1 copy.42
  9.7 0.8 collective-permute-start.9
  10.4 0.8 slice.32
  11.9 1.3 copy.41.nb
  15.9 0.9 copy-done.5
  16.8 0.9 copy-done.8
  17.7 0.9 copy-done.10
  19.3 21.8 %conv.1 = (bf16[1024,256]{1,0:T(8,128)(2,1)S(1)}, bf16[1024,256]{1,0:T(8,128)(2,1)S(1)}) custom-call(s32[3]{0:T(128)S(1)} %pad_add_fusion.sc, bf16[2048,256]{1,0:T(8,128)(2,1)S(1)} %copy-done, bf16[256,256]{1,0:T(8,128)(2,1)S(1)} %copy-done.8, bf16[256,256]{1,0:T(8,128)(2,1)S(1)} %copy-done.10, s32[2048,27]{1,0:T(8,128)S(1)} %copy.41.nb, ...), custom_call_target="tpu_custom_call" | custom-call | flops 30000001024 | bytes 8000000 | tf_op jit(solution)/shard_map/conv/pallas_call | solution.py:63
  42.7 0.8 fusion.3
  43.5 4.3 %collective-permute-start.5 = (bf16[512,256]{1,0:T(8,128)(2,1)}, bf16[512,256]{1,0:T(8,128)(2,1)S(1)}, u32[]{:S(2)}, u32[]{:S(2)}) collective-permute-start(bf16[512,256]{1,0:T(8,128)(2,1)} %get-tuple-element.24), channel_id=1, source_target_pairs={{0,2},{2,4},{4,6},{6,8},{8,10},{10,12},{12,14},{14,16},{16,18},{18... | collective-permute-start | bytes 786440 | tf_op jit(solution)/shard_map/ppermute | solution.py:441
  47.8 3.8 %collective-permute-start.6 = (bf16[512,256]{1,0:T(8,128)(2,1)}, bf16[512,256]{1,0:T(8,128)(2,1)S(1)}, u32[]{:S(2)}, u32[]{:S(2)}) collective-permute-start(bf16[512,256]{1,0:T(8,128)(2,1)} %get-tuple-element.24), channel_id=1, source_target_pairs={{0,3},{1,2},{2,5},{3,4},{4,7},{5,6},{6,9},{7,8},{8,11},{9,10},{10,... | collective-permute-start | bytes 786440 | tf_op jit(solution)/shard_map/ppermute | solution.py:443
  51.6 0.7 broadcast_in_dim.64
  52.3 14.4 %all-to-all-start = ((s32[64,1,128]{2,1,0:T(1,128)}), s32[64,1,128]{2,1,0:T(1,128)S(1)}, u32[]{:S(2)}, u32[]{:S(2)}) async-start(s32[64,1,128]{2,1,0:T(1,128)} %broadcast_in_dim.64), calls=%async_computation | async-start | bytes 65536 | tf_op jit(solution)/shard_map/all_to_all | solution.py:440
  66.8 1.3 collective-permute-start.7
  68.1 1.3 collective-permute-start.8
  70.1 21.6 %near.1 = (f32[4,2,256,256]{3,2,1,0:T(8,128)S(1)}, bf16[1024,256]{1,0:T(8,128)(2,1)S(1)}, f32[8,128]{1,0:T(8,128)S(1)}) custom-call(s32[3]{0:T(128)S(1)} %pad_add_fusion.sc, s32[1,256]{1,0:T(1,128)S(1)} %bitcast.37, bf16[1024,256]{1,0:T(8,128)(2,1)S(1)} %get-tuple-element.12.own, bf16[1024,256]{1,0:T(8,128)(2,1)S(1)} %collective-permute-done.4.oth, ...), custom_call_target="tpu_custom_call" | custom-call | flops 20000000000 | bytes 8000000 | tf_op jit(solution)/shard_map/near/pallas_call | solution.py:217
  91.7 1.3 copy-done.18
  93.1 0.8 copy-done.21
  93.9 1.3 slice_reduce_fusion.sel
  95.2 1.0 copy-done.20
  96.3 1.0 copy-done.22
  97.3 43.4 %far.1 = bf16[2048,256]{1,0:T(8,128)(2,1)S(1)} custom-call(s32[3]{0:T(128)S(1)} %pad_add_fusion.sc, s32[64]{0:T(128)S(1)} %slice_reduce_fusion.sel, s32[1,256]{1,0:T(1,128)S(1)} %bitcast.38, bf16[1024,256]{1,0:T(8,128)(2,1)S(1)} %get-tuple-element.12.own, bf16[1024,256]{1,0:T(8,128)(2,1)S(1)} %collective-permute-done.4.oth, ...), custom_call_target="tpu_custom_call" | custom-call | flops 20000000000 | bytes 8000000 | tf_op jit(solution)/shard_map/far/pallas_call | solution.py:351
  140.8 35.1 %all_to_all.16 = bf16[64,32,256]{2,1,0:T(8,128)(2,1)S(1)} all-to-all(bf16[64,32,256]{2,1,0:T(8,128)(2,1)S(1)} %bitcast.28), channel_id=1, replica_groups=mesh['pts'=64,'grp'=2] {'pts'}, dimensions={0} | all-to-all | bytes 2097152 | tf_op jit(solution)/shard_map/all_to_all | solution.py:458
  175.8 4.7 %collective-permute-start.12 = (bf16[2048,256]{1,0:T(8,128)(2,1)S(1)}, bf16[2048,256]{1,0:T(8,128)(2,1)S(1)}, u32[]{:S(2)}, u32[]{:S(2)}) collective-permute-start(bf16[2048,256]{1,0:T(8,128)(2,1)S(1)} %bitcast.26), channel_id=1, source_target_pairs={{0,1},{1,0},{2,3},{3,2},{4,5},{5,4},{6,7},{7,6},{8,9},{9,8},{10,11... | collective-permute-start | bytes 3145736 | tf_op jit(solution)/shard_map/ppermute | solution.py:416
  180.5 0.7 fusion
  181.3 1.5 collective-permute-done.12.oth
  182.8 3.0 %relabel.1 = bf16[2048,256]{1,0:T(8,128)(2,1)} custom-call(s32[3]{0:T(128)S(1)} %pad_add_fusion.sc, s32[32]{0:T(128)S(1)} %and_select_fusion.2.src, s32[64,1]{1,0:T(8,128)S(1)} %copy.46.inner, bf16[2048,256]{1,0:T(8,128)(2,1)S(1)} %bitcast.27, bf16[2048,256]{1,0:T(8,128)(2,1)S(1)} %collective-permute-done.12.oth), custom_call_target="tpu_custom_call" | custom-call | tf_op jit(solution)/shard_map/relabel/pallas_call | solution.py:394
  (73 shorter events, 6.7 us)
Async XLA Ops:
  0.0 15.8 %copy-start.2 = (f32[128]{0:T(128)S(1)}, f32[128]{0:T(128)}, u32[]{:S(2)}) copy-start(f32[128]{0:T(128)} %param.24) | copy-start | bytes 1540
  0.0 15.8 %copy-start = (bf16[2048,256]{1,0:T(8,128)(2,1)S(1)}, bf16[2048,256]{1,0:T(8,128)(2,1)}, u32[]{:S(2)}) copy-start(bf16[2048,256]{1,0:T(8,128)(2,1)} %pts.1) | copy-start | bytes 3145732
  0.0 13.2 %copy-start.3 = (bf16[256,512]{1,0:T(8,128)(2,1)S(1)}, bf16[256,512]{1,0:T(8,128)(2,1)}, u32[]{:S(2)}) copy-start(bf16[256,512]{1,0:T(8,128)(2,1)} %f1m.1) | copy-start | bytes 786436
  0.0 14.7 %copy-start.4 = (bf16[512,256]{1,0:T(8,128)(2,1)S(1)}, bf16[512,256]{1,0:T(8,128)(2,1)}, u32[]{:S(2)}) copy-start(bf16[512,256]{1,0:T(8,128)(2,1)} %f2m.1) | copy-start | bytes 786436
  0.0 15.8 %copy-start.11 = (f32[256]{0:T(256)S(1)}, f32[256]{0:T(256)}, u32[]{:S(2)}) copy-start(f32[256]{0:T(256)} %param.26) | copy-start | bytes 3076
  0.0 15.8 %copy-start.12 = (f32[256]{0:T(256)S(1)}, f32[256]{0:T(256)}, u32[]{:S(2)}) copy-start(f32[256]{0:T(256)} %param.27) | copy-start | bytes 3076
  0.0 15.8 %collective-permute-start.2 = (bf16[6912,128]{1,0:T(8,128)(2,1)}, bf16[6912,128]{1,0:T(8,128)(2,1)}, u32[]{:S(2)}, u32[]{:S(2)}) collective-permute-start(bf16[6912,128]{1,0:T(8,128)(2,1)} %bitcast.45), channel_id=1, source_target_pairs={{0,1},{1,0},{2,3},{3,2},{4,5},{5,4},{6,7},{7,6},{8,9},{9,8},{10,11... | collective-permute-start | bytes 5308424 | tf_op jit(solution)/shard_map/ppermute | solution.py:416
  2.8 10.4 %collective-permute-start.3 = (f32[1024]{0:T(1024)}, f32[1024]{0:T(1024)}, u32[]{:S(2)}, u32[]{:S(2)}) collective-permute-start(f32[1024]{0:T(1024)} %pad_maximum_fusion), channel_id=1, source_target_pairs={{0,1},{1,0},{2,3},{3,2},{4,5},{5,4},{6,7},{7,6},{8,9},{9,8},{10,11... | collective-permute-start | bytes 12296 | tf_op jit(solution)/shard_map/ppermute | solution.py:416
  3.9 10.1 %collective-permute-start = (bf16[256,256]{1,0:T(8,128)(2,1)S(1)}, bf16[256,256]{1,0:T(8,128)(2,1)S(1)}, u32[]{:S(2)}, u32[]{:S(2)}) collective-permute-start(bf16[256,256]{1,0:T(8,128)(2,1)S(1)} %get-tuple-element.22), channel_id=1, source_target_pairs={{0,2},{2,4},{4,6},{6,8},{8,10},{10,12},{12,14},{14,16},{16,18},{18... | collective-permute-start | bytes 393224 | tf_op jit(solution)/shard_map/ppermute | solution.py:418
  7.2 8.0 %collective-permute-start.1 = (bf16[256,256]{1,0:T(8,128)(2,1)S(1)}, bf16[256,256]{1,0:T(8,128)(2,1)S(1)}, u32[]{:S(2)}, u32[]{:S(2)}) collective-permute-start(bf16[256,256]{1,0:T(8,128)(2,1)S(1)} %get-tuple-element.21), channel_id=1, source_target_pairs={{2,0},{4,2},{6,4},{8,6},{10,8},{12,10},{14,12},{16,14},{18,16},{20... | collective-permute-start | bytes 393224 | tf_op jit(solution)/shard_map/ppermute | solution.py:419
  9.7 57.1 %collective-permute-start.9 = (bf16[256,384]{1,0:T(8,128)(2,1)S(1)}, bf16[256,384]{1,0:T(8,128)(2,1)S(1)}, u32[]{:S(2)}, u32[]{:S(2)}) collective-permute-start(bf16[256,384]{1,0:T(8,128)(2,1)S(1)} %copy.44.qkvm), channel_id=1, source_target_pairs={{0,1},{1,0},{2,3},{3,2},{4,5},{5,4},{6,7},{7,6},{8,9},{9,8},{10,11... | collective-permute-start | bytes 589832 | tf_op jit(solution)/shard_map/ppermute | solution.py:416
  13.3 54.8 %collective-permute-start.10 = (bf16[256,512]{1,0:T(8,128)(2,1)S(1)}, bf16[256,512]{1,0:T(8,128)(2,1)}, u32[]{:S(2)}, u32[]{:S(2)}) collective-permute-start(bf16[256,512]{1,0:T(8,128)(2,1)S(1)} %copy-done.3), channel_id=1, source_target_pairs={{0,1},{1,0},{2,3},{3,2},{4,5},{5,4},{6,7},{7,6},{8,9},{9,8},{10,11... | collective-permute-start | bytes 786440 | tf_op jit(solution)/shard_map/ppermute | solution.py:416
  14.7 80.4 %collective-permute-start.11 = (bf16[512,256]{1,0:T(8,128)(2,1)S(1)}, bf16[512,256]{1,0:T(8,128)(2,1)}, u32[]{:S(2)}, u32[]{:S(2)}) collective-permute-start(bf16[512,256]{1,0:T(8,128)(2,1)S(1)} %copy-done.4), channel_id=1, source_target_pairs={{0,1},{1,0},{2,3},{3,2},{4,5},{5,4},{6,7},{7,6},{8,9},{9,8},{10,11... | collective-permute-start | bytes 786440 | tf_op jit(solution)/shard_map/ppermute | solution.py:416
  19.3 21.9 %copy-start.25 = (s32[32]{0:T(128)S(1)}, s32[32]{0:T(128)}, u32[]{:S(2)}) copy-start(s32[32]{0:T(128)} %get-tuple-element.20) | copy-start | bytes 388
  19.3 21.9 %copy-start.24 = (s32[32]{0:T(128)S(1)}, s32[32]{0:T(128)}, u32[]{:S(2)}) copy-start(s32[32]{0:T(128)} %get-tuple-element.19) | copy-start | bytes 388
  19.3 22.0 %copy-start.23 = (f32[3,128]{1,0:T(4,128)S(1)}, f32[3,128]{1,0:T(4,128)}, u32[]{:S(2)}) copy-start(f32[3,128]{1,0:T(4,128)} %param.30) | copy-start | bytes 4612
  41.1 6.7 %copy-start.19 = (bf16[1024,256]{1,0:T(8,128)(2,1)}, bf16[1024,256]{1,0:T(8,128)(2,1)S(1)}, u32[]{:S(2)}) copy-start(bf16[1024,256]{1,0:T(8,128)(2,1)S(1)} %get-tuple-element.15.sec) | copy-start | bytes 1572868
  41.1 6.7 %collective-permute-start.4 = (bf16[1024,256]{1,0:T(8,128)(2,1)S(1)}, bf16[1024,256]{1,0:T(8,128)(2,1)S(1)}, u32[]{:S(2)}, u32[]{:S(2)}) collective-permute-start(bf16[1024,256]{1,0:T(8,128)(2,1)S(1)} %get-tuple-element.12.own), channel_id=1, source_target_pairs={{0,1},{1,0},{2,3},{3,2},{4,5},{5,4},{6,7},{7,6},{8,9},{9,8},{10,11... | collective-permute-start | bytes 1572872 | tf_op jit(solution)/shard_map/ppermute | solution.py:416
  43.5 51.6 %collective-permute-start.5 = (bf16[512,256]{1,0:T(8,128)(2,1)}, bf16[512,256]{1,0:T(8,128)(2,1)S(1)}, u32[]{:S(2)}, u32[]{:S(2)}) collective-permute-start(bf16[512,256]{1,0:T(8,128)(2,1)} %get-tuple-element.24), channel_id=1, source_target_pairs={{0,2},{2,4},{4,6},{6,8},{8,10},{10,12},{12,14},{14,16},{16,18},{18... | collective-permute-start | bytes 786440 | tf_op jit(solution)/shard_map/ppermute | solution.py:441
  47.8 47.3 %collective-permute-start.6 = (bf16[512,256]{1,0:T(8,128)(2,1)}, bf16[512,256]{1,0:T(8,128)(2,1)S(1)}, u32[]{:S(2)}, u32[]{:S(2)}) collective-permute-start(bf16[512,256]{1,0:T(8,128)(2,1)} %get-tuple-element.24), channel_id=1, source_target_pairs={{0,3},{1,2},{2,5},{3,4},{4,7},{5,6},{6,9},{7,8},{8,11},{9,10},{10,... | collective-permute-start | bytes 786440 | tf_op jit(solution)/shard_map/ppermute | solution.py:443
  52.3 41.5 %all-to-all-start = ((s32[64,1,128]{2,1,0:T(1,128)}), s32[64,1,128]{2,1,0:T(1,128)S(1)}, u32[]{:S(2)}, u32[]{:S(2)}) async-start(s32[64,1,128]{2,1,0:T(1,128)} %broadcast_in_dim.64), calls=%async_computation | async-start | bytes 65536 | tf_op jit(solution)/shard_map/all_to_all | solution.py:440
  66.8 28.4 %collective-permute-start.7 = (bf16[512,256]{1,0:T(8,128)(2,1)}, bf16[512,256]{1,0:T(8,128)(2,1)S(1)}, u32[]{:S(2)}, u32[]{:S(2)}) collective-permute-start(bf16[512,256]{1,0:T(8,128)(2,1)} %get-tuple-element.23), channel_id=1, source_target_pairs={{2,0},{4,2},{6,4},{8,6},{10,8},{12,10},{14,12},{16,14},{18,16},{20... | collective-permute-start | bytes 786440 | tf_op jit(solution)/shard_map/ppermute | solution.py:442
  68.1 27.1 %collective-permute-start.8 = (bf16[512,256]{1,0:T(8,128)(2,1)}, bf16[512,256]{1,0:T(8,128)(2,1)S(1)}, u32[]{:S(2)}, u32[]{:S(2)}) collective-permute-start(bf16[512,256]{1,0:T(8,128)(2,1)} %get-tuple-element.23), channel_id=1, source_target_pairs={{2,1},{3,0},{4,3},{5,2},{6,5},{7,4},{8,7},{9,6},{10,9},{11,8},{12,... | collective-permute-start | bytes 786440 | tf_op jit(solution)/shard_map/ppermute | solution.py:446
  70.1 25.1 %copy-start.1 = (f32[512]{0:T(512)S(1)}, f32[512]{0:T(512)}, u32[]{:S(2)}) copy-start(f32[512]{0:T(512)} %param.35) | copy-start | bytes 6148
  70.1 25.1 %copy-start.6 = (bf16[256,256]{1,0:T(8,128)(2,1)S(1)}, bf16[256,256]{1,0:T(8,128)(2,1)}, u32[]{:S(2)}) copy-start(bf16[256,256]{1,0:T(8,128)(2,1)} %prw.1) | copy-start | bytes 393220
  70.1 25.1 %copy-start.15 = (f32[256]{0:T(256)S(1)}, f32[256]{0:T(256)}, u32[]{:S(2)}) copy-start(f32[256]{0:T(256)} %param.32) | copy-start | bytes 3076
  70.1 25.1 %copy-start.16 = (f32[256]{0:T(256)S(1)}, f32[256]{0:T(256)}, u32[]{:S(2)}) copy-start(f32[256]{0:T(256)} %param.33) | copy-start | bytes 3076
  70.1 25.1 %copy-start.17 = (f32[256]{0:T(256)S(1)}, f32[256]{0:T(256)}, u32[]{:S(2)}) copy-start(f32[256]{0:T(256)} %param.37) | copy-start | bytes 3076
  91.7 1.4 copy-start.18
  95.2 1.0 copy-start.20
  96.3 1.0 copy-start.22
  175.8 7.0 %collective-permute-start.12 = (bf16[2048,256]{1,0:T(8,128)(2,1)S(1)}, bf16[2048,256]{1,0:T(8,128)(2,1)S(1)}, u32[]{:S(2)}, u32[]{:S(2)}) collective-permute-start(bf16[2048,256]{1,0:T(8,128)(2,1)S(1)} %bitcast.26), channel_id=1, source_target_pairs={{0,1},{1,0},{2,3},{3,2},{4,5},{5,4},{6,7},{7,6},{8,9},{9,8},{10,11... | collective-permute-start | bytes 3145736 | tf_op jit(solution)/shard_map/ppermute | solution.py:416
  (8 other events, 6.2 us)

commit v3 on v2

v3 whole, which is shorter than its diff:
```python
import jax
import jax.numpy as jnp
from jax import lax
from jax.experimental import pallas as pl
from jax.experimental.pallas import tpu as pltpu
from jax.sharding import PartitionSpec as P

F32=jnp.float32; BF=jnp.bfloat16

Q_SCALE = 0.25 * 1.4426950408889634


def layer_norm(v, gain):
    c = v - jnp.mean(v, axis=-1, keepdims=True)
    s = jnp.mean(c * c, axis=-1, keepdims=True)
    return c * lax.rsqrt(s + 1e-05) * gain

RB = 128


def copies(sems, pairs):
    out = [pltpu.make_async_copy(src, dst, sems.at[i]) for i, (src, dst) in enumerate(pairs)]
    for copy in out:
        copy.start()
    return out


def wait(some):
    for copy in some:
        copy.wait()


def turned(ref, g):
    first = ref.at[pl.ds(pl.multiple_of(128 * g, 128), 128)]
    return first, ref.at[pl.ds(pl.multiple_of(128 - 128 * g, 128), 128)]


def conv_kernel(
    sc, pts, low, high, nbs, wm, wo, cbm, cbo, cpw, cpb, cpg, n1g, sec_o, nrm_o, lo_o, hi_o,
    X, NT, NB, OH, G, W, CW, CB, CV, sems,
):
    g = sc[0]
    base = sc[1]
    cw_a, cw_b = turned(cpw, g)
    started = copies(
        sems,
        [
            (nbs, NT), (pts, X.at[256:2304]), (low, X.at[0:256]), (high, X.at[2304:2560]),
            (wm, W.at[:, 0:128]), (wo, W.at[:, 128:256]), (cw_a, CW.at[0:128]),
            (cw_b, CW.at[128:256]), (cbm, CB.at[:, 0:128]), (cbo, CB.at[:, 128:256]),
            (cpb, CV.at[0]), (cpg, CV.at[1]), (n1g, CV.at[2]),
        ],
    )
    wait(started[:4])
    lanes = lax.broadcasted_iota(jnp.int32, (RB, 768), 1)
    for b in range(8):
        NB[256 * b : 256 * b + 256, :] = jnp.transpose(NT[:, 256 * b : 256 * b + 256])

    def block(b, _):
        rel = []
        for j in range(RB // 32):
            rel.append(NB[pl.ds(pl.multiple_of(256 * b + 64 * j + 32 * g, 32), 32), :])
        rel = jnp.concatenate(rel, axis=0)
        rel = jnp.where(rel < 0, -1, rel - (base + 256 * b - 256))
        for t in range(27):
            col = rel[:, t : t + 1]
            OH[t * RB : (t + 1) * RB, :] = jnp.where(
                lanes == col, jnp.array(1, BF), jnp.array(0, BF)
            )
        win = X[pl.ds(pl.multiple_of(256 * b, 256), 768), :]
        for q in range(3):
            out = jnp.dot(
                OH[q * 9 * RB : (q + 1) * 9 * RB, :], win, preferred_element_type=F32
            ).astype(BF)
            for t in range(9):
                G[
                    pl.ds(pl.multiple_of(b * RB, RB), RB),
                    (q * 9 + t) * 256 : (q * 9 + t + 1) * 256,
                ] = out[t * RB : (t + 1) * RB, :]
        return 0

    lax.fori_loop(0, 1024 // RB, block, 0)
    wait(started[4:])

    def finish(m, _):
        r0 = pl.multiple_of(m * 256, 256)
        acc = jnp.dot(G[pl.ds(r0, 256), :], W[...], preferred_element_type=F32)
        conv = (acc + CB[...]).astype(BF)
        c = jnp.dot(conv, CW[...], preferred_element_type=F32) + CV[0]
        own = []
        for j in range(8):
            own.append(X[pl.ds(pl.multiple_of(256 + 512 * m + 64 * j + 32 * g, 32), 32), :])
        own = jnp.concatenate(own, axis=0).astype(F32)
        sec = (own + layer_norm(c, CV[1])).astype(BF)
        sec_o[pl.ds(r0, 256), :] = sec
        normed = layer_norm(sec.astype(F32), CV[2]).astype(BF)
        nrm_o[pl.ds(r0, 256), :] = normed

        @pl.when(m < 2)
        def _():
            hi_o[pl.ds(r0, 256), :] = normed

        @pl.when(m >= 2)
        def _():
            lo_o[pl.ds(r0 - 512, 256), :] = normed

        return 0

    lax.fori_loop(0, 4, finish, 0)


def call(kernel, name, smem, args, out_shape, scratch, sems, mib, flops):
    return pl.pallas_call(
        kernel,
        out_shape=out_shape,
        in_specs=[pl.BlockSpec(memory_space=pltpu.SMEM)] * smem
        + [pl.BlockSpec(memory_space=pl.ANY)] * (len(args) - smem),
        out_specs=[pl.BlockSpec(memory_space=pltpu.VMEM)] * len(out_shape),
        scratch_shapes=[pltpu.VMEM(*x) for x in scratch] + [pltpu.SemaphoreType.DMA((sems,))],
        compiler_params=pltpu.CompilerParams(vmem_limit_bytes=mib * 2**20),
        cost_estimate=pl.CostEstimate(flops=flops, bytes_accessed=8 * 10**6, transcendentals=10**7),
        name=name,
    )(*args)


def conv_call(*args):
    out = [jax.ShapeDtypeStruct((n, 256), BF) for n in (1024, 1024, 512, 512)]
    scratch = [
        ((2560, 256), BF), ((27, 2048), jnp.int32), ((2048, 27), jnp.int32), ((27 * RB, 768), BF), ((1024, 6912), BF),
        ((6912, 256), BF), ((256, 256), BF), ((1, 256), F32), ((3, 1, 256), F32),
    ]
    return call(conv_kernel, "conv", 1, args, out, scratch, 13, 50, 30 * 10**9)


def key_values(NE, KT, V, QW, QB):
    wkt = [jnp.transpose(QW[h, 1]) for h in range(2)]
    bkc = [jnp.transpose(jnp.broadcast_to(QB[h, 1:2, :], (8, 128)))[:, :1] for h in range(2)]
    wv = jnp.concatenate([QW[0, 2], QW[1, 2]], axis=1)
    bv = jnp.concatenate([QB[0, 2:3, :], QB[1, 2:3, :]], axis=1)

    def block(i, most):
        r0 = pl.multiple_of(i * 256, 256)
        rows = NE[pl.ds(4 * i, 4)].reshape(256, 256)
        for h in range(2):
            kt = (
                lax.dot_general(
                    wkt[h], rows, (((1,), (1,)), ((), ())), preferred_element_type=F32
                )
                + bkc[h]
            )
            most = jnp.maximum(most, jnp.sum((kt * kt).reshape(8, 16, 256), axis=1))
            KT[128 * h : 128 * h + 128, pl.ds(r0, 256)] = kt.astype(BF)
        V[pl.ds(r0, 256), :] = (jnp.dot(rows, wv, preferred_element_type=F32) + bv).astype(BF)
        return most

    return block


def patch_rows(plen):
    lens = jnp.broadcast_to(plen.astype(F32), (256, 256))
    sub = lax.broadcasted_iota(jnp.int32, (256, 256), 0)
    lane = lax.broadcasted_iota(jnp.int32, (256, 256), 1)
    ends_col = jnp.sum(jnp.where(lane <= sub, lens, 0.0), axis=1, keepdims=True)
    ends_row = jnp.sum(jnp.where(lane == sub, ends_col, 0.0), axis=0, keepdims=True)
    return ends_row - plen.astype(F32), ends_row


def limits(qb, g, base, total, starts_row, ends_row):
    r = lax.broadcasted_iota(jnp.int32, (256, 1), 0)
    row = (base + 512 * qb + 64 * (r // 32) + 32 * g + r % 32).astype(F32)
    first = jnp.max(jnp.where(starts_row <= row, starts_row, 0.0), axis=1, keepdims=True)
    finish = jnp.min(jnp.where(ends_row > row, ends_row, total.astype(F32)), axis=1, keepdims=True)
    shift = (1024 - base).astype(F32)
    first = (first + shift).astype(jnp.int32)
    finish = (finish + shift).astype(jnp.int32)
    kb0 = jnp.maximum(jnp.min(first) // 128, 0)
    kb1 = jnp.minimum((jnp.max(finish) + 127) // 128, 32)
    return first, finish, kb0, kb1


def queries(rows, QW, QB):
    wq = jnp.concatenate([QW[0, 0], QW[1, 0]], axis=1)
    bq = jnp.concatenate([QB[0, 0:1, :], QB[1, 0:1, :]], axis=1)
    return ((jnp.dot(rows, wq, preferred_element_type=F32) + bq) * Q_SCALE).astype(BF)


def pair_tools():
    half = lax.broadcasted_iota(jnp.int32, (32, 128), 0) < 16
    k_low = jnp.where(half, 1.0, 0.0).astype(BF)
    k_high = jnp.where(half, 0.0, 1.0).astype(BF)
    col_head = lax.broadcasted_iota(jnp.int32, (128, 128), 1) // 16
    cols = [jnp.where(col_head == a, 1.0, 0.0).astype(BF) for a in range(8)]

    def mask(kb, first, finish):
        key = kb * 128 + lax.broadcasted_iota(jnp.int32, (256, 128), 1)
        madd = jnp.where((key >= first) & (key < finish), 0.0, -jnp.inf)
        return jnp.concatenate([madd, madd], axis=1)

    def scores(Q8, p, kt, madd):
        part = kt[32 * p : 32 * p + 32, :]
        pair = jnp.concatenate([part * k_low, part * k_high], axis=1)
        return jnp.dot(Q8[p], pair, preferred_element_type=F32) + madd

    def step(kb, k0, Q8, KT, V, first, finish, M=None):
        kt = KT[:, pl.ds(k0, 128)]
        vb = V[pl.ds(k0, 128), :]
        madd = mask(kb, first, finish)
        out = []
        for h in range(2):
            vh = vb[:, 128 * h : 128 * h + 128]
            ps, vs = [], []
            for a in range(4):
                p = 4 * h + a
                s = scores(Q8, p, kt, madd)
                if M is not None:
                    s = s - M[p]
                ps.append(jnp.exp2(s).astype(BF))
                for c in (cols[2 * a], cols[2 * a + 1]):
                    vs.append(jnp.concatenate([vh * c, c], axis=1))
            out.append(
                jnp.dot(
                    jnp.concatenate(ps, axis=1),
                    jnp.concatenate(vs, axis=0),
                    preferred_element_type=F32,
                )
            )
        return out

    return mask, scores, step


def near_kernel(
    sc, plen, own, oth, qkvm, qkvo, qbm, qbo, acc_o, q_o, most_o, NE, KT, V, Q8, QW, QB, PL, sems,
):
    g, base, total = sc[0], sc[1], sc[2]
    wait(
        copies(
            sems,
            [
                (own, NE.at[:, g]), (oth, NE.at[:, 1 - g]), (qkvm, QW.at[0]), (qkvo, QW.at[1]),
                (qbm, QB.at[0]), (qbo, QB.at[1]), (plen, PL),
            ],
        )
    )
    block = key_values(NE, KT, V, QW, QB)
    most = lax.fori_loop(0, 8, block, jnp.zeros((8, 256), F32))
    most_o[...] = jnp.broadcast_to(jnp.max(most), (8, 128))
    starts_row, ends_row = patch_rows(PL[...])
    mask, scores, step = pair_tools()

    def q_block(qb, _):
        r0 = pl.multiple_of(qb * 256, 256)
        q = queries(NE[pl.ds(8 * qb, 8), g].reshape(256, 256), QW, QB)
        q_o[pl.ds(r0, 256), :] = q
        for p in range(8):
            Q8[p] = q[:, 32 * p : 32 * p + 32]
        first, finish, kb0, kb1 = limits(qb, g, base, total, starts_row, ends_row)
        acc_o[qb] = jnp.zeros((2, 256, 256), F32)

        def body(kb, _):
            k0 = pl.multiple_of((kb - 8) * 128, 128)
            for h, x in enumerate(step(kb, k0, Q8, KT, V, first, finish)):
                acc_o[qb, h] += x
            return 0

        lax.fori_loop(jnp.maximum(kb0, 8), jnp.minimum(kb1, 24), body, 0)
        return 0

    lax.fori_loop(0, 4, q_block, 0)


QKV_SCRATCH = [((2, 3, 256, 128), BF), ((2, 3, 128), F32), ((1, 256), jnp.int32)]


def near_call(*args):
    out = [
        jax.ShapeDtypeStruct((4, 2, 256, 256), F32),
        jax.ShapeDtypeStruct((1024, 256), BF),
        jax.ShapeDtypeStruct((8, 128), F32),
    ]
    scratch = [
        ((32, 2, 32, 256), BF), ((256, 2048), BF), ((2048, 256), BF), ((8, 256, 32), BF),
    ] + QKV_SCRATCH
    return call(near_kernel, "near", 1, args, out, scratch, 7, 32, 20 * 10**9)


def far_kernel(
    sc, sel, plen, own, oth, lo_own, lo_oth, hi_own, hi_oth, sec_i, acc_i, q_i, most_i, qkvm, qkvo,
    qbm, qbo, prw, prb, n2g, f1m, f1o, b1m, b1o, f2m, f2o, f2b, send, NE, KT, V, Q8, ACC, OUT, M,
    SEC, AI, QI, MI, PW, VEC, F1, B1, F2, QW, QB, PL, sems,
):
    g, base, total = sc[0], sc[1], sc[2]
    pw_a, pw_b = turned(prw, g)
    started = copies(
        sems,
        [
            (lo_own, NE.at[0:16, g]), (lo_oth, NE.at[0:16, 1 - g]), (hi_own, NE.at[48:64, g]),
            (hi_oth, NE.at[48:64, 1 - g]), (qkvm, QW.at[0]), (qkvo, QW.at[1]), (qbm, QB.at[0]),
            (qbo, QB.at[1]), (plen, PL), (most_i, MI), (q_i, QI), (acc_i, AI), (sec_i, SEC),
            (pw_a, PW.at[0:128]), (pw_b, PW.at[128:256]), (prb, VEC.at[0]), (n2g, VEC.at[1]),
            (f2b, VEC.at[2]), (f1m, F1.at[0]), (f1o, F1.at[1]), (b1m, B1.at[0]), (b1o, B1.at[1]),
            (f2m, F2.at[0]), (f2o, F2.at[1]),
        ],
    )
    wait(started[:11])
    block = key_values(NE, KT, V, QW, QB)
    starts_row, ends_row = patch_rows(PL[...])
    edge_lo = limits(0, g, base, total, starts_row, ends_row)[2]
    edge_hi = limits(3, g, base, total, starts_row, ends_row)[3]
    most = lax.fori_loop(jnp.minimum(edge_lo // 2, 4), 4, block, jnp.zeros((8, 256), F32))
    most = lax.fori_loop(12, jnp.maximum((edge_hi + 1) // 2, 12), block, most)
    key_most = jnp.maximum(jnp.max(most), jnp.max(MI[...]))
    mask, scores, step = pair_tools()
    hs = lax.broadcasted_iota(jnp.int32, (256, 128), 0) // 16
    hl = lax.broadcasted_iota(jnp.int32, (256, 128), 1)
    head_sel = jnp.where(hs == hl, 1.0, 0.0).astype(BF)
    def q_most(r0):
        q = QI[pl.ds(r0, 256), :]
        return jnp.max(jnp.dot(q * q, head_sel, preferred_element_type=F32))

    bound = q_most(0)
    for i in range(1, 4):
        bound = jnp.maximum(bound, q_most(256 * i))
    calm = bound * key_most * 1.05 <= 1e4

    @pl.when(jnp.logical_not(calm))
    def _():
        wait(copies(sems.at[24:26], [(own, NE.at[16:48, g]), (oth, NE.at[16:48, 1 - g])]))
        lax.fori_loop(4, 12, block, jnp.zeros((8, 256), F32))

    wait(started[11:])

    def q_block(qb, _):
        r0 = pl.multiple_of(qb * 256, 256)
        q = QI[pl.ds(r0, 256), :]
        for p in range(8):
            Q8[p] = q[:, 32 * p : 32 * p + 32]
        first, finish, kb0, kb1 = limits(qb, g, base, total, starts_row, ends_row)

        def body(kb, _, M=None):
            k0 = pl.multiple_of(kb * 128, 128)
            for h, x in enumerate(step(kb, k0, Q8, KT, V, first, finish, M)):
                ACC[h] += x
            return 0

        @pl.when(calm)
        def _():
            ACC[...] = AI[qb]
            lax.fori_loop(kb0, jnp.minimum(kb1, 8), body, 0)
            lax.fori_loop(jnp.maximum(kb0, 24), kb1, body, 0)

        @pl.when(jnp.logical_not(calm))
        def _():
            ACC[...] = jnp.zeros_like(ACC)
            M[...] = jnp.full(M.shape, -jnp.inf, F32)

            def top(kb, _):
                kt = KT[:, pl.ds(pl.multiple_of(kb * 128, 128), 128)]
                madd = mask(kb, first, finish)
                for p in range(8):
                    M[p] = jnp.maximum(M[p], scores(Q8, p, kt, madd))
                return 0

            lax.fori_loop(kb0, kb1, top, 0)
            for p in range(8):
                for h in range(2):
                    part = M[p, :, 128 * h : 128 * h + 128]
                    M[p, :, 128 * h : 128 * h + 128] = jnp.broadcast_to(
                        jnp.max(part, axis=1, keepdims=True), (256, 128)
                    )
            lax.fori_loop(kb0, kb1, lambda kb, c: body(kb, c, M), 0)

        attn = jnp.concatenate(
            [ACC[h, :, 0:128] / ACC[h, :, 128:256] for h in range(2)], axis=1
        ).astype(BF)
        two = (
            SEC[pl.ds(r0, 256), :].astype(F32)
            + jnp.dot(attn, PW[...], preferred_element_type=F32)
            + VEC[0]
        ).astype(BF)
        wide = two.astype(F32)
        normed = layer_norm(wide, VEC[1]).astype(BF)
        total_rows = wide + VEC[2]
        for h in range(2):
            x = jnp.dot(normed, F1[h], preferred_element_type=F32) + B1[h]
            x = (0.5 * x * (1.0 + lax.erf(x * 0.7071067811865476))).astype(BF)
            total_rows = total_rows + jnp.dot(x, F2[h], preferred_element_type=F32)
        OUT[pl.ds(r0, 256), :] = total_rows.astype(BF)
        return 0

    lax.fori_loop(0, 4, q_block, 0)

    def place(d, _):
        send[pl.ds(pl.multiple_of(32 * d, 32), 32), :] = OUT[
            pl.ds(pl.multiple_of(32 * sel[d], 32), 32), :
        ]
        return 0

    lax.fori_loop(0, 64, place, 0, unroll=4)


def far_call(*args):
    scratch = [
        ((64, 2, 32, 256), BF), ((256, 4096), BF), ((4096, 256), BF), ((8, 256, 32), BF),
        ((2, 256, 256), F32), ((1024, 256), BF), ((8, 256, 256), F32), ((1024, 256), BF),
        ((4, 2, 256, 256), F32), ((1024, 256), BF), ((8, 128), F32), ((256, 256), BF),
        ((3, 1, 256), F32), ((2, 256, 512), BF), ((2, 1, 512), F32), ((2, 512, 256), BF),
    ] + QKV_SCRATCH
    out = [jax.ShapeDtypeStruct((2048, 256), BF)]
    return call(far_kernel, "far", 2, args, out, scratch, 26, 48, 20 * 10**9)[0]


def last_kernel(sc, zs, zv, own, oth, out, R, Z, sems, zsem):
    g = sc[0]
    order = pltpu.make_async_copy(zv, Z, zsem)
    order.start()

    def piece(k, side, ref):
        src = ref.at[zs[64 * k] // 2048]
        return pltpu.make_async_copy(src, R.at[k, side], sems.at[k, side])

    def start(k, _):
        piece(k, g, own).start()
        piece(k, 1 - g, oth).start()
        return 0

    lax.fori_loop(0, 32, start, 0, unroll=4)
    order.wait()
    place = jnp.where(
        lax.broadcasted_iota(jnp.int32, (64, 64), 0) == Z[0:1, 0:64] % 64, 1.0, 0.0
    )
    perm = jnp.transpose(place).astype(BF)

    def step(k, _):
        piece(k, g, own).wait()
        piece(k, 1 - g, oth).wait()
        out[pl.ds(pl.multiple_of(64 * k, 64), 64), :] = jnp.dot(
            perm, R[k].reshape(64, 256), preferred_element_type=F32
        ).astype(BF)
        return 0

    lax.fori_loop(0, 32, step, 0, unroll=4)


def last_call(*args):
    smem, hbm = pl.BlockSpec(memory_space=pltpu.SMEM), pl.BlockSpec(memory_space=pl.ANY)
    return pl.pallas_call(
        last_kernel,
        out_shape=jax.ShapeDtypeStruct((2048, 256), BF),
        in_specs=[smem] * 2 + [hbm] * 3,
        out_specs=pl.BlockSpec(memory_space=pltpu.VMEM),
        scratch_shapes=[
            pltpu.VMEM((32, 2, 32, 256), BF),
            pltpu.VMEM((16, 128), jnp.int32),
            pltpu.SemaphoreType.DMA((32, 2)),
            pltpu.SemaphoreType.DMA,
        ],
        compiler_params=pltpu.CompilerParams(vmem_limit_bytes=16 * 2**20),
        name="relabel",
    )(*args)


def local(
    points, neighbours, patch_len, zorder, conv_w, conv_b, cpe_w, cpe_b, cpe_gain, norm1_gain,
    qkv_w, qkv_b, proj_w, proj_b, norm2_gain, fc1_w, fc1_b, fc2_w, fc2_b,
):
    g = lax.axis_index("grp").astype(jnp.int32)
    me = lax.axis_index("pts").astype(jnp.int32)
    peers = lax.axis_size("pts")
    rows = points.shape[0]
    forward = [(i, i + 1) for i in range(peers - 1)]
    backward = [(i + 1, i) for i in range(peers - 1)]

    def swap(x):
        return lax.ppermute(x, "grp", [(0, 1), (1, 0)])

    def pieces(x):
        return x.reshape(-1, 32, 256)

    order = zorder.reshape(16, 128)
    inner = [[8 * i + j for j in range(8)] for i in range(8)]
    outer = [[8 * j + i for j in range(8)] for i in range(8)]
    table = lax.all_gather(
        jnp.concatenate([order] * 16), "pts", axis=0, tiled=False, axis_index_groups=inner
    )[:, :32].reshape(256, 128)
    table = lax.all_gather(table, "pts", axis=0, tiled=True, axis_index_groups=outer)
    low = lax.ppermute(points[rows - 256 :], "pts", forward)
    high = lax.ppermute(points[:256], "pts", backward)
    conv_m = conv_w.reshape(27 * 256, 128)
    conv_o, bias_o = swap(conv_m), swap(conv_b)
    scalars = jnp.stack([g, me * rows, jnp.int32(rows * peers)])
    section_one, normed, lo_half, hi_half = conv_call(
        scalars, points, low, high, neighbours.T, conv_m, conv_o, conv_b[None], bias_o[None],
        cpe_w, cpe_b[None], cpe_gain[None], norm1_gain[None],
    )
    qkv_m = jnp.transpose(qkv_w, (1, 0, 2))
    weights = (qkv_m, swap(qkv_m), qkv_b, swap(qkv_b))
    fc1_o, fc2_o, b1_o = swap(fc1_w), swap(fc2_w), swap(fc1_b)
    other = swap(normed)
    lo_own = lax.ppermute(lo_half, "pts", forward)
    hi_own = lax.ppermute(hi_half, "pts", backward)
    acc, query, most = near_call(scalars, patch_len[None], pieces(normed), pieces(other), *weights)
    lo_own, hi_own, most = lax.optimization_barrier((lo_own, hi_own, most))
    lo_oth, hi_oth = swap(lo_own), swap(hi_own)
    table = table.reshape(peers, 32, 128)
    sel = jnp.max(jnp.where(table // rows == me, table % rows // 64, 0), axis=(1, 2))
    send = far_call(
        scalars, sel, patch_len[None], pieces(normed), pieces(other), pieces(lo_own),
        pieces(lo_oth), pieces(hi_own), pieces(hi_oth), section_one, acc, query, most, *weights,
        proj_w, proj_b[None], norm2_gain[None], fc1_w, fc1_o, fc1_b[None], b1_o[None], fc2_w,
        fc2_o, fc2_b[None],
    )
    got = lax.all_to_all(send, "pts", split_axis=0, concat_axis=0, tiled=True)
    return last_call(scalars, zorder, order, pieces(got), pieces(swap(got)))


def solution(mesh):
    placed = (
        P("pts", None), P("pts", None), P(), P("pts"), P(None, None, "grp"), P("grp"), P(), P(), P(),
        P(), P(None, None, "grp"), P(None, "grp"), P(), P(), P(), P(None, "grp"), P("grp"),
        P("grp", None), P(),
    )
    return jax.shard_map(
        local, mesh=mesh, in_specs=placed, out_specs=P("pts", None), check_vma=False
    )
```

time: 189 us -> 231 us (1.22)
  waiting for transfers between devices: 1.53 us -> 31 us
  starting transfers between devices: 37.3 us -> 21.4 us
  local copies, waits for them, and re-layouts: 18.9 us -> 34 us
  between operations: 0.38 us -> 13.7 us
  blocking collectives: 35.1 us -> 27.8 us
  Pallas kernels: 89.8 us -> 96.9 us
    all_gather x0 -> x2, waiting for transfers between devices: none -> 28.7 us  [the longest x1 18.8 us: local(): lax.all_gather(table, 'pts', axis=0, tiled=True, axis_index_groups=outer)]
    unnamed x55 -> x75, local copies, waits for them, and re-layouts: 12 us -> 29.4 us
    all_to_all x1 -> x0, starting transfers between devices: 14.4 us -> none  [local(): lax.all_to_all(wanted, 'pts', split_axis=0, concat_axis=0, tiled=True)]
    ppermute x4 -> x2, starting transfers between devices: 10.6 us -> 2.59 us  [the longest x1 1.29 us: local(): lo_own = lax.ppermute(lo_half, 'pts', forward)]
    all_to_all x1, blocking collectives: 35.1 us -> 27.8 us  [local(): got = lax.all_to_all(send, 'pts', split_axis=0, concat_axis=0, tiled=True)]
    pallas_call x1, Pallas kernels: 2.96 us -> 8.83 us  [last_call(): pl.pallas_call(last_kernel, out_shape=jax.ShapeDtypeStruct((2048, 256), B...]
    ppermute x7 -> x11, starting transfers between devices: 7.74 us -> 13.5 us  [swap(): return lax.ppermute(x, 'grp', [(0, 1), (1, 0)])]
    reduce_max x1 -> x2, other arithmetic: 0.09 us -> 4.35 us  [local(): jnp.max(jnp.where(table // rows == me, table % rows // 64, 0), axis=(1, 2))]
  transfers between devices with their start and end apart: 14 -> 17, of which waited for: 1 -> 3; matrix products, arithmetic and copies ran while one was open for 6% -> 9% of each run, Pallas kernels for 23% -> 19%
where the time goes in v3:
time: 231 us; the launch traced here: 229 us
  Pallas kernels  96.9 us (42%)
  local copies, waits for them, and re-layouts  34 us (15%)
  waiting for transfers between devices  31 us (13%)
  blocking collectives  27.8 us (12%)
  starting transfers between devices  21.4 us (9%)
  between operations  13.7 us (6%)
  other arithmetic  4.43 us (2%)
    pallas_call x3, Pallas kernels, call(): pl.pallas_call(kernel, out_shape=out_shape, in_specs=[pl.BlockSpec(memory...  88.1 us
    unnamed x75, local copies, waits for them, and re-layouts  29.4 us
    all_to_all x1, blocking collectives, local(): got = lax.all_to_all(send, 'pts', split_axis=0, concat_axis=0, tiled=True)  27.8 us
    all_gather x1, waiting for transfers between devices, local(): lax.all_gather(table, 'pts', axis=0, tiled=True, axis_index_groups=outer)  18.8 us
    ppermute x11, starting transfers between devices, swap(): return lax.ppermute(x, 'grp', [(0, 1), (1, 0)])  13.5 us
    all_gather x1, waiting for transfers between devices, local(): lax.all_gather(jnp.concatenate([order] * 16), 'pts', axis=0, tiled=False,...  9.86 us
    pallas_call x1, Pallas kernels, last_call(): pl.pallas_call(last_kernel, out_shape=jax.ShapeDtypeStruct((2048, 256), B...  8.83 us
  transfers between devices with their start and end apart: 17, of which 3 were waited for; matrix products, arithmetic and copies ran while one was open for 9% of the time, Pallas kernels for 19%

profile of v3, /device:TPU:1, one launch (start us, length us, event | category | flops | bytes accessed | tf_op | source)
XLA Modules:
  0.0 229.2 jit_solution(4874169163897432010)
XLA Ops:
  6.5 1.4 collective-permute-start.3
  8.0 1.0 fusion.7
  8.9 1.3 collective-permute-start.1
  10.2 4.0 %collective-permute-start = (bf16[256,256]{1,0:T(8,128)(2,1)S(1)}, bf16[256,256]{1,0:T(8,128)(2,1)S(1)}, u32[]{:S(2)}, u32[]{:S(2)}) collective-permute-start(bf16[256,256]{1,0:T(8,128)(2,1)S(1)} %get-tuple-element.26), channel_id=1, source_target_pairs={{0,2},{2,4},{4,6},{6,8},{8,10},{10,12},{12,14},{14,16},{16,18},{18... | collective-permute-start | bytes 393224 | tf_op jit(solution)/shard_map/ppermute | solution.py:487
  14.9 0.7 constant_dynamic-update-slice_fusion.15
  17.7 0.7 constant_dynamic-update-slice_fusion.11
  26.9 1.2 copy-done.29
  28.1 1.2 copy-done.1
  29.4 0.9 copy-done.2
  30.3 0.9 copy-done.6
  33.9 20.7 %conv.1 = (bf16[1024,256]{1,0:T(8,128)(2,1)S(1)}, bf16[1024,256]{1,0:T(8,128)(2,1)S(1)}, bf16[512,256]{1,0:T(8,128)(2,1)S(1)}, bf16[512,256]{1,0:T(8,128)(2,1)S(1)}) custom-call(s32[3]{0:T(128)S(1)} %pad_add_fusion.sc, bf16[2048,256]{1,0:T(8,128)(2,1)S(1)} %copy-done.1, bf16[256,256]{1,0:T(8,128)(2,1)S(1)} %collective-permute-done.low, ...), custom_call_target="tpu_custom_call" | custom-call | flops 30000001024 | bytes 8000000 | tf_op jit(solution)/shard_map/conv/pallas_call | solution.py:113
  54.7 0.8 copy-done.22
  56.6 9.9 %all-gather.6.cloned.1.call-done = s32[2048,128]{1,0:T(8,128)} async-done(((s32[256,128]{1,0:T(8,128)}), s32[2048,128]{1,0:T(8,128)}) %all-gather.6.cloned.1.call-update) | async-done | bytes 1048592 | tf_op jit(solution)/shard_map/all_gather | solution.py:483
  66.5 1.6 slice.12
  68.1 5.6 %collective-permute-start.13 = (bf16[512,256]{1,0:T(8,128)(2,1)S(1)}, bf16[512,256]{1,0:T(8,128)(2,1)S(1)}, u32[]{:S(2)}, u32[]{:S(2)}) collective-permute-start(bf16[512,256]{1,0:T(8,128)(2,1)S(1)} %copy-done.4), channel_id=1, source_target_pairs={{0,1},{1,0},{2,3},{3,2},{4,5},{5,4},{6,7},{7,6},{8,9},{9,8},{10,11... | collective-permute-start | bytes 786440 | tf_op jit(solution)/shard_map/ppermute | solution.py:475
  73.7 1.3 collective-permute-start.5
  75.0 1.3 collective-permute-start.6
  77.0 23.0 %near.1 = (f32[4,2,256,256]{3,2,1,0:T(8,128)S(1)}, bf16[1024,256]{1,0:T(8,128)(2,1)S(1)}, f32[8,128]{1,0:T(8,128)S(1)}) custom-call(s32[3]{0:T(128)S(1)} %pad_add_fusion.sc, s32[1,256]{1,0:T(1,128)S(1)} %bitcast.64, bf16[32,32,256]{2,1,0:T(8,128)(2,1)S(1)} %bitcast.48, bf16[32,32,256]{2,1,0:T(8,128)(2,1)S(1)} %bitcast.50, bf16[3,256,128]{2,1,0:T(8,128)(2,1)S(1)} %bitcast.58, ...), custom_call_target="tpu_custom_call" | custom-call | flops 20000000000 | bytes 8000000 | tf_op jit(solution)/shard_map/near/pallas_call | solution.py:113
  100.0 1.3 copy-done.21
  101.3 0.8 copy-done.24
  103.3 18.8 %all-gather.4.cloned.1.call-done = s32[2048,128]{1,0:T(8,128)} async-done(((s32[256,128]{1,0:T(8,128)}), s32[2048,128]{1,0:T(8,128)}) %all-gather.4.cloned.1.call-update) | async-done | bytes 1048592 | tf_op jit(solution)/shard_map/all_gather | solution.py:486
  122.1 3.5 %fusion.3 = s32[2048]{0:T(1024)} fusion(s32[2048,128]{1,0:T(8,128)} %all-gather.4.cloned.1.call-done, s32[]{:T(128)S(6)} %axis_index.25), kind=kLoop, calls=%fused_computation.12 | loop fusion | flops 9697280 | bytes 1056772 | tf_op jit(solution)/shard_map/reduce_max | solution.py:506
  125.6 1.4 reduce_max.14
  126.9 0.9 reduce_max.18.sel
  127.9 0.9 copy-done.7
  132.1 1.0 copy-done.23
  133.2 1.0 copy-done.25
  134.9 44.4 %far.1 = bf16[2048,256]{1,0:T(8,128)(2,1)S(1)} custom-call(s32[3]{0:T(128)S(1)} %pad_add_fusion.sc, s32[64]{0:T(128)S(1)} %reduce_max.18.sel, s32[1,256]{1,0:T(1,128)S(1)} %bitcast.65, bf16[32,32,256]{2,1,0:T(8,128)(2,1)S(1)} %bitcast.49, bf16[32,32,256]{2,1,0:T(8,128)(2,1)S(1)} %bitcast.51, bf16[16,32,256]{2,1,0:T(8,128)(2,1)S(1)} %bitcast.53, ...), custom_call_target="tpu_custom_call" | custom-call | flops 20000000000 | bytes 8000000 | tf_op jit(solution)/shard_map/far/pallas_call | solution.py:113
  179.3 27.8 %all_to_all.12.own = bf16[64,32,256]{2,1,0:T(8,128)(2,1)S(1)} all-to-all(bf16[64,32,256]{2,1,0:T(8,128)(2,1)S(1)} %bitcast.46), channel_id=1, replica_groups=mesh['pts'=64,'grp'=2] {'pts'}, dimensions={0} | all-to-all | bytes 2097152 | tf_op jit(solution)/shard_map/all_to_all | solution.py:513
  207.1 4.2 %collective-permute-start.14 = (bf16[2048,256]{1,0:T(8,128)(2,1)S(1)}, bf16[2048,256]{1,0:T(8,128)(2,1)S(1)}, u32[]{:S(2)}, u32[]{:S(2)}) collective-permute-start(bf16[2048,256]{1,0:T(8,128)(2,1)S(1)} %bitcast.44), channel_id=1, source_target_pairs={{0,1},{1,0},{2,3},{3,2},{4,5},{5,4},{6,7},{7,6},{8,9},{9,8},{10,11... | collective-permute-start | bytes 3145736 | tf_op jit(solution)/shard_map/ppermute | solution.py:475
  211.3 2.3 collective-permute-done.14
  213.5 8.8 %relabel.1 = bf16[2048,256]{1,0:T(8,128)(2,1)} custom-call(s32[3]{0:T(128)S(1)} %pad_add_fusion.sc, s32[2048]{0:T(1024)S(1)} %copy-done, s32[16,128]{1,0:T(8,128)S(1)} %bitcast.45, bf16[64,32,256]{2,1,0:T(8,128)(2,1)S(1)} %all_to_all.12.own, bf16[64,32,256]{2,1,0:T(8,128)(2,1)S(1)} %bitcast.47), custom_call_target="tpu_custom_call" | custom-call | tf_op jit(solution)/shard_map/relabel/pallas_call | solution.py:447
  (91 shorter events, 20.9 us)
Async XLA Ops:
  6.5 59.9 %all-gather.6.cloned.1.call-start = ((), (), s32[]{:S(2)}) async-start(), calls=%async_computation.2 | async-start | bytes 1179648 | tf_op jit(solution)/shard_map/all_gather | solution.py:483
  6.5 20.3 %collective-permute-start.3 = (f32[128]{0:T(128)}, f32[128]{0:T(128)S(1)}, u32[]{:S(2)}, u32[]{:S(2)}) collective-permute-start(f32[128]{0:T(128)} %param.24), channel_id=1, source_target_pairs={{0,1},{1,0},{2,3},{3,2},{4,5},{5,4},{6,7},{7,6},{8,9},{9,8},{10,11... | collective-permute-start | bytes 1544 | tf_op jit(solution)/shard_map/ppermute | solution.py:475
  8.9 17.9 %collective-permute-start.1 = (bf16[256,256]{1,0:T(8,128)(2,1)S(1)}, bf16[256,256]{1,0:T(8,128)(2,1)S(1)}, u32[]{:S(2)}, u32[]{:S(2)}) collective-permute-start(bf16[256,256]{1,0:T(8,128)(2,1)S(1)} %get-tuple-element.25), channel_id=1, source_target_pairs={{2,0},{4,2},{6,4},{8,6},{10,8},{12,10},{14,12},{16,14},{18,16},{20... | collective-permute-start | bytes 393224 | tf_op jit(solution)/shard_map/ppermute | solution.py:488
  10.2 16.6 %collective-permute-start = (bf16[256,256]{1,0:T(8,128)(2,1)S(1)}, bf16[256,256]{1,0:T(8,128)(2,1)S(1)}, u32[]{:S(2)}, u32[]{:S(2)}) collective-permute-start(bf16[256,256]{1,0:T(8,128)(2,1)S(1)} %get-tuple-element.26), channel_id=1, source_target_pairs={{0,2},{2,4},{4,6},{6,8},{8,10},{10,12},{12,14},{14,16},{16,18},{18... | collective-permute-start | bytes 393224 | tf_op jit(solution)/shard_map/ppermute | solution.py:487
  14.2 12.6 %collective-permute-start.2 = (bf16[6912,128]{1,0:T(8,128)(2,1)}, bf16[6912,128]{1,0:T(8,128)(2,1)S(1)}, u32[]{:S(2)}, u32[]{:S(2)}) collective-permute-start(bf16[6912,128]{1,0:T(8,128)(2,1)} %bitcast.73), channel_id=1, source_target_pairs={{0,1},{1,0},{2,3},{3,2},{4,5},{5,4},{6,7},{7,6},{8,9},{9,8},{10,11... | collective-permute-start | bytes 5308424 | tf_op jit(solution)/shard_map/ppermute | solution.py:475
  26.7 95.3 %all-gather.4.cloned.1.call-start = ((), (), s32[]{:S(2)}) async-start(), calls=%async_computation.1 | async-start | bytes 1179648 | tf_op jit(solution)/shard_map/all_gather | solution.py:486
  26.9 1.2 copy-start.29
  28.1 1.2 copy-start.1
  29.4 0.9 copy-start.2
  30.3 0.9 copy-start.6
  33.9 21.6 %copy-start.5 = (bf16[256,3,128]{2,0,1:T(8,128)(2,1)S(1)}, bf16[256,3,128]{2,0,1:T(8,128)(2,1)}, u32[]{:S(2)}) copy-start(bf16[256,3,128]{2,0,1:T(8,128)(2,1)} %param.29) | copy-start | bytes 589828
  33.9 22.1 %copy-start.8 = (f32[3,128]{1,0:T(4,128)S(1)}, f32[3,128]{1,0:T(4,128)}, u32[]{:S(2)}) copy-start(f32[3,128]{1,0:T(4,128)} %qbm.3) | copy-start | bytes 4612
  33.9 22.2 %copy-start.9 = (f32[512]{0:T(512)S(1)}, f32[512]{0:T(512)}, u32[]{:S(2)}) copy-start(f32[512]{0:T(512)} %param.35) | copy-start | bytes 6148
  33.9 22.6 %copy-start.3 = (bf16[256,512]{1,0:T(8,128)(2,1)S(1)}, bf16[256,512]{1,0:T(8,128)(2,1)}, u32[]{:S(2)}) copy-start(bf16[256,512]{1,0:T(8,128)(2,1)} %f1m.1) | copy-start | bytes 786436
  33.9 34.1 %copy-start.4 = (bf16[512,256]{1,0:T(8,128)(2,1)S(1)}, bf16[512,256]{1,0:T(8,128)(2,1)}, u32[]{:S(2)}) copy-start(bf16[512,256]{1,0:T(8,128)(2,1)} %f2m.1) | copy-start | bytes 786436
  55.5 19.5 %collective-permute-start.4 = (bf16[1024,256]{1,0:T(8,128)(2,1)S(1)}, bf16[1024,256]{1,0:T(8,128)(2,1)S(1)}, u32[]{:S(2)}, u32[]{:S(2)}) collective-permute-start(bf16[1024,256]{1,0:T(8,128)(2,1)S(1)} %get-tuple-element.15), channel_id=1, source_target_pairs={{0,1},{1,0},{2,3},{3,2},{4,5},{5,4},{6,7},{7,6},{8,9},{9,8},{10,11... | collective-permute-start | bytes 1572872 | tf_op jit(solution)/shard_map/ppermute | solution.py:475
  55.5 18.2 %collective-permute-start.7 = (bf16[3,256,128]{2,1,0:T(8,128)(2,1)S(1)}, bf16[3,256,128]{2,1,0:T(8,128)(2,1)S(1)}, u32[]{:S(2)}, u32[]{:S(2)}) collective-permute-start(bf16[3,256,128]{2,1,0:T(8,128)(2,1)S(1)} %bitcast.57), channel_id=1, source_target_pairs={{0,1},{1,0},{2,3},{3,2},{4,5},{5,4},{6,7},{7,6},{8,9},{9,8},{10,11... | collective-permute-start | bytes 589832 | tf_op jit(solution)/shard_map/ppermute | solution.py:475
  56.0 12.1 %collective-permute-start.8 = (f32[3,128]{1,0:T(4,128)S(1)}, f32[3,128]{1,0:T(4,128)S(1)}, u32[]{:S(2)}, u32[]{:S(2)}) collective-permute-start(f32[3,128]{1,0:T(4,128)S(1)} %copy-done.8), channel_id=1, source_target_pairs={{0,1},{1,0},{2,3},{3,2},{4,5},{5,4},{6,7},{7,6},{8,9},{9,8},{10,11... | collective-permute-start | bytes 4616 | tf_op jit(solution)/shard_map/ppermute | solution.py:475
  56.1 71.7 %collective-permute-start.12 = (f32[512]{0:T(512)S(1)}, f32[512]{0:T(512)}, u32[]{:S(2)}, u32[]{:S(2)}) collective-permute-start(f32[512]{0:T(512)S(1)} %copy-done.9), channel_id=1, source_target_pairs={{0,1},{1,0},{2,3},{3,2},{4,5},{5,4},{6,7},{7,6},{8,9},{9,8},{10,11... | collective-permute-start | bytes 6152 | tf_op jit(solution)/shard_map/ppermute | solution.py:475
  56.5 71.3 %collective-permute-start.11 = (bf16[256,512]{1,0:T(8,128)(2,1)S(1)}, bf16[256,512]{1,0:T(8,128)(2,1)S(1)}, u32[]{:S(2)}, u32[]{:S(2)}) collective-permute-start(bf16[256,512]{1,0:T(8,128)(2,1)S(1)} %copy-done.3), channel_id=1, source_target_pairs={{0,1},{1,0},{2,3},{3,2},{4,5},{5,4},{6,7},{7,6},{8,9},{9,8},{10,11... | collective-permute-start | bytes 786440 | tf_op jit(solution)/shard_map/ppermute | solution.py:475
  68.1 31.9 %copy-start.10 = (f32[3,128]{1,0:T(4,128)}, f32[3,128]{1,0:T(4,128)S(1)}, u32[]{:S(2)}) copy-start(f32[3,128]{1,0:T(4,128)S(1)} %collective-permute-done.8.qbo) | copy-start | bytes 4612
  68.1 59.7 %collective-permute-start.13 = (bf16[512,256]{1,0:T(8,128)(2,1)S(1)}, bf16[512,256]{1,0:T(8,128)(2,1)S(1)}, u32[]{:S(2)}, u32[]{:S(2)}) collective-permute-start(bf16[512,256]{1,0:T(8,128)(2,1)S(1)} %copy-done.4), channel_id=1, source_target_pairs={{0,1},{1,0},{2,3},{3,2},{4,5},{5,4},{6,7},{7,6},{8,9},{9,8},{10,11... | collective-permute-start | bytes 786440 | tf_op jit(solution)/shard_map/ppermute | solution.py:475
  73.7 29.0 %collective-permute-start.5 = (bf16[512,256]{1,0:T(8,128)(2,1)S(1)}, bf16[512,256]{1,0:T(8,128)(2,1)S(1)}, u32[]{:S(2)}, u32[]{:S(2)}) collective-permute-start(bf16[512,256]{1,0:T(8,128)(2,1)S(1)} %get-tuple-element.16), channel_id=1, source_target_pairs={{0,2},{2,4},{4,6},{6,8},{8,10},{10,12},{12,14},{14,16},{16,18},{18... | collective-permute-start | bytes 786440 | tf_op jit(solution)/shard_map/ppermute | solution.py:500
  75.0 27.7 %collective-permute-start.6 = (bf16[512,256]{1,0:T(8,128)(2,1)S(1)}, bf16[512,256]{1,0:T(8,128)(2,1)S(1)}, u32[]{:S(2)}, u32[]{:S(2)}) collective-permute-start(bf16[512,256]{1,0:T(8,128)(2,1)S(1)} %get-tuple-element.17), channel_id=1, source_target_pairs={{2,0},{4,2},{6,4},{8,6},{10,8},{12,10},{14,12},{16,14},{18,16},{20... | collective-permute-start | bytes 786440 | tf_op jit(solution)/shard_map/ppermute | solution.py:501
  100.0 1.3 copy-start.21
  102.7 25.1 %collective-permute-start.9 = (bf16[512,256]{1,0:T(8,128)(2,1)S(1)}, bf16[512,256]{1,0:T(8,128)(2,1)S(1)}, u32[]{:S(2)}, u32[]{:S(2)}) collective-permute-start(bf16[512,256]{1,0:T(8,128)(2,1)S(1)} %collective-permute-done.5), channel_id=1, source_target_pairs={{0,1},{1,0},{2,3},{3,2},{4,5},{5,4},{6,7},{7,6},{8,9},{9,8},{10,11... | collective-permute-start | bytes 786440 | tf_op jit(solution)/shard_map/ppermute | solution.py:475
  102.8 25.1 %collective-permute-start.10 = (bf16[512,256]{1,0:T(8,128)(2,1)S(1)}, bf16[512,256]{1,0:T(8,128)(2,1)S(1)}, u32[]{:S(2)}, u32[]{:S(2)}) collective-permute-start(bf16[512,256]{1,0:T(8,128)(2,1)S(1)} %collective-permute-done.6), channel_id=1, source_target_pairs={{0,1},{1,0},{2,3},{3,2},{4,5},{5,4},{6,7},{7,6},{8,9},{9,8},{10,11... | collective-permute-start | bytes 786440 | tf_op jit(solution)/shard_map/ppermute | solution.py:475
  127.9 0.9 copy-start.7
  132.1 1.0 copy-start.23
  133.2 1.0 copy-start.25
  179.3 34.2 %copy-start = (s32[2048]{0:T(1024)S(1)}, s32[2048]{0:T(1024)}, u32[]{:S(2)}) copy-start(s32[2048]{0:T(1024)} %zs.1) | copy-start | bytes 24580
  207.1 6.5 %collective-permute-start.14 = (bf16[2048,256]{1,0:T(8,128)(2,1)S(1)}, bf16[2048,256]{1,0:T(8,128)(2,1)S(1)}, u32[]{:S(2)}, u32[]{:S(2)}) collective-permute-start(bf16[2048,256]{1,0:T(8,128)(2,1)S(1)} %bitcast.44), channel_id=1, source_target_pairs={{0,1},{1,0},{2,3},{3,2},{4,5},{5,4},{6,7},{7,6},{8,9},{9,8},{10,11... | collective-permute-start | bytes 3145736 | tf_op jit(solution)/shard_map/ppermute | solution.py:475
  (15 other events, 10.3 us)
Sparse Core Ops, SparseCore 0:
  26.8 39.5 all-gather.5
  68.8 53.2 all-gather.3

commit v4 on v3

--- a/solution.py
+++ b/solution.py
@@ -7,6 +7,7 @@
 
 F32=jnp.float32; BF=jnp.bfloat16
 
+VMEM_BYTES = 64 * 2**20 - 65536
 Q_SCALE = 0.25 * 1.4426950408889634
 
 
@@ -109,15 +110,15 @@
     lax.fori_loop(0, 4, finish, 0)
 
 
-def call(kernel, name, smem, args, out_shape, scratch, sems, mib, flops):
+def call(kernel, name, smem, args, out_shape, scratch, sems, flops):
     return pl.pallas_call(
         kernel,
         out_shape=out_shape,
         in_specs=[pl.BlockSpec(memory_space=pltpu.SMEM)] * smem
-        + [pl.BlockSpec(memory_space=pl.ANY)] * (len(args) - smem),
+        + [pl.BlockSpec(memory_space=pltpu.HBM)] * (len(args) - smem),
         out_specs=[pl.BlockSpec(memory_space=pltpu.VMEM)] * len(out_shape),
         scratch_shapes=[pltpu.VMEM(*x) for x in scratch] + [pltpu.SemaphoreType.DMA((sems,))],
-        compiler_params=pltpu.CompilerParams(vmem_limit_bytes=mib * 2**20),
+        compiler_params=pltpu.CompilerParams(vmem_limit_bytes=VMEM_BYTES),
         cost_estimate=pl.CostEstimate(flops=flops, bytes_accessed=8 * 10**6, transcendentals=10**7),
         name=name,
     )(*args)
@@ -129,7 +130,7 @@
         ((2560, 256), BF), ((27, 2048), jnp.int32), ((2048, 27), jnp.int32), ((27 * RB, 768), BF), ((1024, 6912), BF),
         ((6912, 256), BF), ((256, 256), BF), ((1, 256), F32), ((3, 1, 256), F32),
     ]
-    return call(conv_kernel, "conv", 1, args, out, scratch, 13, 50, 30 * 10**9)
+    return call(conv_kernel, "conv", 1, args, out, scratch, 13, 30 * 10**9)
 
 
 def key_values(NE, KT, V, QW, QB):
@@ -281,7 +282,7 @@
     scratch = [
         ((32, 2, 32, 256), BF), ((256, 2048), BF), ((2048, 256), BF), ((8, 256, 32), BF),
     ] + QKV_SCRATCH
-    return call(near_kernel, "near", 1, args, out, scratch, 7, 32, 20 * 10**9)
+    return call(near_kernel, "near", 1, args, out, scratch, 7, 20 * 10**9)
 
 
 def far_kernel(
@@ -407,57 +408,31 @@
         ((3, 1, 256), F32), ((2, 256, 512), BF), ((2, 1, 512), F32), ((2, 512, 256), BF),
     ] + QKV_SCRATCH
     out = [jax.ShapeDtypeStruct((2048, 256), BF)]
-    return call(far_kernel, "far", 2, args, out, scratch, 26, 48, 20 * 10**9)[0]
-
-
-def last_kernel(sc, zs, zv, own, oth, out, R, Z, sems, zsem):
+    return call(far_kernel, "far", 2, args, out, scratch, 26, 20 * 10**9)[0]
+
+
+def last_kernel(sc, zs, zv, own, oth, out, R, Z, sems):
     g = sc[0]
-    order = pltpu.make_async_copy(zv, Z, zsem)
-    order.start()
-
-    def piece(k, side, ref):
-        src = ref.at[zs[64 * k] // 2048]
-        return pltpu.make_async_copy(src, R.at[k, side], sems.at[k, side])
-
-    def start(k, _):
-        piece(k, g, own).start()
-        piece(k, 1 - g, oth).start()
-        return 0
-
-    lax.fori_loop(0, 32, start, 0, unroll=4)
-    order.wait()
+    wait(copies(sems, [(zv, Z), (own, R.at[:, g]), (oth, R.at[:, 1 - g])]))
     place = jnp.where(
         lax.broadcasted_iota(jnp.int32, (64, 64), 0) == Z[0:1, 0:64] % 64, 1.0, 0.0
     )
     perm = jnp.transpose(place).astype(BF)
 
     def step(k, _):
-        piece(k, g, own).wait()
-        piece(k, 1 - g, oth).wait()
+        rows = R[lax.shift_right_logical(zs[64 * k], 11)].reshape(64, 256)
         out[pl.ds(pl.multiple_of(64 * k, 64), 64), :] = jnp.dot(
-            perm, R[k].reshape(64, 256), preferred_element_type=F32
+            perm, rows, preferred_element_type=F32
         ).astype(BF)
         return 0
 
-    lax.fori_loop(0, 32, step, 0, unroll=4)
+    lax.fori_loop(0, 32, step, 0, unroll=8)
 
 
 def last_call(*args):
-    smem, hbm = pl.BlockSpec(memory_space=pltpu.SMEM), pl.BlockSpec(memory_space=pl.ANY)
-    return pl.pallas_call(
-        last_kernel,
-        out_shape=jax.ShapeDtypeStruct((2048, 256), BF),
-        in_specs=[smem] * 2 + [hbm] * 3,
-        out_specs=pl.BlockSpec(memory_space=pltpu.VMEM),
-        scratch_shapes=[
-            pltpu.VMEM((32, 2, 32, 256), BF),
-            pltpu.VMEM((16, 128), jnp.int32),
-            pltpu.SemaphoreType.DMA((32, 2)),
-            pltpu.SemaphoreType.DMA,
-        ],
-        compiler_params=pltpu.CompilerParams(vmem_limit_bytes=16 * 2**20),
-        name="relabel",
-    )(*args)
+    out = [jax.ShapeDtypeStruct((2048, 256), BF)]
+    scratch = [((64, 2, 32, 256), BF), ((16, 128), jnp.int32)]
+    return call(last_kernel, "relabel", 2, args, out, scratch, 3, 10**9)[0]
 
 
 def local(
@@ -480,12 +455,16 @@
     order = zorder.reshape(16, 128)
     inner = [[8 * i + j for j in range(8)] for i in range(8)]
     outer = [[8 * j + i for j in range(8)] for i in range(8)]
-    table = lax.all_gather(
-        jnp.concatenate([order] * 16), "pts", axis=0, tiled=False, axis_index_groups=inner
-    )[:, :32].reshape(256, 128)
-    table = lax.all_gather(table, "pts", axis=0, tiled=True, axis_index_groups=outer)
+    sources = jnp.arange(64, dtype=jnp.int32).reshape(8, 8).T[:, :, None, None]
+    wanted = jnp.max(
+        jnp.where(order // rows == sources, order % rows // 64, 0), axis=2
+    )
+    wanted = lax.all_to_all(
+        wanted, "pts", split_axis=0, concat_axis=0, tiled=True, axis_index_groups=inner
+    )
     low = lax.ppermute(points[rows - 256 :], "pts", forward)
     high = lax.ppermute(points[:256], "pts", backward)
+    wanted, low = lax.optimization_barrier((wanted, low))
     conv_m = conv_w.reshape(27 * 256, 128)
     conv_o, bias_o = swap(conv_m), swap(conv_b)
     scalars = jnp.stack([g, me * rows, jnp.int32(rows * peers)])
@@ -497,13 +476,16 @@
     weights = (qkv_m, swap(qkv_m), qkv_b, swap(qkv_b))
     fc1_o, fc2_o, b1_o = swap(fc1_w), swap(fc2_w), swap(fc1_b)
     other = swap(normed)
+    wanted, other = lax.optimization_barrier((jnp.transpose(wanted, (1, 0, 2)), other))
+    sel = lax.all_to_all(
+        wanted, "pts", split_axis=0, concat_axis=0, tiled=True, axis_index_groups=outer
+    )
     lo_own = lax.ppermute(lo_half, "pts", forward)
     hi_own = lax.ppermute(hi_half, "pts", backward)
     acc, query, most = near_call(scalars, patch_len[None], pieces(normed), pieces(other), *weights)
     lo_own, hi_own, most = lax.optimization_barrier((lo_own, hi_own, most))
     lo_oth, hi_oth = swap(lo_own), swap(hi_own)
-    table = table.reshape(peers, 32, 128)
-    sel = jnp.max(jnp.where(table // rows == me, table % rows // 64, 0), axis=(1, 2))
+    sel = jnp.max(sel, axis=2).reshape(64)
     send = far_call(
         scalars, sel, patch_len[None], pieces(normed), pieces(other), pieces(lo_own),
         pieces(lo_oth), pieces(hi_own), pieces(hi_oth), section_one, acc, query, most, *weights,

time: 231 us -> 188 us (0.81); the launches traced: 229 us -> 189 us
  local copies, waits for them, and re-layouts: 34 us -> 5.61 us
  waiting for transfers between devices: 31 us -> 13.7 us
  starting transfers between devices: 21.4 us -> 38.1 us
  between operations: 13.7 us -> 0.32 us
  Pallas kernels: 96.9 us -> 99.6 us
    all_gather x2 -> x0, waiting for transfers between devices: 28.7 us -> none  [the longest x1 18.8 us: local(): lax.all_gather(table, 'pts', axis=0, tiled=True, axis_index_groups=outer)]
    unnamed x75 -> x10, local copies, waits for them, and re-layouts: 29.4 us -> 2.66 us
    all_to_all x0 -> x2, starting transfers between devices: none -> 18.9 us  [local(): lax.all_to_all(wanted, 'pts', split_axis=0, concat_axis=0, tiled=True, ax...]
    pallas_call x3 -> x4, Pallas kernels: 88.1 us -> 99.6 us  [call(): pl.pallas_call(kernel, out_shape=out_shape, in_specs=[pl.BlockSpec(memory...]
    all_to_all x0 -> x2, waiting for transfers between devices: none -> 10.5 us  [local(): lax.all_to_all(wanted, 'pts', split_axis=0, concat_axis=0, tiled=True, ax...]
    pallas_call x1 -> x0, Pallas kernels: 8.83 us -> none  [last_call(): pl.pallas_call(last_kernel, out_shape=jax.ShapeDtypeStruct((2048, 256), B...]
    ppermute x11, starting transfers between devices: 13.5 us -> 9.64 us  [swap(): return lax.ppermute(x, 'grp', [(0, 1), (1, 0)])]
    reduce_max x2, other arithmetic: 4.35 us -> 1.04 us  [the longest x1 0.83 us: local(): jnp.max(jnp.where(order // rows == sources, order % rows // 64, 0), axis=2)]
  transfers between devices with their start and end apart: 17 -> 17, of which waited for: 3 -> 4; matrix products, arithmetic and copies ran while one was open for 9% -> 3% of each run, Pallas kernels for 19% -> 13%
where the time goes in v4:
time: 188 us; the launch traced here: 189 us
  Pallas kernels  99.6 us (53%)
  starting transfers between devices  38.1 us (20%)
  blocking collectives  29.1 us (15%)
  waiting for transfers between devices  13.7 us (7%)
  local copies, waits for them, and re-layouts  5.61 us (3%)
  other arithmetic  2.37 us (1%)
    pallas_call x4, Pallas kernels, call(): pl.pallas_call(kernel, out_shape=out_shape, in_specs=[pl.BlockSpec(memory...  99.6 us
    all_to_all x1, blocking collectives, local(): got = lax.all_to_all(send, 'pts', split_axis=0, concat_axis=0, tiled=True)  29.1 us
    all_to_all x2, starting transfers between devices, local(): lax.all_to_all(wanted, 'pts', split_axis=0, concat_axis=0, tiled=True, ax...  18.9 us
    all_to_all x2, waiting for transfers between devices, local(): lax.all_to_all(wanted, 'pts', split_axis=0, concat_axis=0, tiled=True, ax...  10.5 us
    ppermute x11, starting transfers between devices, swap(): return lax.ppermute(x, 'grp', [(0, 1), (1, 0)])  9.64 us
    ppermute x1, starting transfers between devices, local(): low = lax.ppermute(points[rows - 256:], 'pts', forward)  3.99 us
  transfers between devices with their start and end apart: 17, of which 4 were waited for; matrix products, arithmetic and copies ran while one was open for 3% of the time, Pallas kernels for 13%

profile of v4, /device:TPU:1, one launch (start us, length us, event | category | flops | bytes accessed | tf_op | source)
XLA Modules:
  0.0 188.8 jit_solution(9531050386240123230)
XLA Ops:
  0.0 1.4 collective-permute-start.2
  1.4 1.0 fusion.4
  2.4 1.3 collective-permute-start.1
  3.7 4.0 %collective-permute-start = (bf16[256,256]{1,0:T(8,128)(2,1)S(1)}, bf16[256,256]{1,0:T(8,128)(2,1)S(1)}, u32[]{:S(2)}, u32[]{:S(2)}) collective-permute-start(bf16[256,256]{1,0:T(8,128)(2,1)S(1)} %get-tuple-element.34), channel_id=1, source_target_pairs={{0,2},{2,4},{4,6},{6,8},{8,10},{10,12},{12,14},{14,16},{16,18},{18... | collective-permute-start | bytes 393224 | tf_op jit(solution)/shard_map/ppermute | solution.py:465
  7.7 0.7 add_select_fusion.2
  8.4 0.8 select_reduce_fusion
  9.3 7.0 %all-to-all-start = ((s32[8,8,128]{2,1,0:T(8,128)}), s32[8,8,128]{2,1,0:T(8,128)}, u32[]{:S(2)}, u32[]{:S(2)}) async-start(s32[8,8,128]{2,1,0:T(8,128)} %select_reduce_fusion), calls=%async_computation | async-start | bytes 65536 | tf_op jit(solution)/shard_map/all_to_all | solution.py:462
  16.2 0.6 pad_add_fusion.sc
  16.8 4.6 %all-to-all-done = s32[8,8,128]{2,1,0:T(8,128)} async-done(((s32[8,8,128]{2,1,0:T(8,128)}), s32[8,8,128]{2,1,0:T(8,128)}, u32[]{:S(2)}, u32[]{:S(2)}) %all-to-all-start) | async-done | bytes 32800 | tf_op jit(solution)/shard_map/all_to_all | solution.py:462
  21.5 0.7 copy-done.2
  22.2 22.7 %conv.1 = (bf16[1024,256]{1,0:T(8,128)(2,1)}, bf16[1024,256]{1,0:T(8,128)(2,1)}, bf16[512,256]{1,0:T(8,128)(2,1)}, bf16[512,256]{1,0:T(8,128)(2,1)}) custom-call(s32[3]{0:T(128)} %pad_add_fusion.sc, bf16[2048,256]{1,0:T(8,128)(2,1)} %pts.1, bf16[256,256]{1,0:T(8,128)(2,1)} %copy-done.3, bf16[256,256]{1,0:T(8,128)(2,1)} %copy-done.2, s32[27,2048]{1,0:T(8,128)} %bitcast.37, ...), custom_call_target="tpu_custom_call" | custom-call | flops 30000001024 | bytes 8000000 | tf_op jit(solution)/shard_map/conv/pallas_call | solution.py:114
  44.9 2.6 %collective-permute-start.4 = (bf16[1024,256]{1,0:T(8,128)(2,1)}, bf16[1024,256]{1,0:T(8,128)(2,1)}, u32[]{:S(2)}, u32[]{:S(2)}) collective-permute-start(bf16[1024,256]{1,0:T(8,128)(2,1)} %get-tuple-element.21), channel_id=1, source_target_pairs={{0,1},{1,0},{2,3},{3,2},{4,5},{5,4},{6,7},{7,6},{8,9},{9,8},{10,11... | collective-permute-start | bytes 1572872 | tf_op jit(solution)/shard_map/ppermute | solution.py:450
  47.6 0.4 collective-permute-start.8
  48.1 0.4 collective-permute-start.13
  48.5 0.9 collective-permute-done.4
  49.4 3.0 %collective-permute-start.5 = (bf16[512,256]{1,0:T(8,128)(2,1)}, bf16[512,256]{1,0:T(8,128)(2,1)}, u32[]{:S(2)}, u32[]{:S(2)}) collective-permute-start(bf16[512,256]{1,0:T(8,128)(2,1)} %get-tuple-element.24), channel_id=1, source_target_pairs={{0,2},{2,4},{4,6},{6,8},{8,10},{10,12},{12,14},{14,16},{16,18},{18... | collective-permute-start | bytes 786440 | tf_op jit(solution)/shard_map/ppermute | solution.py:483
  52.4 1.3 collective-permute-start.6
  53.7 25.4 %near.1 = (f32[4,2,256,256]{3,2,1,0:T(8,128)}, bf16[1024,256]{1,0:T(8,128)(2,1)}, f32[8,128]{1,0:T(8,128)}) custom-call(s32[3]{0:T(128)} %pad_add_fusion.sc, s32[1,256]{1,0:T(1,128)} %bitcast.45, bf16[32,32,256]{2,1,0:T(8,128)(2,1)} %bitcast.35, bf16[32,32,256]{2,1,0:T(8,128)(2,1)} %bitcast.13.oth, bf16[3,256,128]{2,1,0:T(8,128)(2,1)} %bitcast.39, ...), custom_call_target="tpu_custom_call" | custom-call | flops 20000000000 | bytes 8000000 | tf_op jit(solution)/shard_map/near/pallas_call | solution.py:114
  79.1 0.7 collective-permute-start.9
  79.9 1.4 copy.21
  81.3 11.9 %all-to-all-start.1 = ((s32[8,8,128]{2,1,0:T(8,128)}), s32[8,8,128]{2,1,0:T(8,128)S(1)}, u32[]{:S(2)}, u32[]{:S(2)}) async-start(s32[8,8,128]{2,1,0:T(8,128)} %copy.21), calls=%async_computation.1 | async-start | bytes 65536 | tf_op jit(solution)/shard_map/all_to_all | solution.py:480
  93.2 0.7 collective-permute-start.12
  93.9 5.9 %all-to-all-done.1 = s32[8,8,128]{2,1,0:T(8,128)S(1)} async-done(((s32[8,8,128]{2,1,0:T(8,128)}), s32[8,8,128]{2,1,0:T(8,128)S(1)}, u32[]{:S(2)}, u32[]{:S(2)}) %all-to-all-start.1) | async-done | bytes 32800 | tf_op jit(solution)/shard_map/all_to_all | solution.py:480
  99.8 0.2 reduce_max.19
  100.0 0.6 reshape.84.sel
  100.7 47.2 %far.1 = bf16[2048,256]{1,0:T(8,128)(2,1)} custom-call(s32[3]{0:T(128)} %pad_add_fusion.sc, s32[64]{0:T(128)} %reshape.84.sel, s32[1,256]{1,0:T(1,128)} %bitcast.46, bf16[32,32,256]{2,1,0:T(8,128)(2,1)} %bitcast.36, bf16[32,32,256]{2,1,0:T(8,128)(2,1)} %bitcast.13.oth, bf16[16,32,256]{2,1,0:T(8,128)(2,1)} %bitcast.15.lo_own, ...), custom_call_target="tpu_custom_call" | custom-call | flops 20000000000 | bytes 8000000 | tf_op jit(solution)/shard_map/far/pallas_call | solution.py:114
  147.9 29.1 %all_to_all.22.own = bf16[64,32,256]{2,1,0:T(8,128)(2,1)S(1)} all-to-all(bf16[64,32,256]{2,1,0:T(8,128)(2,1)} %bitcast.29), channel_id=1, replica_groups=mesh['pts'=64,'grp'=2] {'pts'}, dimensions={0} | all-to-all | bytes 2097152 | tf_op jit(solution)/shard_map/all_to_all | solution.py:495
  177.0 1.0 copy-done
  178.0 3.1 %collective-permute-start.14 = (bf16[2048,256]{1,0:T(8,128)(2,1)S(1)}, bf16[2048,256]{1,0:T(8,128)(2,1)S(1)}, u32[]{:S(2)}, u32[]{:S(2)}) collective-permute-start(bf16[2048,256]{1,0:T(8,128)(2,1)S(1)} %bitcast.30), channel_id=1, source_target_pairs={{0,1},{1,0},{2,3},{3,2},{4,5},{5,4},{6,7},{7,6},{8,9},{9,8},{10,11... | collective-permute-start | bytes 3145736 | tf_op jit(solution)/shard_map/ppermute | solution.py:450
  181.1 2.3 %collective-permute-done.14 = bf16[2048,256]{1,0:T(8,128)(2,1)S(1)} collective-permute-done((bf16[2048,256]{1,0:T(8,128)(2,1)S(1)}, bf16[2048,256]{1,0:T(8,128)(2,1)S(1)}, u32[]{:S(2)}, u32[]{:S(2)}) %collective-permute-start.14) | collective-permute-done | bytes 1048608 | tf_op jit(solution)/shard_map/ppermute | solution.py:450
  183.4 1.0 copy-done.1
  184.4 4.3 %relabel.1 = bf16[2048,256]{1,0:T(8,128)(2,1)} custom-call(s32[3]{0:T(128)} %pad_add_fusion.sc, s32[2048]{0:T(1024)} %zs.1, s32[16,128]{1,0:T(8,128)} %bitcast.31, bf16[64,32,256]{2,1,0:T(8,128)(2,1)} %copy-done, bf16[64,32,256]{2,1,0:T(8,128)(2,1)} %bitcast.34), custom_call_target="tpu_custom_call" | custom-call | flops 1000000000 | bytes 8000000 | tf_op jit(solution)/shard_map/relabel/pallas_call | solution.py:114
  (25 shorter events, 0.3 us)
Async XLA Ops:
  0.0 22.2 %collective-permute-start.2 = (bf16[6912,128]{1,0:T(8,128)(2,1)}, bf16[6912,128]{1,0:T(8,128)(2,1)}, u32[]{:S(2)}, u32[]{:S(2)}) collective-permute-start(bf16[6912,128]{1,0:T(8,128)(2,1)} %bitcast.32), channel_id=1, source_target_pairs={{0,1},{1,0},{2,3},{3,2},{4,5},{5,4},{6,7},{7,6},{8,9},{9,8},{10,11... | collective-permute-start | bytes 5308424 | tf_op jit(solution)/shard_map/ppermute | solution.py:450
  1.4 20.0 %collective-permute-start.3 = (f32[128]{0:T(128)}, f32[128]{0:T(128)S(1)}, u32[]{:S(2)}, u32[]{:S(2)}) collective-permute-start(f32[128]{0:T(128)} %param.24), channel_id=1, source_target_pairs={{0,1},{1,0},{2,3},{3,2},{4,5},{5,4},{6,7},{7,6},{8,9},{9,8},{10,11... | collective-permute-start | bytes 1544 | tf_op jit(solution)/shard_map/ppermute | solution.py:450
  2.4 19.1 %collective-permute-start.1 = (bf16[256,256]{1,0:T(8,128)(2,1)S(1)}, bf16[256,256]{1,0:T(8,128)(2,1)S(1)}, u32[]{:S(2)}, u32[]{:S(2)}) collective-permute-start(bf16[256,256]{1,0:T(8,128)(2,1)S(1)} %get-tuple-element.33), channel_id=1, source_target_pairs={{2,0},{4,2},{6,4},{8,6},{10,8},{12,10},{14,12},{16,14},{18,16},{20... | collective-permute-start | bytes 393224 | tf_op jit(solution)/shard_map/ppermute | solution.py:466
  3.7 17.7 %collective-permute-start = (bf16[256,256]{1,0:T(8,128)(2,1)S(1)}, bf16[256,256]{1,0:T(8,128)(2,1)S(1)}, u32[]{:S(2)}, u32[]{:S(2)}) collective-permute-start(bf16[256,256]{1,0:T(8,128)(2,1)S(1)} %get-tuple-element.34), channel_id=1, source_target_pairs={{0,2},{2,4},{4,6},{6,8},{8,10},{10,12},{12,14},{14,16},{16,18},{18... | collective-permute-start | bytes 393224 | tf_op jit(solution)/shard_map/ppermute | solution.py:465
  9.3 12.2 %all-to-all-start = ((s32[8,8,128]{2,1,0:T(8,128)}), s32[8,8,128]{2,1,0:T(8,128)}, u32[]{:S(2)}, u32[]{:S(2)}) async-start(s32[8,8,128]{2,1,0:T(8,128)} %select_reduce_fusion), calls=%async_computation | async-start | bytes 65536 | tf_op jit(solution)/shard_map/all_to_all | solution.py:462
  21.5 0.7 copy-start.3
  21.5 0.7 copy-start.4
  21.5 0.7 copy-start.2
  44.9 4.5 %collective-permute-start.4 = (bf16[1024,256]{1,0:T(8,128)(2,1)}, bf16[1024,256]{1,0:T(8,128)(2,1)}, u32[]{:S(2)}, u32[]{:S(2)}) collective-permute-start(bf16[1024,256]{1,0:T(8,128)(2,1)} %get-tuple-element.21), channel_id=1, source_target_pairs={{0,1},{1,0},{2,3},{3,2},{4,5},{5,4},{6,7},{7,6},{8,9},{9,8},{10,11... | collective-permute-start | bytes 1572872 | tf_op jit(solution)/shard_map/ppermute | solution.py:450
  47.5 6.2 %collective-permute-start.7 = (bf16[3,256,128]{2,1,0:T(8,128)(2,1)}, bf16[3,256,128]{2,1,0:T(8,128)(2,1)}, u32[]{:S(2)}, u32[]{:S(2)}) collective-permute-start(bf16[3,256,128]{2,1,0:T(8,128)(2,1)} %bitcast.38), channel_id=1, source_target_pairs={{0,1},{1,0},{2,3},{3,2},{4,5},{5,4},{6,7},{7,6},{8,9},{9,8},{10,11... | collective-permute-start | bytes 589832 | tf_op jit(solution)/shard_map/ppermute | solution.py:450
  47.6 4.8 %collective-permute-start.8 = (f32[3,128]{1,0:T(4,128)}, f32[3,128]{1,0:T(4,128)}, u32[]{:S(2)}, u32[]{:S(2)}) collective-permute-start(f32[3,128]{1,0:T(4,128)} %qbm.3), channel_id=1, source_target_pairs={{0,1},{1,0},{2,3},{3,2},{4,5},{5,4},{6,7},{7,6},{8,9},{9,8},{10,11... | collective-permute-start | bytes 4616 | tf_op jit(solution)/shard_map/ppermute | solution.py:450
  48.0 52.6 %collective-permute-start.11 = (bf16[256,512]{1,0:T(8,128)(2,1)}, bf16[256,512]{1,0:T(8,128)(2,1)}, u32[]{:S(2)}, u32[]{:S(2)}) collective-permute-start(bf16[256,512]{1,0:T(8,128)(2,1)} %f1m.1), channel_id=1, source_target_pairs={{0,1},{1,0},{2,3},{3,2},{4,5},{5,4},{6,7},{7,6},{8,9},{9,8},{10,11... | collective-permute-start | bytes 786440 | tf_op jit(solution)/shard_map/ppermute | solution.py:450
  48.1 52.5 %collective-permute-start.13 = (bf16[512,256]{1,0:T(8,128)(2,1)}, bf16[512,256]{1,0:T(8,128)(2,1)}, u32[]{:S(2)}, u32[]{:S(2)}) collective-permute-start(bf16[512,256]{1,0:T(8,128)(2,1)} %f2m.1), channel_id=1, source_target_pairs={{0,1},{1,0},{2,3},{3,2},{4,5},{5,4},{6,7},{7,6},{8,9},{9,8},{10,11... | collective-permute-start | bytes 786440 | tf_op jit(solution)/shard_map/ppermute | solution.py:450
  49.4 29.7 %collective-permute-start.5 = (bf16[512,256]{1,0:T(8,128)(2,1)}, bf16[512,256]{1,0:T(8,128)(2,1)}, u32[]{:S(2)}, u32[]{:S(2)}) collective-permute-start(bf16[512,256]{1,0:T(8,128)(2,1)} %get-tuple-element.24), channel_id=1, source_target_pairs={{0,2},{2,4},{4,6},{6,8},{8,10},{10,12},{12,14},{14,16},{16,18},{18... | collective-permute-start | bytes 786440 | tf_op jit(solution)/shard_map/ppermute | solution.py:483
  52.4 26.7 %collective-permute-start.6 = (bf16[512,256]{1,0:T(8,128)(2,1)}, bf16[512,256]{1,0:T(8,128)(2,1)}, u32[]{:S(2)}, u32[]{:S(2)}) collective-permute-start(bf16[512,256]{1,0:T(8,128)(2,1)} %get-tuple-element.25), channel_id=1, source_target_pairs={{2,0},{4,2},{6,4},{8,6},{10,8},{12,10},{14,12},{16,14},{18,16},{20... | collective-permute-start | bytes 786440 | tf_op jit(solution)/shard_map/ppermute | solution.py:484
  79.1 21.5 %collective-permute-start.9 = (bf16[512,256]{1,0:T(8,128)(2,1)}, bf16[512,256]{1,0:T(8,128)(2,1)}, u32[]{:S(2)}, u32[]{:S(2)}) collective-permute-start(bf16[512,256]{1,0:T(8,128)(2,1)} %collective-permute-done.5), channel_id=1, source_target_pairs={{0,1},{1,0},{2,3},{3,2},{4,5},{5,4},{6,7},{7,6},{8,9},{9,8},{10,11... | collective-permute-start | bytes 786440 | tf_op jit(solution)/shard_map/ppermute | solution.py:450
  79.8 20.8 %collective-permute-start.10 = (bf16[512,256]{1,0:T(8,128)(2,1)}, bf16[512,256]{1,0:T(8,128)(2,1)}, u32[]{:S(2)}, u32[]{:S(2)}) collective-permute-start(bf16[512,256]{1,0:T(8,128)(2,1)} %collective-permute-done.6), channel_id=1, source_target_pairs={{0,1},{1,0},{2,3},{3,2},{4,5},{5,4},{6,7},{7,6},{8,9},{9,8},{10,11... | collective-permute-start | bytes 786440 | tf_op jit(solution)/shard_map/ppermute | solution.py:450
  81.3 18.5 %all-to-all-start.1 = ((s32[8,8,128]{2,1,0:T(8,128)}), s32[8,8,128]{2,1,0:T(8,128)S(1)}, u32[]{:S(2)}, u32[]{:S(2)}) async-start(s32[8,8,128]{2,1,0:T(8,128)} %copy.21), calls=%async_computation.1 | async-start | bytes 65536 | tf_op jit(solution)/shard_map/all_to_all | solution.py:480
  93.2 7.4 %collective-permute-start.12 = (f32[512]{0:T(512)}, f32[512]{0:T(512)}, u32[]{:S(2)}, u32[]{:S(2)}) collective-permute-start(f32[512]{0:T(512)} %param.35), channel_id=1, source_target_pairs={{0,1},{1,0},{2,3},{3,2},{4,5},{5,4},{6,7},{7,6},{8,9},{9,8},{10,11... | collective-permute-start | bytes 6152 | tf_op jit(solution)/shard_map/ppermute | solution.py:450
  177.0 1.0 copy-start
  178.0 5.4 %collective-permute-start.14 = (bf16[2048,256]{1,0:T(8,128)(2,1)S(1)}, bf16[2048,256]{1,0:T(8,128)(2,1)S(1)}, u32[]{:S(2)}, u32[]{:S(2)}) collective-permute-start(bf16[2048,256]{1,0:T(8,128)(2,1)S(1)} %bitcast.30), channel_id=1, source_target_pairs={{0,1},{1,0},{2,3},{3,2},{4,5},{5,4},{6,7},{7,6},{8,9},{9,8},{10,11... | collective-permute-start | bytes 3145736 | tf_op jit(solution)/shard_map/ppermute | solution.py:450
  183.4 1.0 copy-start.1

commit v5 on v4

--- a/solution.py
+++ b/solution.py
@@ -110,7 +110,7 @@
     lax.fori_loop(0, 4, finish, 0)
 
 
-def call(kernel, name, smem, args, out_shape, scratch, sems, flops):
+def call(kernel, name, smem, args, out_shape, scratch, sems, flops, moved=8 * 10**6):
     return pl.pallas_call(
         kernel,
         out_shape=out_shape,
@@ -119,7 +119,7 @@
         out_specs=[pl.BlockSpec(memory_space=pltpu.VMEM)] * len(out_shape),
         scratch_shapes=[pltpu.VMEM(*x) for x in scratch] + [pltpu.SemaphoreType.DMA((sems,))],
         compiler_params=pltpu.CompilerParams(vmem_limit_bytes=VMEM_BYTES),
-        cost_estimate=pl.CostEstimate(flops=flops, bytes_accessed=8 * 10**6, transcendentals=10**7),
+        cost_estimate=pl.CostEstimate(flops=flops, bytes_accessed=moved, transcendentals=0),
         name=name,
     )(*args)
 
@@ -282,7 +282,7 @@
     scratch = [
         ((32, 2, 32, 256), BF), ((256, 2048), BF), ((2048, 256), BF), ((8, 256, 32), BF),
     ] + QKV_SCRATCH
-    return call(near_kernel, "near", 1, args, out, scratch, 7, 20 * 10**9)
+    return call(near_kernel, "near", 1, args, out, scratch, 7, 0, 0)
 
 
 def far_kernel(
@@ -411,16 +411,16 @@
     return call(far_kernel, "far", 2, args, out, scratch, 26, 20 * 10**9)[0]
 
 
-def last_kernel(sc, zs, zv, own, oth, out, R, Z, sems):
+def last_kernel(sc, zs, zv, own, oth, out):
     g = sc[0]
-    wait(copies(sems, [(zv, Z), (own, R.at[:, g]), (oth, R.at[:, 1 - g])]))
-    place = jnp.where(
-        lax.broadcasted_iota(jnp.int32, (64, 64), 0) == Z[0:1, 0:64] % 64, 1.0, 0.0
-    )
+    place = zv[0:1, 0:64] % 64
+    place = place % 32 + jnp.where(place // 32 == g, 0, 32)
+    place = jnp.where(lax.broadcasted_iota(jnp.int32, (64, 64), 0) == place, 1.0, 0.0)
     perm = jnp.transpose(place).astype(BF)
 
     def step(k, _):
-        rows = R[lax.shift_right_logical(zs[64 * k], 11)].reshape(64, 256)
+        source = lax.shift_right_logical(zs[64 * k], 11)
+        rows = jnp.concatenate([own[source], oth[source]], axis=0)
         out[pl.ds(pl.multiple_of(64 * k, 64), 64), :] = jnp.dot(
             perm, rows, preferred_element_type=F32
         ).astype(BF)
@@ -430,9 +430,15 @@
 
 
 def last_call(*args):
-    out = [jax.ShapeDtypeStruct((2048, 256), BF)]
-    scratch = [((64, 2, 32, 256), BF), ((16, 128), jnp.int32)]
-    return call(last_kernel, "relabel", 2, args, out, scratch, 3, 10**9)[0]
+    smem, vmem = pl.BlockSpec(memory_space=pltpu.SMEM), pl.BlockSpec(memory_space=pltpu.VMEM)
+    return pl.pallas_call(
+        last_kernel,
+        out_shape=jax.ShapeDtypeStruct((2048, 256), BF),
+        in_specs=[smem] * 2 + [vmem] * 3,
+        out_specs=vmem,
+        compiler_params=pltpu.CompilerParams(vmem_limit_bytes=16 * 2**20),
+        name="relabel",
+    )(*args)
 
 
 def local(
@@ -453,18 +459,12 @@
         return x.reshape(-1, 32, 256)
 
     order = zorder.reshape(16, 128)
-    inner = [[8 * i + j for j in range(8)] for i in range(8)]
-    outer = [[8 * j + i for j in range(8)] for i in range(8)]
-    sources = jnp.arange(64, dtype=jnp.int32).reshape(8, 8).T[:, :, None, None]
-    wanted = jnp.max(
-        jnp.where(order // rows == sources, order % rows // 64, 0), axis=2
-    )
-    wanted = lax.all_to_all(
-        wanted, "pts", split_axis=0, concat_axis=0, tiled=True, axis_index_groups=inner
+    run = zorder[::64] // 64
+    table = lax.all_gather(
+        jnp.broadcast_to(jnp.pad(run, (0, 96))[None], (32, 128)), "pts", axis=0, tiled=True
     )
     low = lax.ppermute(points[rows - 256 :], "pts", forward)
     high = lax.ppermute(points[:256], "pts", backward)
-    wanted, low = lax.optimization_barrier((wanted, low))
     conv_m = conv_w.reshape(27 * 256, 128)
     conv_o, bias_o = swap(conv_m), swap(conv_b)
     scalars = jnp.stack([g, me * rows, jnp.int32(rows * peers)])
@@ -476,16 +476,13 @@
     weights = (qkv_m, swap(qkv_m), qkv_b, swap(qkv_b))
     fc1_o, fc2_o, b1_o = swap(fc1_w), swap(fc2_w), swap(fc1_b)
     other = swap(normed)
-    wanted, other = lax.optimization_barrier((jnp.transpose(wanted, (1, 0, 2)), other))
-    sel = lax.all_to_all(
-        wanted, "pts", split_axis=0, concat_axis=0, tiled=True, axis_index_groups=outer
-    )
     lo_own = lax.ppermute(lo_half, "pts", forward)
     hi_own = lax.ppermute(hi_half, "pts", backward)
     acc, query, most = near_call(scalars, patch_len[None], pieces(normed), pieces(other), *weights)
-    lo_own, hi_own, most = lax.optimization_barrier((lo_own, hi_own, most))
+    lo_own, hi_own, table, most = lax.optimization_barrier((lo_own, hi_own, table, most))
     lo_oth, hi_oth = swap(lo_own), swap(hi_own)
-    sel = jnp.max(sel, axis=2).reshape(64)
+    table = table.reshape(64, 32, 128)[:, 0, :32]
+    sel = jnp.max(jnp.where(table // 32 == me, table % 32, 0), axis=1)
     send = far_call(
         scalars, sel, patch_len[None], pieces(normed), pieces(other), pieces(lo_own),
         pieces(lo_oth), pieces(hi_own), pieces(hi_oth), section_one, acc, query, most, *weights,

time: 188 us -> 181 us (0.963); the launches traced: 189 us -> 180 us
  starting transfers between devices: 38.1 us -> 19.6 us
  between operations: 0.32 us -> 13.5 us
  Pallas kernels: 99.6 us -> 93.8 us
  blocking collectives: 29.1 us -> 31.4 us
    all_to_all x2 -> x0, starting transfers between devices: 18.9 us -> none  [local(): lax.all_to_all(wanted, 'pts', split_axis=0, concat_axis=0, tiled=True, ax...]
    all_gather x0 -> x1, waiting for transfers between devices: none -> 11.7 us  [local(): lax.all_gather(jnp.broadcast_to(jnp.pad(run, (0, 96))[None], (32, 128)),...]
    all_to_all x2 -> x0, waiting for transfers between devices: 10.5 us -> none  [local(): lax.all_to_all(wanted, 'pts', split_axis=0, concat_axis=0, tiled=True, ax...]
    pallas_call x4 -> x3, Pallas kernels: 99.6 us -> 91.2 us  [call(): pl.pallas_call(kernel, out_shape=out_shape, in_specs=[pl.BlockSpec(memory...]
    pallas_call x0 -> x1, Pallas kernels: none -> 2.59 us  [last_call(): pl.pallas_call(last_kernel, out_shape=jax.ShapeDtypeStruct((2048, 256), B...]
    all_to_all x1, blocking collectives: 29.1 us -> 31.4 us  [local(): got = lax.all_to_all(send, 'pts', split_axis=0, concat_axis=0, tiled=True)]
  transfers between devices with their start and end apart: 17 -> 16, of which waited for: 4 -> 3; matrix products, arithmetic and copies ran while one was open for 3% -> 3% of each run, Pallas kernels for 13% -> 26%
where the time goes in v5:
time: 181 us; the launch traced here: 180 us
  Pallas kernels  93.8 us (52%)
  blocking collectives  31.4 us (17%)
  starting transfers between devices  19.6 us (11%)
  waiting for transfers between devices  15.3 us (8%)
  between operations  13.5 us (7%)
  local copies, waits for them, and re-layouts  4.65 us (3%)
    pallas_call x3, Pallas kernels, call(): pl.pallas_call(kernel, out_shape=out_shape, in_specs=[pl.BlockSpec(memory...  91.2 us
    all_to_all x1, blocking collectives, local(): got = lax.all_to_all(send, 'pts', split_axis=0, concat_axis=0, tiled=True)  31.4 us
    all_gather x1, waiting for transfers between devices, local(): lax.all_gather(jnp.broadcast_to(jnp.pad(run, (0, 96))[None], (32, 128)),...  11.7 us
    ppermute x11, starting transfers between devices, swap(): return lax.ppermute(x, 'grp', [(0, 1), (1, 0)])  8.41 us
    ppermute x1, starting transfers between devices, local(): lo_own = lax.ppermute(lo_half, 'pts', forward)  4.65 us
    ppermute x1, starting transfers between devices, local(): low = lax.ppermute(points[rows - 256:], 'pts', forward)  3.99 us
  transfers between devices with their start and end apart: 16, of which 3 were waited for; matrix products, arithmetic and copies ran while one was open for 3% of the time, Pallas kernels for 26%

profile of v5, /device:TPU:1, one launch (start us, length us, event | category | flops | bytes accessed | tf_op | source)
XLA Modules:
  0.0 179.7 jit_solution(1874401362664796185)
XLA Ops:
  6.5 1.4 collective-permute-start.2
  8.0 0.0 collective-permute-start.3
  8.0 1.0 fusion.5
  9.0 1.3 collective-permute-start.1
  10.3 4.0 %collective-permute-start = (bf16[256,256]{1,0:T(8,128)(2,1)S(1)}, bf16[256,256]{1,0:T(8,128)(2,1)S(1)}, u32[]{:S(2)}, u32[]{:S(2)}) collective-permute-start(bf16[256,256]{1,0:T(8,128)(2,1)S(1)} %get-tuple-element.28), channel_id=1, source_target_pairs={{0,2},{2,4},{4,6},{6,8},{8,10},{10,12},{12,14},{14,16},{16,18},{18... | collective-permute-start | bytes 393224 | tf_op jit(solution)/shard_map/ppermute | solution.py:466
  14.3 0.8 slice.14
  15.1 0.6 broadcast_in_dim.47
  15.7 0.0 all-gather.2.cloned.1.call-update
  15.7 0.6 pad_add_fusion.sc
  16.4 0.6 copy-done.2
  17.0 0.6 copy-done.3
  17.7 22.7 %conv.1 = (bf16[1024,256]{1,0:T(8,128)(2,1)}, bf16[1024,256]{1,0:T(8,128)(2,1)}, bf16[512,256]{1,0:T(8,128)(2,1)}, bf16[512,256]{1,0:T(8,128)(2,1)}) custom-call(s32[3]{0:T(128)} %pad_add_fusion.sc, bf16[2048,256]{1,0:T(8,128)(2,1)} %pts.1, bf16[256,256]{1,0:T(8,128)(2,1)} %copy-done.3, bf16[256,256]{1,0:T(8,128)(2,1)} %copy-done.2, s32[27,2048]{1,0:T(8,128)} %bitcast.43, ...), custom_call_target="tpu_custom_call" | custom-call | flops 30000001024 | bytes 8000000 | tf_op jit(solution)/shard_map/conv/pallas_call | solution.py:114
  40.4 1.1 collective-permute-start.6
  41.5 4.7 %collective-permute-start.4 = (bf16[512,256]{1,0:T(8,128)(2,1)}, bf16[512,256]{1,0:T(8,128)(2,1)}, u32[]{:S(2)}, u32[]{:S(2)}) collective-permute-start(bf16[512,256]{1,0:T(8,128)(2,1)} %get-tuple-element.16), channel_id=1, source_target_pairs={{0,2},{2,4},{4,6},{6,8},{8,10},{10,12},{12,14},{14,16},{16,18},{18... | collective-permute-start | bytes 786440 | tf_op jit(solution)/shard_map/ppermute | solution.py:479
  46.2 1.3 collective-permute-start.5
  47.5 0.4 collective-permute-start.7
  47.9 0.2 collective-permute-start.8
  48.1 1.3 collective-permute-done.8.qbo
  49.4 0.3 collective-permute-start.11
  49.7 0.2 collective-permute-start.13
  49.9 23.7 %near.1 = (f32[4,2,256,256]{3,2,1,0:T(8,128)}, bf16[1024,256]{1,0:T(8,128)(2,1)}, f32[8,128]{1,0:T(8,128)}) custom-call(s32[3]{0:T(128)} %pad_add_fusion.sc, s32[1,256]{1,0:T(1,128)} %bitcast.38, bf16[32,32,256]{2,1,0:T(8,128)(2,1)} %bitcast.32, bf16[32,32,256]{2,1,0:T(8,128)(2,1)} %bitcast.12.oth, bf16[3,256,128]{2,1,0:T(8,128)(2,1)} %bitcast.35, ...), custom_call_target="tpu_custom_call" | custom-call | tf_op jit(solution)/shard_map/near/pallas_call | solution.py:114
  73.7 11.7 %all-gather.2.cloned.1.call-done = s32[2048,128]{1,0:T(8,128)} async-done(((s32[32,128]{1,0:T(8,128)}), s32[2048,128]{1,0:T(8,128)}) %all-gather.2.cloned.1.call-update) | async-done | bytes 1048592 | tf_op jit(solution)/shard_map/all_gather | solution.py:463
  85.4 2.5 %collective-permute-start.9 = (bf16[512,256]{1,0:T(8,128)(2,1)}, bf16[512,256]{1,0:T(8,128)(2,1)}, u32[]{:S(2)}, u32[]{:S(2)}) collective-permute-start(bf16[512,256]{1,0:T(8,128)(2,1)} %collective-permute-done.4), channel_id=1, source_target_pairs={{0,1},{1,0},{2,3},{3,2},{4,5},{5,4},{6,7},{7,6},{8,9},{9,8},{10,11... | collective-permute-start | bytes 786440 | tf_op jit(solution)/shard_map/ppermute | solution.py:456
  87.8 0.5 collective-permute-start.12
  88.3 1.0 slice.16
  89.3 0.7 fusion.2.sel
  90.0 44.8 %far.1 = bf16[2048,256]{1,0:T(8,128)(2,1)} custom-call(s32[3]{0:T(128)} %pad_add_fusion.sc, s32[64]{0:T(128)} %fusion.2.sel, s32[1,256]{1,0:T(1,128)} %bitcast.39, bf16[32,32,256]{2,1,0:T(8,128)(2,1)} %bitcast.33, bf16[32,32,256]{2,1,0:T(8,128)(2,1)} %bitcast.12.oth, bf16[16,32,256]{2,1,0:T(8,128)(2,1)} %bitcast.16.lo_own, ...), custom_call_target="tpu_custom_call" | custom-call | flops 20000000000 | bytes 8000000 | tf_op jit(solution)/shard_map/far/pallas_call | solution.py:114
  134.8 0.0 copy-start
  134.8 31.4 %all_to_all.12.own = bf16[64,32,256]{2,1,0:T(8,128)(2,1)S(1)} all-to-all(bf16[64,32,256]{2,1,0:T(8,128)(2,1)} %bitcast.31), channel_id=1, replica_groups=mesh['pts'=64,'grp'=2] {'pts'}, dimensions={0} | all-to-all | bytes 2097152 | tf_op jit(solution)/shard_map/all_to_all | solution.py:492
  166.2 1.8 collective-permute-start.14
  168.0 2.3 %collective-permute-done.14 = bf16[2048,256]{1,0:T(8,128)(2,1)S(1)} collective-permute-done((bf16[2048,256]{1,0:T(8,128)(2,1)S(1)}, bf16[2048,256]{1,0:T(8,128)(2,1)S(1)}, u32[]{:S(2)}, u32[]{:S(2)}) %collective-permute-start.14) | collective-permute-done | bytes 1048608 | tf_op jit(solution)/shard_map/ppermute | solution.py:456
  170.3 2.6 %relabel.1 = bf16[2048,256]{1,0:T(8,128)(2,1)} custom-call(s32[3]{0:T(128)S(1)} %copy-done.1, s32[2048]{0:T(1024)S(1)} %copy-done, s32[16,128]{1,0:T(8,128)S(1)} %bitcast.30, bf16[64,32,256]{2,1,0:T(8,128)(2,1)S(1)} %all_to_all.12.own, bf16[64,32,256]{2,1,0:T(8,128)(2,1)S(1)} %bitcast.29), custom_call_target="tpu_custom_call" | custom-call | tf_op jit(solution)/shard_map/relabel/pallas_call | solution.py:434
  (24 shorter events, 0.1 us)
Async XLA Ops:
  6.5 78.8 %all-gather.2.cloned.1.call-start = ((), (), s32[]{:S(2)}) async-start(), calls=%async_computation.1 | async-start | bytes 1064960 | tf_op jit(solution)/shard_map/all_gather | solution.py:463
  6.5 10.5 %collective-permute-start.2 = (bf16[6912,128]{1,0:T(8,128)(2,1)}, bf16[6912,128]{1,0:T(8,128)(2,1)}, u32[]{:S(2)}, u32[]{:S(2)}) collective-permute-start(bf16[6912,128]{1,0:T(8,128)(2,1)} %bitcast.41), channel_id=1, source_target_pairs={{0,1},{1,0},{2,3},{3,2},{4,5},{5,4},{6,7},{7,6},{8,9},{9,8},{10,11... | collective-permute-start | bytes 5308424 | tf_op jit(solution)/shard_map/ppermute | solution.py:456
  8.0 8.4 %collective-permute-start.3 = (f32[128]{0:T(128)}, f32[128]{0:T(128)S(1)}, u32[]{:S(2)}, u32[]{:S(2)}) collective-permute-start(f32[128]{0:T(128)} %param.24), channel_id=1, source_target_pairs={{0,1},{1,0},{2,3},{3,2},{4,5},{5,4},{6,7},{7,6},{8,9},{9,8},{10,11... | collective-permute-start | bytes 1544 | tf_op jit(solution)/shard_map/ppermute | solution.py:456
  9.0 7.4 %collective-permute-start.1 = (bf16[256,256]{1,0:T(8,128)(2,1)S(1)}, bf16[256,256]{1,0:T(8,128)(2,1)S(1)}, u32[]{:S(2)}, u32[]{:S(2)}) collective-permute-start(bf16[256,256]{1,0:T(8,128)(2,1)S(1)} %get-tuple-element.27), channel_id=1, source_target_pairs={{2,0},{4,2},{6,4},{8,6},{10,8},{12,10},{14,12},{16,14},{18,16},{20... | collective-permute-start | bytes 393224 | tf_op jit(solution)/shard_map/ppermute | solution.py:467
  10.3 6.1 %collective-permute-start = (bf16[256,256]{1,0:T(8,128)(2,1)S(1)}, bf16[256,256]{1,0:T(8,128)(2,1)S(1)}, u32[]{:S(2)}, u32[]{:S(2)}) collective-permute-start(bf16[256,256]{1,0:T(8,128)(2,1)S(1)} %get-tuple-element.28), channel_id=1, source_target_pairs={{0,2},{2,4},{4,6},{6,8},{8,10},{10,12},{12,14},{14,16},{16,18},{18... | collective-permute-start | bytes 393224 | tf_op jit(solution)/shard_map/ppermute | solution.py:466
  16.4 1.3 copy-start.4
  16.4 0.7 copy-start.2
  17.0 0.6 copy-start.3
  40.4 9.5 %collective-permute-start.6 = (bf16[1024,256]{1,0:T(8,128)(2,1)}, bf16[1024,256]{1,0:T(8,128)(2,1)}, u32[]{:S(2)}, u32[]{:S(2)}) collective-permute-start(bf16[1024,256]{1,0:T(8,128)(2,1)} %get-tuple-element.18), channel_id=1, source_target_pairs={{0,1},{1,0},{2,3},{3,2},{4,5},{5,4},{6,7},{7,6},{8,9},{9,8},{10,11... | collective-permute-start | bytes 1572872 | tf_op jit(solution)/shard_map/ppermute | solution.py:456
  41.5 32.1 %collective-permute-start.4 = (bf16[512,256]{1,0:T(8,128)(2,1)}, bf16[512,256]{1,0:T(8,128)(2,1)}, u32[]{:S(2)}, u32[]{:S(2)}) collective-permute-start(bf16[512,256]{1,0:T(8,128)(2,1)} %get-tuple-element.16), channel_id=1, source_target_pairs={{0,2},{2,4},{4,6},{6,8},{8,10},{10,12},{12,14},{14,16},{16,18},{18... | collective-permute-start | bytes 786440 | tf_op jit(solution)/shard_map/ppermute | solution.py:479
  46.2 27.5 %collective-permute-start.5 = (bf16[512,256]{1,0:T(8,128)(2,1)}, bf16[512,256]{1,0:T(8,128)(2,1)}, u32[]{:S(2)}, u32[]{:S(2)}) collective-permute-start(bf16[512,256]{1,0:T(8,128)(2,1)} %get-tuple-element.17), channel_id=1, source_target_pairs={{2,0},{4,2},{6,4},{8,6},{10,8},{12,10},{14,12},{16,14},{18,16},{20... | collective-permute-start | bytes 786440 | tf_op jit(solution)/shard_map/ppermute | solution.py:480
  47.5 2.2 %collective-permute-start.7 = (bf16[3,256,128]{2,1,0:T(8,128)(2,1)}, bf16[3,256,128]{2,1,0:T(8,128)(2,1)}, u32[]{:S(2)}, u32[]{:S(2)}) collective-permute-start(bf16[3,256,128]{2,1,0:T(8,128)(2,1)} %bitcast.34), channel_id=1, source_target_pairs={{0,1},{1,0},{2,3},{3,2},{4,5},{5,4},{6,7},{7,6},{8,9},{9,8},{10,11... | collective-permute-start | bytes 589832 | tf_op jit(solution)/shard_map/ppermute | solution.py:456
  47.9 1.5 collective-permute-start.8
  49.4 40.6 %collective-permute-start.11 = (bf16[256,512]{1,0:T(8,128)(2,1)}, bf16[256,512]{1,0:T(8,128)(2,1)}, u32[]{:S(2)}, u32[]{:S(2)}) collective-permute-start(bf16[256,512]{1,0:T(8,128)(2,1)} %f1m.1), channel_id=1, source_target_pairs={{0,1},{1,0},{2,3},{3,2},{4,5},{5,4},{6,7},{7,6},{8,9},{9,8},{10,11... | collective-permute-start | bytes 786440 | tf_op jit(solution)/shard_map/ppermute | solution.py:456
  49.7 40.4 %collective-permute-start.13 = (bf16[512,256]{1,0:T(8,128)(2,1)}, bf16[512,256]{1,0:T(8,128)(2,1)}, u32[]{:S(2)}, u32[]{:S(2)}) collective-permute-start(bf16[512,256]{1,0:T(8,128)(2,1)} %f2m.1), channel_id=1, source_target_pairs={{0,1},{1,0},{2,3},{3,2},{4,5},{5,4},{6,7},{7,6},{8,9},{9,8},{10,11... | collective-permute-start | bytes 786440 | tf_op jit(solution)/shard_map/ppermute | solution.py:456
  85.4 4.7 %collective-permute-start.9 = (bf16[512,256]{1,0:T(8,128)(2,1)}, bf16[512,256]{1,0:T(8,128)(2,1)}, u32[]{:S(2)}, u32[]{:S(2)}) collective-permute-start(bf16[512,256]{1,0:T(8,128)(2,1)} %collective-permute-done.4), channel_id=1, source_target_pairs={{0,1},{1,0},{2,3},{3,2},{4,5},{5,4},{6,7},{7,6},{8,9},{9,8},{10,11... | collective-permute-start | bytes 786440 | tf_op jit(solution)/shard_map/ppermute | solution.py:456
  87.8 2.2 %collective-permute-start.10 = (bf16[512,256]{1,0:T(8,128)(2,1)}, bf16[512,256]{1,0:T(8,128)(2,1)}, u32[]{:S(2)}, u32[]{:S(2)}) collective-permute-start(bf16[512,256]{1,0:T(8,128)(2,1)} %collective-permute-done.5), channel_id=1, source_target_pairs={{0,1},{1,0},{2,3},{3,2},{4,5},{5,4},{6,7},{7,6},{8,9},{9,8},{10,11... | collective-permute-start | bytes 786440 | tf_op jit(solution)/shard_map/ppermute | solution.py:456
  87.8 2.2 %collective-permute-start.12 = (f32[512]{0:T(512)}, f32[512]{0:T(512)}, u32[]{:S(2)}, u32[]{:S(2)}) collective-permute-start(f32[512]{0:T(512)} %param.35), channel_id=1, source_target_pairs={{0,1},{1,0},{2,3},{3,2},{4,5},{5,4},{6,7},{7,6},{8,9},{9,8},{10,11... | collective-permute-start | bytes 6152 | tf_op jit(solution)/shard_map/ppermute | solution.py:456
  134.8 35.5 %copy-start = (s32[2048]{0:T(1024)S(1)}, s32[2048]{0:T(1024)}, u32[]{:S(2)}) copy-start(s32[2048]{0:T(1024)} %zs.1) | copy-start | bytes 24580
  134.8 35.4 %copy-start.1 = (s32[3]{0:T(128)S(1)}, s32[3]{0:T(128)}, u32[]{:S(2)}) copy-start(s32[3]{0:T(128)} %pad_add_fusion.sc) | copy-start | bytes 40
  166.2 4.0 %collective-permute-start.14 = (bf16[2048,256]{1,0:T(8,128)(2,1)S(1)}, bf16[2048,256]{1,0:T(8,128)(2,1)S(1)}, u32[]{:S(2)}, u32[]{:S(2)}) collective-permute-start(bf16[2048,256]{1,0:T(8,128)(2,1)S(1)} %bitcast.28), channel_id=1, source_target_pairs={{0,1},{1,0},{2,3},{3,2},{4,5},{5,4},{6,7},{7,6},{8,9},{9,8},{10,11... | collective-permute-start | bytes 3145736 | tf_op jit(solution)/shard_map/ppermute | solution.py:456
Sparse Core Ops, SparseCore 0:
  15.8 69.4 all-gather.1
